TPU v7x, 256 devices: a whole 4x4x8 slice. The times are simulated.
256 devices in a mesh: grp: 4 (over y), path: 64 (over x, z, core).
Axes of the slice: x: 4, y: 4, z: 8, core: 2. Of those that a mesh axis runs over, the one named last changes fastest.
Arguments:
- path_sens: bfloat16 [65536, 4800], P(('grp', 'path')), may hold values from -6 to 6
- discounts: bfloat16 [65536, 128], P(('grp', 'path')), may hold values from 0.29882812 to 1
- cash_flows: float32 [2048, 8], P('grp'), may hold values from -384 to 384
- flow_index: int32 [2048, 8], P('grp'), may hold values from 0 to 127
- exercise_step: int32 [2048], P('grp'), may hold values from 0 to 127
- trade_steps: int32 [2048], P('grp'), may hold values from 1 to 40
- jacobian_inv: bfloat16 [4800, 4800], P('path'), may hold values from -0.09375 to 0.09375
Outputs:
- quote_vega: float32 [2048, 4800], P(('grp', 'path'))
All inputs are finite; a program needn't handle non-finite values.
Results may differ from a plain program's by a relative error of at most 0.004.
Values may be sent and summed in bfloat16 or wider, within the bound.
A program may use at most 64 MiB of HBM per device.

v0:
```python
import jax
import jax.numpy as jnp
from jax import lax
from jax.sharding import PartitionSpec as P

NB = 40


def per_device(
    path_sens, discounts, cash_flows, flow_index, exercise_step, trade_steps, jacobian_inv
):
    sens_all, disc_all = (
        lax.all_gather(path_sens, "grp", axis=0, tiled=True),
        lax.all_gather(discounts, "grp", axis=0, tiled=True),
    )
    path_count = lax.axis_size("path")
    mine = lax.axis_index("path")
    path_scale = 1.0 / (sens_all.shape[0] * path_count)
    group_rows = cash_flows.shape[0]
    params = path_sens.shape[1]
    trade_share = group_rows // path_count
    bucket_width = params // NB
    forward_count = discounts.shape[1]
    forwards = jnp.arange(forward_count, dtype=jnp.int32)
    live = (flow_index[:, :, None] == forwards[None, None, :]) & (
        forwards[None, None, :] >= exercise_step[:, None, None]
    )
    weights = jnp.einsum(
        "tc,tcf->ft", cash_flows, live.astype(jnp.float32), precision=lax.Precision.HIGHEST
    )
    adjoint = jnp.dot(
        disc_all.astype(jnp.float32), weights, precision=lax.Precision.HIGHEST
    ).astype(jnp.bfloat16)
    partial_vega = (
        lax.dot_general(
            adjoint, sens_all, (((0,), (0,)), ((), ())), preferred_element_type=jnp.float32
        )
        * path_scale
    )
    trade_rows = lax.psum_scatter(partial_vega, "path", scatter_dimension=0, tiled=True)
    row_steps = lax.dynamic_slice_in_dim(trade_steps, mine * trade_share, trade_share)
    bucket = jnp.arange(params, dtype=jnp.int32) // bucket_width
    masked = jnp.where(bucket[None, :] < row_steps[:, None], trade_rows, 0.0).astype(jnp.bfloat16)
    by_param = lax.all_to_all(masked, "path", split_axis=1, concat_axis=0, tiled=True)
    vega_cols = by_param.T
    return lax.psum_scatter(
        lax.dot_general(
            vega_cols, jacobian_inv, (((0,), (0,)), ((), ())), preferred_element_type=jnp.float32
        ),
        "path",
        scatter_dimension=0,
        tiled=True,
    )


def solution(mesh):
    placed = (
        P(("grp", "path"), None),
        P(("grp", "path"), None),
        P("grp", None),
        P("grp", None),
        P("grp"),
        P("grp"),
        P("path", None),
    )
    return jax.shard_map(
        per_device, mesh=mesh, in_specs=placed, out_specs=P(("grp", "path"), None), check_vma=False
    )
```

profile of v0, /device:TPU:1, one launch (start us, length us, event | category | flops | bytes accessed | tf_op | source)
XLA Modules:
  0.0 460.3 jit_solution(1160963694546193891)
XLA Ops:
  6.5 0.0 copy-start
  6.5 0.0 all-gather.2.cloned.1.call-start
  6.5 0.7 all-gather.2.cloned.1.call-update
  7.3 0.0 reduce-scatter.3.cloned.1.call-start
  7.3 0.8 copy.11
  8.2 0.8 copy.9
  9.0 11.5 %all_gather.6 = bf16[1024,128]{1,0:T(8,128)(2,1)S(1)} all-gather(bf16[256,128]{1,0:T(8,128)(2,1)} %param.8), channel_id=1, replica_groups=mesh['grp'=4,'path'=64] {'grp'}, dimensions={0}, use_global_device_ids=true | all-gather | bytes 327680 | tf_op jit(solution)/shard_map/all_gather | solution.py:14
  20.5 0.8 iota_compare_fusion.1
  21.3 4.0 fusion.1
  25.3 1.0 convolution_convert_fusion
  26.3 87.7 %all-gather.2.cloned.1.call-done = bf16[1024,4800]{0,1:T(8,128)(2,1)} async-done(((bf16[256,4800]{0,1:T(8,128)(2,1)}), bf16[1024,4800]{0,1:T(8,128)(2,1)}) %all-gather.2.cloned.1.call-update) | async-done | bytes 9830416 | tf_op jit(solution)/shard_map/all_gather | solution.py:13
  114.0 11.6 %convolution_multiply_fusion = f32[512,4800]{1,0:T(8,128)} fusion(bf16[512,1024]{1,0:T(8,128)(2,1)S(1)} %convolution_convert_fusion, bf16[1024,4800]{0,1:T(8,128)(2,1)} %all-gather.2.cloned.1.call-done), kind=kOutput, calls=%fused_computation | convolution fusion | flops 5035622400 | bytes 20709376 | tf_op jit(solution)/shard_map/dot_general | solution.py:35
  125.6 0.0 reduce-scatter.3.cloned.1.call-update
  125.6 0.0 reduce-scatter.5.cloned.1.call-start
  125.7 0.8 dynamic_slice.3
  126.5 152.1 %reduce-scatter.3.cloned.1.call-done = f32[8,4800]{1,0:T(8,128)} async-done(((f32[512,4800]{1,0:T(8,128)}), f32[8,4800]{1,0:T(8,128)}) %reduce-scatter.3.cloned.1.call-update) | async-done | bytes 153616 | tf_op jit(solution)/shard_map/reduce_scatter | solution.py:40
  278.6 1.0 select_convert_fusion
  279.6 0.3 all_to_all.14
  279.9 0.1 copy.10
  280.0 22.1 %all_to_all.19 = bf16[8,64,75]{2,0,1:T(8,128)(2,1)S(1)} all-to-all(bf16[8,64,75]{2,0,1:T(8,128)(2,1)S(1)} %copy.10), channel_id=1, replica_groups=mesh['grp'=4,'path'=64] {'path'}, dimensions={1} | all-to-all | bytes 153600 | tf_op jit(solution)/shard_map/all_to_all | solution.py:44
  302.1 0.0 copy-done
  302.1 5.2 %fusion.5 = f32[512,4800]{1,0:T(8,128)} fusion(bf16[75,4800]{1,0:T(8,128)(2,1)S(1)} %copy-done, bf16[8,64,75]{2,0,1:T(8,128)(2,1)S(1)} %all_to_all.19), kind=kOutput, calls=%fused_computation.9 | convolution fusion | flops 368640000 | bytes 10627200 | tf_op jit(solution)/shard_map/dot_general | solution.py:47
  307.4 0.0 reduce-scatter.5.cloned.1.call-update
  307.4 146.4 %reduce-scatter.5.cloned.1.call-done = f32[8,4800]{1,0:T(8,128)} async-done(((f32[512,4800]{1,0:T(8,128)}), f32[8,4800]{1,0:T(8,128)}) %reduce-scatter.5.cloned.1.call-update) | async-done | bytes 153616 | tf_op jit(solution)/shard_map/reduce_scatter | solution.py:46
  (1 shorter events, 0.0 us)
Async XLA Ops:
  6.5 295.6 %copy-start = (bf16[75,4800]{1,0:T(8,128)(2,1)S(1)}, bf16[75,4800]{1,0:T(8,128)(2,1)}, u32[]{:S(2)}) copy-start(bf16[75,4800]{1,0:T(8,128)(2,1)} %param.13) | copy-start | bytes 2160004
  6.5 107.4 %all-gather.2.cloned.1.call-start = ((), (), s32[]{:S(2)}) async-start(), calls=%async_computation.3 | async-start | bytes 12288000 | tf_op jit(solution)/shard_map/all_gather | solution.py:13
  7.3 271.3 %reduce-scatter.3.cloned.1.call-start = ((), (), s32[]{:S(2)}) async-start(), calls=%async_computation.4 | async-start | bytes 10117120 | tf_op jit(solution)/shard_map/reduce_scatter | solution.py:40
  125.6 328.1 %reduce-scatter.5.cloned.1.call-start = ((), (), s32[]{:S(2)}) async-start(), calls=%async_computation.5 | async-start | bytes 10117120 | tf_op jit(solution)/shard_map/reduce_scatter | solution.py:46
Sparse Core Ops, SparseCore 0:
  9.2 104.7 all-gather.1
  125.8 152.7 reduce-scatter.2
  307.5 146.2 reduce-scatter.4
where the time goes:
time: 465 us; the launch traced here: 460 us
  waiting for transfers between devices  387 us (83%)
  blocking collectives  33.5 us (7%)
  matrix products  21.9 us (5%)
  between operations  13.2 us (3%)
    reduce_scatter x1, waiting for transfers between devices, per_device(): lax.psum_scatter(partial_vega, 'path', scatter_dimension=0, tiled=True)  152 us
    reduce_scatter x1, waiting for transfers between devices, per_device(): lax.psum_scatter(lax.dot_general(vega_cols, jacobian_inv, (((0,), (0,)),...  146 us
    all_gather x1, waiting for transfers between devices, per_device(): lax.all_gather(path_sens, 'grp', axis=0, tiled=True)  87.7 us
    all_to_all x1, blocking collectives, per_device(): lax.all_to_all(masked, 'path', split_axis=1, concat_axis=0, tiled=True)  22.1 us
    dot_general x1, matrix products, per_device(): lax.dot_general(adjoint, sens_all, (((0,), (0,)), ((), ())), preferred_el...  11.6 us
    all_gather x1, blocking collectives, per_device(): lax.all_gather(discounts, 'grp', axis=0, tiled=True)  11.5 us
  transfers between devices with their start and end apart: 3, of which 3 were waited for; matrix products, arithmetic and copies ran while one was open for 2% of the time, Pallas kernels for 0%

commit v1 on v0

v1 whole, which is shorter than its diff:
```python
import jax
import jax.numpy as jnp
from jax import lax
from jax.sharding import PartitionSpec as P

NB = 40


def per_device(
    path_sens, discounts, cash_flows, flow_index, exercise_step, trade_steps, jacobian_inv
):
    params = path_sens.shape[1]
    path_scale = 1.0 / (path_sens.shape[0] * lax.axis_size("path") * lax.axis_size("grp"))
    bucket_width = params // NB
    forward_count = discounts.shape[1]
    by_quote = lax.all_to_all(jacobian_inv, "path", split_axis=1, concat_axis=0, tiled=True)
    moments = lax.dot_general(
        discounts, path_sens, (((0,), (0,)), ((), ())), preferred_element_type=jnp.float32
    )
    moments = lax.psum(moments, ("grp", "path"))
    forwards = jnp.arange(forward_count, dtype=jnp.int32)
    live = (flow_index[:, :, None] == forwards[None, None, :]) & (
        forwards[None, None, :] >= exercise_step[:, None, None]
    )
    weights = jnp.einsum(
        "tc,tcf->tf", cash_flows, live.astype(jnp.float32), precision=lax.Precision.HIGHEST
    )
    vega = jnp.dot(weights, moments, precision=lax.Precision.HIGHEST) * path_scale
    bucket = jnp.arange(params, dtype=jnp.int32) // bucket_width
    masked = jnp.where(bucket[None, :] < trade_steps[:, None], vega, 0.0).astype(jnp.bfloat16)
    quotes = jnp.dot(masked, by_quote, preferred_element_type=jnp.float32)
    return lax.all_to_all(quotes, "path", split_axis=0, concat_axis=1, tiled=True)


def solution(mesh):
    placed = (
        P(("grp", "path"), None),
        P(("grp", "path"), None),
        P("grp", None),
        P("grp", None),
        P("grp"),
        P("grp"),
        P("path", None),
    )
    return jax.shard_map(
        per_device, mesh=mesh, in_specs=placed, out_specs=P(("grp", "path"), None), check_vma=False
    )
```

time: 465 us -> 347 us (0.75)
  waiting for transfers between devices: 387 us -> 249 us
  local copies, waits for them, and re-layouts: 2.87 us -> 25.5 us
  starting transfers between devices: 0.08 us -> 13.2 us
  blocking collectives: 33.5 us -> 22.9 us
    reduce_scatter x2 -> x0, waiting for transfers between devices: 299 us -> none  [the longest x1 152 us: per_device(): lax.psum_scatter(partial_vega, 'path', scatter_dimension=0, tiled=True)]
    psum x0 -> x1, waiting for transfers between devices: none -> 249 us  [per_device(): moments = lax.psum(moments, ('grp', 'path'))]
    all_gather x1 -> x0, waiting for transfers between devices: 87.7 us -> none  [per_device(): lax.all_gather(path_sens, 'grp', axis=0, tiled=True)]
    all_to_all x2 -> x6, local copies, waits for them, and re-layouts: 0.42 us -> 14.9 us  [the longest x4 14 us: per_device(): lax.all_to_all(jacobian_inv, 'path', split_axis=1, concat_axis=0, tiled=T...]
    all_to_all x0 -> x1, starting transfers between devices: none -> 13.2 us  [per_device(): lax.all_to_all(jacobian_inv, 'path', split_axis=1, concat_axis=0, tiled=T...]
    all_gather x1 -> x0, blocking collectives: 11.5 us -> none  [per_device(): lax.all_gather(discounts, 'grp', axis=0, tiled=True)]
    convert_element_type x0 -> x1, local copies, waits for them, and re-layouts: none -> 7.52 us  [per_device(): jnp.where(bucket[None, :] < trade_steps[:, None], vega, 0.0)]
  transfers between devices with their start and end apart: 3 -> 2, of which waited for: 3 -> 1; matrix products, arithmetic and copies ran while one was open for 2% -> 8% of each run, Pallas kernels for 0% -> 0%
where the time goes in v1:
time: 347 us
  waiting for transfers between devices  249 us (72%)
  local copies, waits for them, and re-layouts  25.5 us (7%)
  matrix products  22.9 us (7%)
  blocking collectives  22.9 us (7%)
  between operations  13.5 us (4%)
  starting transfers between devices  13.2 us (4%)
    psum x1, waiting for transfers between devices, per_device(): moments = lax.psum(moments, ('grp', 'path'))  249 us
    all_to_all x1, blocking collectives, per_device(): lax.all_to_all(quotes, 'path', split_axis=0, concat_axis=1, tiled=True)  22.9 us
    all_to_all x4, local copies, waits for them, and re-layouts, per_device(): lax.all_to_all(jacobian_inv, 'path', split_axis=1, concat_axis=0, tiled=T...  14 us
    all_to_all x1, starting transfers between devices, per_device(): lax.all_to_all(jacobian_inv, 'path', split_axis=1, concat_axis=0, tiled=T...  13.2 us
    dot_general x1, matrix products, per_device(): jnp.dot(weights, moments, precision=lax.Precision.HIGHEST) * path_scale  12 us
    convert_element_type x1, local copies, waits for them, and re-layouts, per_device(): jnp.where(bucket[None, :] < trade_steps[:, None], vega, 0.0)  7.52 us
  transfers between devices with their start and end apart: 2, of which 1 were waited for; matrix products, arithmetic and copies ran while one was open for 8% of the time, Pallas kernels for 0%

profile of v1, /device:TPU:1, one launch (start us, length us, event | category | flops | bytes accessed | tf_op | source)
XLA Modules:
  0.0 346.8 jit_solution(15424829769251917122)
XLA Ops:
  6.5 0.0 copy-start
  6.5 0.0 all-reduce.2.cloned.1.call-start
  6.5 1.7 copy-done
  8.2 3.1 fusion.10
  11.3 0.0 copy-start.1
  11.3 0.0 all-reduce.2.cloned.1.call-update
  11.3 1.1 copy-done.1
  12.4 5.1 %all_to_all.26 = bf16[75,64,75]{2,1,0:T(8,128)(2,1)} reshape(bf16[75,4800]{1,0:T(8,128)(2,1)S(1)} %copy-done.1) | data formatting | bytes 1440000 | tf_op jit(solution)/shard_map/all_to_all | solution.py:16
  17.6 0.0 copy-start.2
  17.6 0.0 copy-start.3
  17.6 0.0 copy-start.4
  17.6 3.4 copy.22
  21.0 13.2 %all-to-all-start = ((bf16[75,64,75]{0,2,1:T(8,128)(2,1)}), bf16[75,64,75]{0,2,1:T(8,128)(2,1)}, u32[]{:S(2)}, u32[]{:S(2)}) async-start(bf16[75,64,75]{0,2,1:T(8,128)(2,1)} %copy.22), calls=%async_computation | async-start | bytes 2621440 | tf_op jit(solution)/shard_map/all_to_all | solution.py:16
  34.2 0.0 copy-done.2
  34.2 0.0 copy-start.5
  34.2 0.1 copy.20
  34.3 0.0 copy-done.3
  34.4 0.1 copy.25
  34.5 0.0 copy-done.4
  34.5 0.1 iota_compare_fusion.1
  34.7 4.0 %fusion.3 = f32[512,1,128]{2,1,0:T(1,128)S(1)} fusion(f32[512,8,1]{1,2,0:T(1,128)S(1)} %copy.25, s32[512,8]{1,0:T(8,128)S(1)} %copy.20, pred[512,128]{1,0:T(8,128)(4,1)S(1)} %iota_compare_fusion.1), kind=kOutput, calls=%fused_computation.5 | convolution fusion | flops 7340032 | bytes 360448 | tf_op jit(solution)/shard_map/tc,tcf->tf/dot_general | solution.py:25
  38.7 248.6 %all-reduce.2.cloned.1.call-done = f32[128,4800]{0,1:T(8,128)} async-done(((f32[128,4800]{0,1:T(8,128)}), f32[128,4800]{0,1:T(8,128)}) %all-reduce.2.cloned.1.call-update) | async-done | bytes 2457616 | tf_op jit(solution)/shard_map/psum | solution.py:20
  287.3 0.0 copy-done.5
  287.3 12.0 %select_convert_fusion = bf16[512,4800]{0,1:T(8,128)(2,1)} fusion(f32[512,128]{1,0:T(8,128)S(1)} %bitcast.18, f32[128,4800]{0,1:T(8,128)} %all-reduce.2.cloned.1.call-done, s32[512]{0:T(512)S(1)} %copy-done.5, s32[4800]{0:T(1024)S(1)} %add_select_fusion), kind=kOutput, calls=%fused_computation | convolution fusion | flops 3784704000 | bytes 7656192 | tf_op jit(solution)/shard_map/dot_general | solution.py:28
  299.3 7.5 %copy.21 = bf16[512,4800]{1,0:T(8,128)(2,1)} copy(bf16[512,4800]{0,1:T(8,128)(2,1)} %select_convert_fusion) | data formatting | bytes 9830400 | tf_op jit(solution)/shard_map/convert_element_type | solution.py:30
  306.8 0.0 all-to-all-done
  306.8 2.7 copy.23
  309.5 2.7 reshape.42
  312.2 3.8 %fusion = f32[64,8,75]{2,1,0:T(8,128)S(1)} fusion(bf16[4800,75,1]{0,1,2:T(8,128)(2,1)S(1)} %reshape.42, bf16[512,4800]{1,0:T(8,128)(2,1)} %copy.21), kind=kOutput, calls=%fused_computation.1 | convolution fusion | flops 368640000 | bytes 5788800 | tf_op jit(solution)/shard_map/dot_general | solution.py:31
  316.1 22.9 %all_to_all.35 = f32[64,8,75]{2,1,0:T(8,128)S(1)} all-to-all(f32[64,8,75]{2,1,0:T(8,128)S(1)} %fusion), channel_id=1, replica_groups=mesh['grp'=4,'path'=64] {'path'}, dimensions={0} | all-to-all | bytes 307200 | tf_op jit(solution)/shard_map/all_to_all | solution.py:32
  339.0 0.1 copy.24
  339.1 0.8 all_to_all.32
  (1 shorter events, 0.0 us)
Async XLA Ops:
  6.5 1.7 copy-start
  6.5 280.8 %all-reduce.2.cloned.1.call-start = ((), (), s32[]{:S(2)}) async-start(), calls=%async_computation.2 | async-start | bytes 4915200 | tf_op jit(solution)/shard_map/psum | solution.py:20
  11.3 1.1 copy-start.1
  17.6 16.6 %copy-start.2 = (s32[512,8]{0,1:T(8,128)S(1)}, s32[512,8]{0,1:T(8,128)}, u32[]{:S(2)}) copy-start(s32[512,8]{0,1:T(8,128)} %param.10) | copy-start | bytes 49156
  17.6 16.8 %copy-start.3 = (f32[512,8]{0,1:T(8,128)S(1)}, f32[512,8]{0,1:T(8,128)}, u32[]{:S(2)}) copy-start(f32[512,8]{0,1:T(8,128)} %param.9) | copy-start | bytes 49156
  17.6 16.9 %copy-start.4 = (s32[512]{0:T(512)S(1)}, s32[512]{0:T(512)}, u32[]{:S(2)}) copy-start(s32[512]{0:T(512)} %param.11) | copy-start | bytes 6148
  21.0 285.8 %all-to-all-start = ((bf16[75,64,75]{0,2,1:T(8,128)(2,1)}), bf16[75,64,75]{0,2,1:T(8,128)(2,1)}, u32[]{:S(2)}, u32[]{:S(2)}) async-start(bf16[75,64,75]{0,2,1:T(8,128)(2,1)} %copy.22), calls=%async_computation | async-start | bytes 2621440 | tf_op jit(solution)/shard_map/all_to_all | solution.py:16
  34.2 253.1 %copy-start.5 = (s32[512]{0:T(512)S(1)}, s32[512]{0:T(512)}, u32[]{:S(2)}) copy-start(s32[512]{0:T(512)} %param.12) | copy-start | bytes 6148
Sparse Core Ops, SparseCore 0:
  12.8 274.4 all-reduce.1

commit v2 on v1

v2 whole, which is shorter than its diff:
```python
import jax
import jax.numpy as jnp
from jax import lax
from jax.experimental import pallas as pl
from jax.experimental.pallas import tpu as pltpu
from jax.sharding import PartitionSpec as P

NB = 40
LANE = 128
RING = 4
DEPTH = 8
CHIPS = RING * DEPTH
EXTRA = 6
F32 = jnp.float32
BF16 = jnp.bfloat16


def kernel(
    disc, sens, cash, index, exer, steps, jac, out,
    s_out, s_in, d_in, xp, r1, y2, r2, zb, rz, zr, zf, g2, xf,
    jp, jr, jf, jb, mk, pm, pr, po, ob,
    ss_s, rs_s, ss_1, rs_1, ss_2, rs_2, ss_z, rs_z, ss_g, rs_g,
    ss_a2, rs_a2, ss_a1, rs_a1, ss_j, rs_j, ss_p, rs_p, ss_o, rs_o,
):
    y = lax.axis_index("grp")
    me = lax.axis_index("path")
    j = lax.div(me, 2)
    c = lax.rem(me, 2)
    x = lax.div(j, DEPTH)
    z = lax.rem(j, DEPTH)
    sib = 1 - c
    paths = 2 * CHIPS
    half = xp.shape[0]
    params = sens.shape[1]
    width = params // NB
    split = half * LANE
    cut = half // 2 + 1
    quarter = (cut + 1) // 2
    parts = ((0, cut), (cut, half - cut))

    def halves(part):
        t0, n = parts[part]
        return (t0, quarter), (t0 + quarter, n - quarter)

    def at_chip(xx, zz, cc):
        return {"grp": y, "path": (xx * DEPTH + zz) * 2 + cc}

    def at_grp(yy):
        return {"grp": yy, "path": me}

    def rdma(src, dst, ss, rs, dev):
        return pltpu.make_async_remote_copy(
            src_ref=src, dst_ref=dst, send_sem=ss, recv_sem=rs,
            device_id=dev, device_id_type=pl.DeviceIdType.MESH,
        )

    sent = []

    def send(*args):
        d = rdma(*args)
        d.start()
        sent.append(d)

    ring_x = (x, at_chip(lax.rem(x + 1, RING), z, c), at_chip(lax.rem(x + 3, RING), z, c))
    ring_y = (y, at_grp(lax.rem(y + 1, RING)), at_grp(lax.rem(y + 3, RING)))
    sibling = at_chip(x, z, sib)

    barrier = pltpu.get_barrier_semaphore()
    for d in (ring_y[1], ring_y[2]):
        pl.semaphore_signal(barrier, inc=1, device_id=d, device_id_type=pl.DeviceIdType.MESH)

    @pl.loop(1, paths)
    def _(k):
        pl.semaphore_signal(
            barrier, inc=1, device_id={"grp": y, "path": lax.rem(me + k, paths)},
            device_id_type=pl.DeviceIdType.MESH,
        )

    last = half - 1
    tail = params - split - last * LANE

    @pl.loop(0, last)
    def _(t):
        s_out[t] = sens[:, pl.ds(pl.multiple_of((sib * half + t) * LANE, LANE), LANE)]

    @pl.when(sib == 0)
    def _():
        s_out[last] = sens[:, last * LANE : split]

    @pl.when(sib == 1)
    def _():
        s_out[last] = jnp.zeros(s_out.shape[1:], BF16)
        s_out[last, :, 0:tail] = sens[:, split + last * LANE : params]

    d_own = disc[...].astype(F32).T.astype(BF16)

    pl.semaphore_wait(barrier, paths + 1)

    send(disc, d_in, ss_s.at[4], rs_s.at[4], sibling)
    pieces = (halves(0)[0], halves(1)[0], halves(0)[1], halves(1)[1])
    for q, (t0, n) in enumerate(pieces):
        blk = pl.ds(t0, n)
        send(s_out.at[blk], s_in.at[blk], ss_s.at[q], rs_s.at[q], sibling)

    @pl.loop(0, last)
    def _(t):
        xp[t] = jnp.dot(
            d_own, sens[:, pl.ds(pl.multiple_of((c * half + t) * LANE, LANE), LANE)],
            preferred_element_type=F32,
        )

    @pl.when(c == 0)
    def _():
        xp[last] = jnp.dot(d_own, sens[:, last * LANE : split], preferred_element_type=F32)

    @pl.when(c == 1)
    def _():
        xp[last] = jnp.zeros(xp.shape[1:], F32)
        xp[last, :, 0:tail] = jnp.dot(
            d_own, sens[:, split + last * LANE : params], preferred_element_type=F32
        )

    rdma(disc, d_in, ss_s.at[4], rs_s.at[4], sibling).wait_recv()
    d_sib = d_in[...].astype(F32).T.astype(BF16)

    def rows(k, size):
        return pl.ds(pl.multiple_of(k * size, size), size)

    class Scatter:
        def __init__(self, src, rbuf, ss, rs, ring, hs, size):
            self.src, self.rbuf, self.ss, self.rs, self.hs = src, rbuf, ss, rs, hs
            i, self.right, self.left = ring
            self.own = rows(i, size)
            self.nr, self.far, self.nl = (rows(lax.rem(i + k, RING), size) for k in (1, 2, 3))

        def msg(self, n, h, rws, dev):
            t0, cnt = self.hs[h]
            return (
                self.src.at[pl.ds(t0, cnt), rws], self.rbuf.at[n, pl.ds(0, cnt)],
                self.ss.at[n], self.rs.at[n], dev,
            )

        def first(self, h):
            if h == 0:
                send(*self.msg(0, 0, self.far, self.right))
                send(*self.msg(1, 0, self.nl, self.left))
            else:
                send(*self.msg(2, 1, self.far, self.left))
                send(*self.msg(3, 1, self.nr, self.right))

        def second(self, h):
            n, rws, dev = ((0, self.nr, self.right), (2, self.nl, self.left))[h]
            t0, cnt = self.hs[h]
            rdma(*self.msg(n, h, rws, dev)).wait_recv()
            self.src[pl.ds(t0, cnt), rws] += self.rbuf[n, 0:cnt]
            send(*self.msg(4 + h, h, rws, dev))

        def result(self, h):
            t0, cnt = self.hs[h]
            n = (1, 3)[h]
            rdma(*self.msg(n, h, self.own, self.left)).wait_recv()
            rdma(*self.msg(4 + h, h, self.own, self.left)).wait_recv()
            return (
                self.src[pl.ds(t0, cnt), self.own]
                + self.rbuf[n, 0:cnt]
                + self.rbuf[4 + h, 0:cnt]
            )

    rings = (ring_x, ring_y)
    big, small = xp.shape[1] // RING, xp.shape[1] // RING // RING
    one = [
        Scatter(xp, r1.at[p], ss_1.at[p], rs_1.at[p], rings[p], halves(p), big) for p in (0, 1)
    ]
    for q, (t0, n) in enumerate(pieces):
        blk = pl.ds(t0, n)
        rdma(s_out.at[blk], s_in.at[blk], ss_s.at[q], rs_s.at[q], sibling).wait_recv()

        @pl.loop(t0, t0 + n)
        def _(t):
            xp[t] += jnp.dot(d_sib, s_in[t], preferred_element_type=F32)

        one[q % 2].first(q // 2)

    jt = jp.shape[0]
    jrows = jac.shape[0]
    jp[...] = jnp.zeros(jp.shape, BF16)

    @pl.loop(0, jt - 1)
    def _(t):
        jp[t, 0:jrows] = jac[:, pl.ds(pl.multiple_of(t * LANE, LANE), LANE)]

    jl = params - (jt - 1) * LANE
    jp[jt - 1, 0:jrows, 0:jl] = jac[:, (jt - 1) * LANE : params]

    for h in (0, 1):
        for p in (0, 1):
            one[p].second(h)

    top = lax.div(me, CHIPS)
    slot = me - CHIPS * top
    straddle = me == CHIPS

    def j_one(tile, e, chip, core, sl, sem):
        dst = chip * 2 + core

        @pl.when(dst == me)
        def _():
            pltpu.make_async_copy(jp.at[tile], jr.at[e, sl], rs_j.at[e, sl]).start()

        @pl.when(dst != me)
        def _():
            rdma(
                jp.at[tile], jr.at[e, sl], sem, rs_j.at[e, sl], {"grp": y, "path": dst}
            ).start()

    @pl.loop(0, CHIPS)
    def _(k):
        chip = lax.rem(j + k, CHIPS)
        j_one(chip, 0, chip, top, slot, ss_j.at[0, chip])

        @pl.when(straddle)
        def _():
            j_one(chip, 0, chip, 0, CHIPS, ss_j.at[1, chip])

    @pl.loop(0, EXTRA)
    def _(e):
        chip = 5 * e + 2
        j_one(CHIPS + e, 1, chip, top, slot, ss_j.at[0, CHIPS + e])

        @pl.when(straddle)
        def _():
            j_one(CHIPS + e, 1, chip, 0, CHIPS, ss_j.at[1, CHIPS + e])

    trades, slots = cash.shape
    forwards = lax.broadcasted_iota(jnp.int32, (trades, LANE), 1)
    late = forwards >= exer[...]
    weights = jnp.zeros((trades, LANE), F32)
    for s in range(slots):
        weights += jnp.where(late & (index[:, s : s + 1] == forwards), cash[:, s : s + 1], 0.0)
    weights = weights * (1.0 / (sens.shape[0] * paths * RING))
    w_hi = weights.astype(BF16)
    w_lo = (weights - w_hi.astype(F32)).astype(BF16)
    wide = jnp.concatenate([w_hi, w_hi, w_lo], axis=1)
    jf[...] = jnp.zeros(jf.shape, F32)

    two = [
        Scatter(y2, r2.at[p], ss_2.at[p], rs_2.at[p], rings[1 - p], halves(p), small)
        for p in (0, 1)
    ]
    for h in (0, 1):
        for p in (0, 1):
            t0, cnt = halves(p)[h]
            y2[pl.ds(t0, cnt)] = one[p].result(h)
            two[p].first(h)
    for h in (0, 1):
        for p in (0, 1):
            two[p].second(h)
    share = zr.shape[0]
    zb[pl.ds(half, zb.shape[0] - half)] = jnp.zeros((zb.shape[0] - half,) + zb.shape[1:], F32)
    for h in (0, 1):
        for p in (0, 1):
            t0, cnt = halves(p)[h]
            zb[pl.ds(t0, cnt)] = two[p].result(h)

    def z_at(k):
        return lax.rem(z + k, DEPTH)

    for k in range(1, DEPTH):
        d = z_at(k)
        send(
            zb.at[pl.ds(d * share, share)], rz.at[z], ss_z.at[k], rs_z.at[z], at_chip(x, d, c)
        )
    acc = zb[pl.ds(z * share, share)]
    for k in range(1, DEPTH):
        d = z_at(k)
        rdma(zr, rz.at[d], ss_z.at[k], rs_z.at[d], at_chip(x, d, c)).wait_recv()
        acc += rz[d]
    zr[...] = acc
    mine = pl.ds(z * share, share)
    for k in range(1, DEPTH):
        d = z_at(k)
        send(zr, zf.at[mine], ss_g.at[k], rs_g.at[z], at_chip(x, d, c))
    zf[mine] = acc

    has_extra = (lax.rem(j, 5) == 2) & (j < 5 * EXTRA)
    pad_rows = jp.shape[1]

    def take(e):
        lanes = slice(e * LANE, (e + 1) * LANE)

        def strip_rows(s):
            pltpu.make_async_copy(jp.at[0], jr.at[e, s], rs_j.at[e, s]).wait()
            return jr[e, s].astype(F32)

        @pl.loop(0, CHIPS // DEPTH)
        def _(q):
            first = pl.multiple_of(q * (jrows * DEPTH), DEPTH)
            view = jf.at[pl.ds(first, jrows * DEPTH + DEPTH)]
            for r in range(DEPTH):
                view[r * jrows : r * jrows + pad_rows, lanes] = strip_rows(q * DEPTH + r)

        @pl.when(c == 0)
        def _():
            jf[CHIPS * jrows : CHIPS * jrows + pad_rows, lanes] = strip_rows(CHIPS)

    take(0)

    @pl.when(has_extra)
    def _():
        take(1)

    base = split - (split // jrows) * jrows
    jb[...] = jf[pl.ds(pl.multiple_of(base * c, 8), jb.shape[0])].astype(BF16)

    for k in range(1, DEPTH):
        d = z_at(k)
        rdma(zr, zf.at[pl.ds(d * share, share)], ss_g.at[k], rs_g.at[d], sibling).wait_recv()

    class Gather:
        def __init__(self, buf, ss, rs, ring, hs, size):
            self.buf, self.ss, self.rs, self.hs = buf, ss, rs, hs
            i, self.right, self.left = ring
            self.own = rows(i, size)
            self.nr, self.far, self.nl = (rows(lax.rem(i + k, RING), size) for k in (1, 2, 3))

        def msg(self, n, h, rws, dev):
            t0, cnt = self.hs[h]
            ref = self.buf.at[pl.ds(t0, cnt), rws]
            return ref, ref, self.ss.at[n], self.rs.at[n], dev

        def start(self):
            send(*self.msg(0, 0, self.own, self.right))
            send(*self.msg(2, 1, self.own, self.left))
            send(*self.msg(1, 1, self.own, self.right))
            send(*self.msg(3, 0, self.own, self.left))

        def forward(self):
            rdma(*self.msg(0, 0, self.nl, self.right)).wait_recv()
            send(*self.msg(4, 0, self.nl, self.right))
            rdma(*self.msg(2, 1, self.nr, self.left)).wait_recv()
            send(*self.msg(5, 1, self.nr, self.left))

        def finish(self):
            rdma(*self.msg(1, 1, self.nl, self.right)).wait_recv()
            rdma(*self.msg(3, 0, self.nr, self.left)).wait_recv()
            rdma(*self.msg(4, 0, self.far, self.right)).wait_recv()
            rdma(*self.msg(5, 1, self.far, self.left)).wait_recv()

    back2 = [
        Gather(g2, ss_a2.at[p], rs_a2.at[p], rings[1 - p], halves(p), small) for p in (0, 1)
    ]
    for p in (0, 1):
        t0, cnt = parts[p]
        g2[pl.ds(t0, cnt), back2[p].own] = zf[pl.ds(t0, cnt)]
        back2[p].start()
    for p in (0, 1):
        back2[p].forward()
    back1 = [Gather(xf, ss_a1.at[p], rs_a1.at[p], rings[p], halves(p), big) for p in (0, 1)]
    for p in (0, 1):
        t0, cnt = parts[p]
        back2[p].finish()
        xf[pl.ds(t0, cnt), back1[p].own] = g2[pl.ds(t0, cnt)]
        back1[p].start()
    for p in (0, 1):
        back1[p].forward()
    for p in (0, 1):
        back1[p].finish()

    reach = steps[...] * width - c * split

    def masked(t, n):
        span = n * LANE
        block = jnp.concatenate([xf[t + k] for k in range(n)], axis=1)
        hi = block.astype(BF16)
        lo = (block - hi.astype(F32)).astype(BF16)
        vega = jnp.dot(wide, jnp.concatenate([hi, lo, hi], axis=0), preferred_element_type=F32)
        column = lax.broadcasted_iota(jnp.int32, (trades, span), 1) + t * LANE
        cols = pl.ds(pl.multiple_of(t * LANE, LANE), span)
        mk[:, cols] = jnp.where(column < reach, vega, 0.0).astype(BF16)

    @pl.loop(0, half // 2)
    def _(i):
        masked(2 * i, 2)

    masked(half - 1, 1)

    block_rows = trades // RING
    strip = out.shape[0]

    def block_copy(e, b):
        blk = rows(b, DEPTH)
        return (
            pm.at[e, blk, sib], pr.at[e, blk], ss_p.at[e, b], rs_p.at[e, b], sibling,
        )

    @pl.loop(0, RING)
    def _(b):
        part = jnp.dot(
            mk[rows(b, block_rows)], jb[...], preferred_element_type=F32
        )
        for e in (0, 1):
            pm[e, rows(b, DEPTH)] = part[:, e * LANE : (e + 1) * LANE].reshape(
                DEPTH, 2, strip, LANE
            )
        rdma(*block_copy(0, b)).start()

        @pl.when(has_extra)
        def _():
            rdma(*block_copy(1, b)).start()

    def finish_block(e, tile, b):
        rdma(*block_copy(e, b)).wait()
        blk = rows(b, DEPTH)
        po[e, blk] = pm[e, blk, c] + pr[e, blk]

        @pl.loop(b * DEPTH, (b + 1) * DEPTH)
        def _(k):
            @pl.when(k != j)
            def _():
                rdma(
                    po.at[e, k], ob.at[tile], ss_o.at[e, k], rs_o.at[tile],
                    {"grp": y, "path": 2 * k + c},
                ).start()

            @pl.when(k == j)
            def _():
                ob[tile] = po[e, k]

    @pl.loop(0, RING)
    def _(b):
        finish_block(0, j, b)

        @pl.when(has_extra)
        def _():
            finish_block(1, CHIPS + lax.div(j, 5), b)

    @pl.loop(0, jt)
    def _(t):
        owner = jnp.where(t < CHIPS, t, 5 * (t - CHIPS) + 2)

        @pl.when(owner != j)
        def _():
            rdma(po.at[0, 0], ob.at[t], ss_o.at[0, 0], rs_o.at[t], sibling).wait_recv()

    for t in range(jt - 1):
        out[:, t * LANE : (t + 1) * LANE] = ob[t]
    out[:, (jt - 1) * LANE : params] = ob[jt - 1, :, 0:jl]

    for d in sent:
        d.wait_send()

    def j_sent(n, tile, chip, core):
        @pl.when(chip * 2 + core != me)
        def _():
            rdma(
                jp.at[0], jr.at[0, 0], ss_j.at[n, tile], rs_j.at[0, 0], sibling
            ).wait_send()

    @pl.loop(0, jt)
    def _(t):
        owner = jnp.where(t < CHIPS, t, 5 * (t - CHIPS) + 2)
        j_sent(0, t, owner, top)

        @pl.when(straddle)
        def _():
            j_sent(1, t, owner, 0)

    @pl.loop(0, CHIPS)
    def _(k):
        @pl.when(k != j)
        def _():
            rdma(po.at[0, 0], ob.at[0], ss_o.at[0, k], rs_o.at[0], sibling).wait_send()

            @pl.when(has_extra)
            def _():
                rdma(po.at[0, 0], ob.at[0], ss_o.at[1, k], rs_o.at[0], sibling).wait_send()


def per_device(
    path_sens, discounts, cash_flows, flow_index, exercise_step, trade_steps, jacobian_inv
):
    paths_own, params = path_sens.shape
    forwards = discounts.shape[1]
    trades = cash_flows.shape[0]
    jrows = jacobian_inv.shape[0]
    strip = trades // (2 * CHIPS)
    tiles = -(-params // LANE)
    half = -(-tiles // 2)
    cut = half // 2 + 1
    quarter = (cut + 1) // 2
    big, small = forwards // RING, forwards // RING // RING
    share = -(-half // DEPTH)
    padded = -(-jrows // 16) * 16
    vm = pltpu.VMEM
    dma = pltpu.SemaphoreType.DMA
    scratch = [
        vm((half, paths_own, LANE), BF16),
        vm((half, paths_own, LANE), BF16),
        vm((paths_own, forwards), BF16),
        vm((half, forwards, LANE), F32),
        vm((2, 6, quarter, big, LANE), F32),
        vm((half, big, LANE), F32),
        vm((2, 6, quarter, small, LANE), F32),
        vm((share * DEPTH, small, LANE), F32),
        vm((DEPTH, share, small, LANE), F32),
        vm((share, small, LANE), F32),
        vm((share * DEPTH, small, LANE), F32),
        vm((half, big, LANE), F32),
        vm((half, forwards, LANE), F32),
        vm((tiles, padded, LANE), BF16),
        vm((2, CHIPS + 1, padded, LANE), BF16),
        vm(((CHIPS + 2) * padded, 2 * LANE), F32),
        vm((half * LANE, 2 * LANE), BF16),
        vm((trades, half * LANE), BF16),
        vm((2, CHIPS, 2, strip, LANE), F32),
        vm((2, CHIPS, strip, LANE), F32),
        vm((2, CHIPS, strip, LANE), F32),
        vm((tiles, strip, LANE), F32),
        dma((5,)), dma((5,)),
        dma((2, 6)), dma((2, 6)),
        dma((2, 6)), dma((2, 6)),
        dma((DEPTH,)), dma((DEPTH,)),
        dma((DEPTH,)), dma((DEPTH,)),
        dma((2, 6)), dma((2, 6)),
        dma((2, 6)), dma((2, 6)),
        dma((2, tiles)), dma((2, CHIPS + 1)),
        dma((2, RING)), dma((2, RING)),
        dma((2, CHIPS)), dma((tiles,)),
    ]
    return pl.pallas_call(
        kernel,
        out_shape=jax.ShapeDtypeStruct((strip, params), F32),
        in_specs=[pl.BlockSpec(memory_space=pltpu.VMEM)] * 7,
        out_specs=pl.BlockSpec(memory_space=pltpu.VMEM),
        scratch_shapes=scratch,
        compiler_params=pltpu.CompilerParams(
            collective_id=0, has_side_effects=True, vmem_limit_bytes=56 * 1024 * 1024
        ),
    )(
        discounts,
        path_sens,
        cash_flows,
        flow_index,
        exercise_step.reshape(trades, 1),
        trade_steps.reshape(trades, 1),
        jacobian_inv,
    )


def solution(mesh):
    placed = (
        P(("grp", "path"), None),
        P(("grp", "path"), None),
        P("grp", None),
        P("grp", None),
        P("grp"),
        P("grp"),
        P("path", None),
    )
    return jax.shard_map(
        per_device, mesh=mesh, in_specs=placed, out_specs=P(("grp", "path"), None), check_vma=False
    )
```

time: 347 us -> 98 us (0.28)
  waiting for transfers between devices: 249 us -> 0 us
  Pallas kernels: 0 us -> 84.7 us
  matrix products: 22.9 us -> 0 us
  blocking collectives: 22.9 us -> 0 us
  between operations: 13.5 us -> 0.01 us
  local copies, waits for them, and re-layouts: 25.5 us -> 12.1 us
  starting transfers between devices: 13.2 us -> 0 us
    psum x1 -> x0, waiting for transfers between devices: 249 us -> none  [per_device(): moments = lax.psum(moments, ('grp', 'path'))]
    pallas_call x0 -> x1, Pallas kernels: none -> 84.7 us  [per_device(): pl.pallas_call(kernel, out_shape=jax.ShapeDtypeStruct((strip, params), F3...]
    all_to_all x1 -> x0, blocking collectives: 22.9 us -> none  [per_device(): lax.all_to_all(quotes, 'path', split_axis=0, concat_axis=1, tiled=True)]
    dot_general x4 -> x0, matrix products: 22.9 us -> none  [the longest x1 12 us: per_device(): jnp.dot(weights, moments, precision=lax.Precision.HIGHEST) * path_scale]
    all_to_all x6 -> x0, local copies, waits for them, and re-layouts: 14.9 us -> none  [the longest x4 14 us: per_device(): lax.all_to_all(jacobian_inv, 'path', split_axis=1, concat_axis=0, tiled=T...]
    all_to_all x1 -> x0, starting transfers between devices: 13.2 us -> none  [per_device(): lax.all_to_all(jacobian_inv, 'path', split_axis=1, concat_axis=0, tiled=T...]
    convert_element_type x1 -> x0, local copies, waits for them, and re-layouts: 7.52 us -> none  [per_device(): jnp.where(bucket[None, :] < trade_steps[:, None], vega, 0.0)]
    unnamed x14 -> x4, local copies, waits for them, and re-layouts: 3.06 us -> 9.06 us
  transfers between devices with their start and end apart: 2 -> 0, of which waited for: 1 -> 0; matrix products, arithmetic and copies ran while one was open for 8% -> 0% of each run, Pallas kernels for 0% -> 0%
where the time goes in v2:
time: 98 us; the launch traced here: 96.8 us
  Pallas kernels  84.7 us (86%)
  local copies, waits for them, and re-layouts  12.1 us (12%)
    pallas_call x1, Pallas kernels, per_device(): pl.pallas_call(kernel, out_shape=jax.ShapeDtypeStruct((strip, params), F3...  84.7 us
    unnamed x4, local copies, waits for them, and re-layouts  9.06 us

profile of v2, /device:TPU:1, one launch (start us, length us, event | category | flops | bytes accessed | tf_op | source)
XLA Modules:
  0.0 96.8 jit_solution(15980848553297731209)
XLA Ops:
  0.0 1.6 %copy.12.cash = f32[512,8]{1,0:T(8,128)} copy(f32[512,8]{0,1:T(8,128)} %param.9) | data formatting | bytes 32768 | tf_op args[2]
  1.6 1.6 %copy.13.index = s32[512,8]{1,0:T(8,128)} copy(s32[512,8]{0,1:T(8,128)} %param.10) | data formatting | bytes 32768 | tf_op args[3]
  3.1 1.5 %copy.14.exer = s32[512,1]{1,0:T(8,128)} copy(s32[512,1]{0,1:T(1,128)} %bitcast.2) | data formatting | bytes 4096 | tf_op jit(solution)/shard_map/reshape | solution.py:544
  4.7 1.5 %copy.15.steps = s32[512,1]{1,0:T(8,128)} copy(s32[512,1]{0,1:T(1,128)} %bitcast.3) | data formatting | bytes 4096 | tf_op jit(solution)/shard_map/reshape | solution.py:545
  6.2 4.4 %copy.11.sens = bf16[256,4800]{1,0:T(8,128)(2,1)} copy(bf16[256,4800]{0,1:T(8,128)(2,1)} %param.7) | data formatting | bytes 4915200 | tf_op args[0]
  10.5 84.7 %shard_map.73 = f32[8,4800]{1,0:T(8,128)} custom-call(bf16[256,128]{1,0:T(8,128)(2,1)} %disc.1, bf16[256,4800]{1,0:T(8,128)(2,1)} %copy.11.sens, f32[512,8]{1,0:T(8,128)} %copy.12.cash, s32[512,8]{1,0:T(8,128)} %copy.13.index, s32[512,1]{1,0:T(8,128)} %copy.14.exer, s32[512,1]{1,0:T(8,128)} %copy.15.steps, bf16[75,4800]{1,0:T(8,128)(2,1)} %jac.1), custom_call_target="tpu_custom_call" | custom-call | tf_op jit(solution)/shard_map/pallas_call | solution.py:530
  95.2 1.6 %copy.17 = f32[8,4800]{1,0:T(8,128)} copy(f32[8,4800]{1,0:T(8,128)} %shard_map.73) | data formatting | bytes 307200

commit v3 on v1

v3 whole, which is shorter than its diff:
```python
import jax
import jax.numpy as jnp
from jax import lax
from jax.experimental import pallas as pl
from jax.experimental.pallas import tpu as pltpu
from jax.sharding import PartitionSpec as P

NB = 40
LANE = 128
RING = 4
DEPTH = 8
CHIPS = RING * DEPTH
PATHS = 2 * CHIPS
EXTRA = 6
F32 = jnp.float32
BF16 = jnp.bfloat16
MESH = pl.DeviceIdType.MESH


def kernel(
    disc, sens, cash, index, exer, steps, jac, out,
    s_own, s_in, d_in, xs, xp, r1, y2, r2, zb, rz, zr, zf, xf,
    jv, jp, jr, jt, mk, acc, acce, pr, pre, po, ob,
    ss_s, rs_s, ls, ss_1, rs_1, ss_2, rs_2, ss_z, rs_z, ss_g, rs_g,
    ss_a2, rs_a2, ss_a1, rs_a1, ss_j, rs_j, ss_ja, rs_ja, ss_p, rs_p, ss_o, rs_o,
):
    y = lax.axis_index("grp")
    me = lax.axis_index("path")
    j = lax.div(me, 2)
    c = lax.rem(me, 2)
    x = lax.div(j, DEPTH)
    z = lax.rem(j, DEPTH)
    sib = 1 - c
    params = sens.shape[0]
    width = params // NB
    half = params // 2
    jrows = jac.shape[0]
    pad = xp.shape[2] // 2
    trades = cash.shape[1]

    def at_chip(xx, zz, cc):
        return {"grp": y, "path": (xx * DEPTH + zz) * 2 + cc}

    def rdma(src, dst, ss, rs, dev):
        return pltpu.make_async_remote_copy(
            src_ref=src, dst_ref=dst, send_sem=ss, recv_sem=rs, device_id=dev, device_id_type=MESH
        )

    sent = []

    def send(*args):
        d = rdma(*args)
        d.start()
        sent.append(d)

    sibling = at_chip(x, z, sib)

    def on_x(k):
        return at_chip(lax.rem(x + k, RING), z, c)

    def on_y(k):
        return {"grp": lax.rem(y + k, RING), "path": me}

    def on_z(k):
        return at_chip(x, lax.rem(z + k, DEPTH), c)

    lines = ((x, on_x), (y, on_y))

    barrier = pltpu.get_barrier_semaphore()
    partners = (
        [sibling]
        + [on_x(k) for k in range(1, RING)]
        + [on_y(k) for k in range(1, RING)]
        + [on_z(k) for k in range(1, DEPTH)]
    )
    for d in partners:
        pl.semaphore_signal(barrier, inc=1, device_id=d, device_id_type=MESH)

    own_half = pltpu.make_async_copy(
        sens.at[pl.ds(pl.multiple_of(c * half, 16), half)], s_own, ls.at[0]
    )
    own_half.start()
    jac_in = pltpu.make_async_copy(jac, jv, ls.at[1])
    jac_in.start()

    first_cut = (half // 4 // 16 + 1) * 16
    cuts = (0, first_cut, half // 2, half // 2 + first_cut, half)
    order = (0, 2, 1, 3)

    def s_copy(q):
        n = cuts[q + 1] - cuts[q]
        return (
            sens.at[pl.ds(pl.multiple_of(sib * half + cuts[q], 16), n)],
            s_in.at[pl.ds(cuts[q], n)], ss_s.at[q], rs_s.at[q], sibling,
        )

    d_copy = (disc, d_in, ss_s.at[4], rs_s.at[4], sibling)

    slots = cash.shape[0]
    forwards = lax.broadcasted_iota(jnp.int32, (LANE, trades), 0)
    late = forwards >= exer[...]
    weights = jnp.zeros((LANE, trades), F32)
    for s in range(slots):
        weights += jnp.where(late & (index[s : s + 1] == forwards), cash[s : s + 1], 0.0)
    weights = weights * (1.0 / (disc.shape[0] * PATHS * RING))
    w_hi = weights.astype(BF16)
    w_lo = (weights - w_hi.astype(F32)).astype(BF16)
    wide = jnp.concatenate([w_hi, w_hi, w_lo], axis=0)

    pl.semaphore_wait(barrier, len(partners))
    send(*d_copy)
    for q in order:
        send(*s_copy(q))

    own_half.wait()
    xs[half : half + 8] = jnp.zeros((8, LANE), F32)
    for q in order:
        xs[cuts[q] : cuts[q + 1]] = jnp.dot(
            s_own[cuts[q] : cuts[q + 1]], disc[...], preferred_element_type=F32
        )

    class Scatter:
        def __init__(self, p):
            self.p = p
            self.i, self.on = lines[p]
            self.own = self.i
            self.nr, self.far, self.nl = (lax.rem(self.i + k, RING) for k in (1, 2, 3))
            self.right, self.left = self.on(1), self.on(3)

        def msg(self, n, h, k, dev):
            p = self.p
            return xp.at[2 * p + h, k], r1.at[p, n], ss_1.at[p, n], rs_1.at[p, n], dev

        def first(self, h):
            if h == 0:
                send(*self.msg(0, 0, self.far, self.right))
                send(*self.msg(1, 0, self.nl, self.left))
            else:
                send(*self.msg(2, 1, self.far, self.left))
                send(*self.msg(3, 1, self.nr, self.right))

        def second(self, h):
            n, k, dev = ((0, self.nr, self.right), (2, self.nl, self.left))[h]
            rdma(*self.msg(n, h, k, dev)).wait_recv()
            xp[2 * self.p + h, k] += r1[self.p, n]
            send(*self.msg(4 + h, h, k, dev))

        def result(self, h):
            n = (1, 3)[h]
            rdma(*self.msg(n, h, self.own, self.left)).wait_recv()
            rdma(*self.msg(4 + h, h, self.own, self.left)).wait_recv()
            return xp[2 * self.p + h, self.own] + r1[self.p, n] + r1[self.p, 4 + h]

    one = [Scatter(p) for p in (0, 1)]
    rdma(*d_copy).wait_recv()
    for q in order:
        rdma(*s_copy(q)).wait_recv()
        xs[cuts[q] : cuts[q + 1]] += jnp.dot(
            s_in[cuts[q] : cuts[q + 1]], d_in[...], preferred_element_type=F32
        )
        for k in range(RING):
            for u in (0, 1):
                top = (8 * q + 2 * k + u) * jrows
                xp[q, k, u * pad : (u + 1) * pad] = xs[top : top + pad]
        one[q // 2].first(q % 2)

    tiles = jp.shape[0]
    tail = params - (tiles - 1) * LANE
    turn = lax.rem(z, RING) == y
    core = lax.div(x, 2)
    strip = jr.at[:, 2 * lax.rem(x, 2) + lax.div(z, RING), y, pl.ds(pl.multiple_of(c * pad, 16), pad)]
    j_sem = 4 * lax.rem(x, 2) + 2 * lax.div(z, RING) + c
    jac_in.wait()

    @pl.when(turn)
    def _():
        jp[...] = jnp.zeros(jp.shape, BF16)

        @pl.loop(0, tiles - 1)
        def _(t):
            jp[t, 0:jrows] = jv[:, pl.ds(pl.multiple_of(t * LANE, LANE), LANE)]

        jp[tiles - 1, 0:jrows, 0:tail] = jv[:, (tiles - 1) * LANE : params]

    def j_column(step):
        xx = lax.rem(x + step, RING)

        def one_tile(e, tile, zz):
            dst = (xx * DEPTH + zz) * 2 + core
            n = step * (DEPTH + EXTRA) + e * DEPTH + zz

            @pl.when(dst == me)
            def _():
                pltpu.make_async_copy(jp.at[tile], strip.at[e], rs_j.at[e, j_sem]).start()

            @pl.when(dst != me)
            def _():
                rdma(
                    jp.at[tile], strip.at[e], ss_j.at[n], rs_j.at[e, j_sem],
                    {"grp": y, "path": dst},
                ).start()

        @pl.when(turn)
        def _():
            @pl.loop(0, DEPTH)
            def _(zz):
                one_tile(0, xx * DEPTH + zz, zz)

            @pl.loop(0, EXTRA)
            def _(zz):
                one_tile(1, CHIPS + zz, zz)

    j_column(0)
    for h in (0, 1):
        for p in (0, 1):
            one[p].second(h)
    j_column(1)
    j_column(3)

    for h in (0, 1):
        for p in (0, 1):
            y2[p, 2 * h : 2 * h + 2] = one[p].result(h).reshape(2, pad, LANE)

    def two(p, k):
        i, on = lines[1 - p]
        to = lax.rem(i + k, RING)
        return y2.at[p, to], r2.at[p, i], ss_2.at[p, k], rs_2.at[p, i], on(k)

    for k in (1, 3, 2):
        for p in (0, 1):
            send(*two(p, k))
    j_column(2)

    zb[2 * pad :] = jnp.zeros((zb.shape[0] - 2 * pad, LANE), F32)
    for p in (0, 1):
        i, on = lines[1 - p]
        total = y2[p, i]
        for k in (1, 3, 2):
            frm = lax.rem(i + k, RING)
            rdma(y2.at[p, i], r2.at[p, frm], ss_2.at[p, k], rs_2.at[p, frm], on(k)).wait_recv()
            total += r2[p, frm]
        zb[p * pad : (p + 1) * pad] = total

    share = zr.shape[0]

    def z_rows(d):
        return pl.ds(pl.multiple_of(d * share, 8), share)

    spread = (4, 3, 5, 2, 6, 1, 7)
    for k in spread:
        send(zb.at[z_rows(lax.rem(z + k, DEPTH))], rz.at[z], ss_z.at[k], rs_z.at[z], on_z(k))

    has_extra = z < EXTRA
    jblocks = jr.shape[1] * 2

    def j_ring(e, half_, k, n, dev):
        ref = jr.at[e, pl.ds(2 * half_, 2), k]
        return ref, ref, ss_ja.at[e, n], rs_ja.at[e, n], dev

    yr, yl = on_y(1), on_y(3)
    ynr, yfar, ynl = (lax.rem(y + k, RING) for k in (1, 2, 3))

    def j_start(e):
        for n in range(jblocks):
            pltpu.make_async_copy(
                jp.at[0], jr.at[e, n // 2, 0, pl.ds(0, pad)], rs_j.at[e, n]
            ).wait()
        for n, (hh, d) in enumerate(((0, yr), (1, yl), (1, yr), (0, yl))):
            rdma(*j_ring(e, hh, y, n, d)).start()

    def j_forward(e):
        rdma(*j_ring(e, 0, ynl, 0, yr)).wait_recv()
        rdma(*j_ring(e, 0, ynl, 4, yr)).start()
        rdma(*j_ring(e, 1, ynr, 1, yl)).wait_recv()
        rdma(*j_ring(e, 1, ynr, 5, yl)).start()

    def j_finish(e):
        for hh, k, n, d in ((1, ynl, 2, yr), (0, ynr, 3, yl), (0, yfar, 4, yr), (1, yfar, 5, yl)):
            rdma(*j_ring(e, hh, k, n, d)).wait_recv()

        @pl.loop(0, jr.shape[1] * RING)
        def _(n):
            block = jr[e, lax.div(n, RING), lax.rem(n, RING)]
            jt[e, n] = block.astype(F32).T.astype(BF16)

    def both(f):
        f(0)

        @pl.when(has_extra)
        def _():
            f(1)

    total = zb[z_rows(z)]
    for k in spread:
        d = lax.rem(z + k, DEPTH)
        rdma(zr, rz.at[d], ss_z.at[k], rs_z.at[d], on_z(k)).wait_recv()
        total += rz[d]
    zr[...] = total
    for k in spread:
        send(zr, zf.at[z_rows(z)], ss_g.at[k], rs_g.at[z], on_z(k))
    zf[z_rows(z)] = total

    both(j_start)

    for k in spread:
        d = lax.rem(z + k, DEPTH)
        rdma(zr, zf.at[z_rows(d)], ss_g.at[k], rs_g.at[d], on_z(k)).wait_recv()

    def strip_of(p, i):
        k = lines[p][0]
        return xf.at[2 * p + lax.div(i, 2), k, pl.ds(pl.multiple_of(lax.rem(i, 2) * pad, 8), pad)]

    def back2(p, k):
        i, on = lines[1 - p]
        return zf.at[pl.ds(p * pad, pad)], strip_of(p, i), ss_a2.at[p, k], rs_a2.at[p, i], on(k)

    for k in (2, 1, 3):
        for p in (0, 1):
            send(*back2(p, k))
    for p in (0, 1):
        i, _ = lines[1 - p]
        strip_of(p, i)[...] = zf[p * pad : (p + 1) * pad]

    both(j_forward)

    reach = steps[...] * width
    row = lax.broadcasted_iota(jnp.int32, (2 * pad, trades), 0)
    row = row - jnp.where(row >= pad, pad - jrows, 0) + c * half

    def block(ab, k, fresh=False):
        values = xf[ab, k]
        hi = values.astype(BF16)
        lo = (values - hi.astype(F32)).astype(BF16)
        vega = jnp.dot(jnp.concatenate([hi, lo, hi], axis=1), wide, preferred_element_type=F32)
        keep = row < reach - (8 * ab + 2 * k) * jrows
        masked = jnp.where(keep, vega, 0.0).astype(BF16)
        mk[...] = masked
        n = RING * ab + k
        part = jnp.dot(jt[0, n], masked, preferred_element_type=F32)
        for s in (0, 1):
            span = slice(s * trades // 2, (s + 1) * trades // 2)
            if fresh:
                acc[s] = part[:, span]
            else:
                acc[s] += part[:, span]

        @pl.when(has_extra)
        def _():
            mine = mk[:, pl.ds(pl.multiple_of(x * LANE, LANE), LANE)]
            more = jnp.dot(jt[1, n], mine, preferred_element_type=F32)
            if fresh:
                acce[...] = more
            else:
                acce[...] += more

    class Gather:
        def __init__(self, p):
            self.p = p
            self.i, self.on = lines[p]
            self.nr, self.far, self.nl = (lax.rem(self.i + k, RING) for k in (1, 2, 3))
            self.right, self.left = self.on(1), self.on(3)

        def msg(self, n, h, k, dev):
            ref = xf.at[2 * self.p + h, k]
            return ref, ref, ss_a1.at[self.p, n], rs_a1.at[self.p, n], dev

        def start(self):
            send(*self.msg(0, 0, self.i, self.right))
            send(*self.msg(1, 1, self.i, self.left))
            send(*self.msg(2, 1, self.i, self.right))
            send(*self.msg(3, 0, self.i, self.left))

        def forward(self):
            rdma(*self.msg(0, 0, self.nl, self.right)).wait_recv()
            send(*self.msg(4, 0, self.nl, self.right))
            rdma(*self.msg(1, 1, self.nr, self.left)).wait_recv()
            send(*self.msg(5, 1, self.nr, self.left))

        def near(self):
            rdma(*self.msg(2, 1, self.nl, self.right)).wait_recv()
            rdma(*self.msg(3, 0, self.nr, self.left)).wait_recv()

        def end(self):
            rdma(*self.msg(4, 0, self.far, self.right)).wait_recv()
            rdma(*self.msg(5, 1, self.far, self.left)).wait_recv()

    ring = [Gather(p) for p in (0, 1)]
    for p in (0, 1):
        i, on = lines[1 - p]
        for k in (1, 3, 2):
            frm = lax.rem(i + k, RING)
            rdma(
                zf.at[pl.ds(p * pad, pad)], strip_of(p, frm), ss_a2.at[p, k], rs_a2.at[p, frm],
                on(k),
            ).wait_recv()
        ring[p].start()

    both(j_finish)

    def blocks(p, k, fresh=False):
        if fresh:
            block(2 * p, k, True)
            block(2 * p + 1, k)
        else:

            @pl.loop(2 * p, 2 * p + 2)
            def _(ab):
                block(ab, k)

    ring[0].forward()
    ring[1].forward()
    blocks(0, ring[0].i, True)
    blocks(1, ring[1].i)
    for p in (0, 1):
        ring[p].near()
        blocks(p, ring[p].nl)
        blocks(p, ring[p].nr)
    for p in (0, 1):
        ring[p].end()
        blocks(p, ring[p].far)

    swap = (acc.at[sib], pr, ss_p.at[0], rs_p.at[0], sibling)
    send(*swap)
    closer = lax.rem(z, 2)
    swap_extra = (acce, pre, ss_p.at[1], rs_p.at[1], sibling)

    @pl.when(has_extra & (c != closer))
    def _():
        rdma(*swap_extra).start()

    strip_rows = out.shape[0]
    rdma(*swap).wait_recv()
    po[0] = (acc[c] + pr[...]).T.reshape(CHIPS, strip_rows, LANE)

    def deliver(e, n, tile, dst):
        @pl.when(dst != me)
        def _():
            rdma(
                po.at[e, n], ob.at[tile], ss_o.at[e, n], rs_o.at[tile], {"grp": y, "path": dst}
            ).start()

        @pl.when(dst == me)
        def _():
            ob[tile] = po[e, n]

    @pl.loop(0, CHIPS)
    def _(n):
        deliver(0, n, j, c * CHIPS + n)

    closing = has_extra & (c == closer)

    @pl.when(closing)
    def _():
        rdma(*swap_extra).wait_recv()
        po[1, 0 : CHIPS // 2] = (acce[...] + pre[...]).T.reshape(CHIPS // 2, strip_rows, LANE)

        @pl.loop(0, CHIPS // 2)
        def _(n):
            deliver(1, n, CHIPS + z, x * (CHIPS // 2) + n)

    def arrived(tile, frm):
        @pl.when(frm != me)
        def _():
            rdma(po.at[0, 0], ob.at[tile], ss_o.at[0, 0], rs_o.at[tile], sibling).wait_recv()

    @pl.loop(0, CHIPS)
    def _(t):
        arrived(t, 2 * t + core)

    @pl.loop(0, EXTRA)
    def _(e):
        arrived(CHIPS + e, (x * DEPTH + e) * 2 + lax.rem(e, 2))

    for t in range(tiles - 1):
        out[:, t * LANE : (t + 1) * LANE] = ob[t]
    out[:, (tiles - 1) * LANE : params] = ob[tiles - 1, :, 0:tail]

    for d in sent:
        d.wait_send()

    @pl.when(has_extra & (c != closer))
    def _():
        rdma(*swap_extra).wait_send()

    def j_sent(e):
        for n, hh in enumerate((0, 1, 1, 0, 0, 1)):
            rdma(*j_ring(e, hh, y, n, yr)).wait_send()

    both(j_sent)

    @pl.when(turn)
    def _():
        for step in range(RING):
            xx = lax.rem(x + step, RING)

            @pl.loop(0, DEPTH + EXTRA)
            def _(n):
                zz = jnp.where(n < DEPTH, n, n - DEPTH)

                @pl.when((xx * DEPTH + zz) * 2 + core != me)
                def _():
                    rdma(
                        jp.at[0], strip.at[0], ss_j.at[step * (DEPTH + EXTRA) + n],
                        rs_j.at[0, 0], sibling,
                    ).wait_send()

    def po_sent(e, n, dst):
        @pl.when(dst != me)
        def _():
            rdma(po.at[0, 0], ob.at[0], ss_o.at[e, n], rs_o.at[0], sibling).wait_send()

    @pl.loop(0, CHIPS)
    def _(n):
        po_sent(0, n, c * CHIPS + n)

    @pl.when(closing)
    def _():
        @pl.loop(0, CHIPS // 2)
        def _(n):
            po_sent(1, n, x * (CHIPS // 2) + n)


def per_device(
    path_sens, discounts, cash_flows, flow_index, exercise_step, trade_steps, jacobian_inv
):
    paths_own, params = path_sens.shape
    trades = cash_flows.shape[0]
    jrows = jacobian_inv.shape[0]
    strip = trades // PATHS
    tiles = -(-params // LANE)
    pad = -(-jrows // 16) * 16
    half = params // 2
    share = -(-2 * pad // (8 * DEPTH)) * 8
    vm = pltpu.VMEM
    dma = pltpu.SemaphoreType.DMA
    scratch = [
        vm((half, paths_own), BF16),
        vm((half, paths_own), BF16),
        vm((paths_own, LANE), BF16),
        vm((half + 8, LANE), F32),
        vm((RING, RING, 2 * pad, LANE), F32),
        vm((2, 6, 2 * pad, LANE), F32),
        vm((2, RING, pad, LANE), F32),
        vm((2, RING, pad, LANE), F32),
        vm((share * DEPTH, LANE), F32),
        vm((DEPTH, share, LANE), F32),
        vm((share, LANE), F32),
        vm((share * DEPTH, LANE), F32),
        vm((RING, RING, 2 * pad, LANE), F32),
        vm((jrows, params), BF16),
        vm((tiles, pad, LANE), BF16),
        vm((2, RING, RING, 2 * pad, LANE), BF16),
        vm((2, RING * RING, LANE, 2 * pad), BF16),
        vm((2 * pad, trades), BF16),
        vm((2, LANE, trades // 2), F32),
        vm((LANE, LANE), F32),
        vm((LANE, trades // 2), F32),
        vm((LANE, LANE), F32),
        vm((2, CHIPS, strip, LANE), F32),
        vm((tiles, strip, LANE), F32),
        dma((5,)), dma((5,)), dma((2,)),
        dma((2, 6)), dma((2, 6)),
        dma((2, RING)), dma((2, RING)),
        dma((DEPTH,)), dma((DEPTH,)),
        dma((DEPTH,)), dma((DEPTH,)),
        dma((2, RING)), dma((2, RING)),
        dma((2, 6)), dma((2, 6)),
        dma((RING * (DEPTH + EXTRA),)), dma((2, 8)),
        dma((2, 6)), dma((2, 6)),
        dma((2,)), dma((2,)),
        dma((2, CHIPS)), dma((tiles,)),
    ]
    vmem = pl.BlockSpec(memory_space=pltpu.VMEM)
    hbm = pl.BlockSpec(memory_space=pl.ANY)
    return pl.pallas_call(
        kernel,
        out_shape=jax.ShapeDtypeStruct((strip, params), F32),
        in_specs=[vmem, hbm, vmem, vmem, vmem, vmem, hbm],
        out_specs=vmem,
        scratch_shapes=scratch,
        compiler_params=pltpu.CompilerParams(
            collective_id=0, has_side_effects=True, vmem_limit_bytes=56 * 1024 * 1024
        ),
    )(
        discounts,
        path_sens.T,
        cash_flows.T,
        flow_index.T,
        exercise_step.reshape(1, trades),
        trade_steps.reshape(1, trades),
        jacobian_inv,
    )


def solution(mesh):
    placed = (
        P(("grp", "path"), None),
        P(("grp", "path"), None),
        P("grp", None),
        P("grp", None),
        P("grp"),
        P("grp"),
        P("path", None),
    )
    return jax.shard_map(
        per_device, mesh=mesh, in_specs=placed, out_specs=P(("grp", "path"), None), check_vma=False
    )
```

time: 347 us -> 74 us (0.21)
  waiting for transfers between devices: 249 us -> 0 us
  Pallas kernels: 0 us -> 72.2 us
  local copies, waits for them, and re-layouts: 25.5 us -> 1.59 us
  matrix products: 22.9 us -> 0 us
  blocking collectives: 22.9 us -> 0 us
  between operations: 13.5 us -> 0.01 us
  starting transfers between devices: 13.2 us -> 0 us
    psum x1 -> x0, waiting for transfers between devices: 249 us -> none  [per_device(): moments = lax.psum(moments, ('grp', 'path'))]
    pallas_call x0 -> x1, Pallas kernels: none -> 72.2 us  [per_device(): pl.pallas_call(kernel, out_shape=jax.ShapeDtypeStruct((strip, params), F3...]
    all_to_all x1 -> x0, blocking collectives: 22.9 us -> none  [per_device(): lax.all_to_all(quotes, 'path', split_axis=0, concat_axis=1, tiled=True)]
    dot_general x4 -> x0, matrix products: 22.9 us -> none  [the longest x1 12 us: per_device(): jnp.dot(weights, moments, precision=lax.Precision.HIGHEST) * path_scale]
    all_to_all x6 -> x0, local copies, waits for them, and re-layouts: 14.9 us -> none  [the longest x4 14 us: per_device(): lax.all_to_all(jacobian_inv, 'path', split_axis=1, concat_axis=0, tiled=T...]
    all_to_all x1 -> x0, starting transfers between devices: 13.2 us -> none  [per_device(): lax.all_to_all(jacobian_inv, 'path', split_axis=1, concat_axis=0, tiled=T...]
    convert_element_type x1 -> x0, local copies, waits for them, and re-layouts: 7.52 us -> none  [per_device(): jnp.where(bucket[None, :] < trade_steps[:, None], vega, 0.0)]
  transfers between devices with their start and end apart: 2 -> 0, of which waited for: 1 -> 0; matrix products, arithmetic and copies ran while one was open for 8% -> 0% of each run, Pallas kernels for 0% -> 0%
where the time goes in v3:
time: 74 us; the launch traced here: 73.8 us
  Pallas kernels  72.2 us (98%)
  local copies, waits for them, and re-layouts  1.59 us (2%)
    pallas_call x1, Pallas kernels, per_device(): pl.pallas_call(kernel, out_shape=jax.ShapeDtypeStruct((strip, params), F3...  72.2 us
    unnamed x1, local copies, waits for them, and re-layouts  1.59 us

profile of v3, /device:TPU:1, one launch (start us, length us, event | category | flops | bytes accessed | tf_op | source)
XLA Modules:
  0.0 73.8 jit_solution(16347631579858459503)
XLA Ops:
  0.0 72.2 %shard_map.73 = f32[8,4800]{1,0:T(8,128)} custom-call(bf16[256,128]{1,0:T(8,128)(2,1)} %disc.1, bf16[4800,256]{1,0:T(8,128)(2,1)} %bitcast.5, f32[8,512]{1,0:T(8,128)} %bitcast.6, s32[8,512]{1,0:T(8,128)} %bitcast.7, s32[1,512]{1,0:T(1,128)} %bitcast.8, s32[1,512]{1,0:T(1,128)} %bitcast.9, bf16[75,4800]{1,0:T(8,128)(2,1)} %jac.1), custom_call_target="tpu_custom_call" | custom-call | tf_op jit(solution)/shard_map/pallas_call | solution.py:575
  72.3 1.6 %copy.9 = f32[8,4800]{1,0:T(8,128)} copy(f32[8,4800]{1,0:T(8,128)} %shard_map.73) | data formatting | bytes 307200

commit v4 on v3

v4 whole, which is shorter than its diff:
```python
import jax
import jax.numpy as jnp
from jax import lax
from jax.experimental import pallas as pl
from jax.experimental.pallas import tpu as pltpu
from jax.sharding import PartitionSpec as P

NB = 40
LANE = 128
RING = 4
DEPTH = 8
CHIPS = RING * DEPTH
PATHS = 2 * CHIPS
EXTRA = 6
F32 = jnp.float32
BF16 = jnp.bfloat16
MESH = pl.DeviceIdType.MESH


def kernel(
    disc, sens, cash, index, exer, steps, jac, out,
    dv, cv, iv, ev, sv, s_own, s_in, d_in, xs, xp, r1, y2, r2, zb, rz, zr, zf, xf,
    jv, jp, jr, jt, mk, acc, acce, pr, pre, po, ob,
    ss_s, rs_s, ls, ss_1, rs_1, ss_2, rs_2, ss_z, rs_z, ss_g, rs_g,
    ss_a2, rs_a2, ss_a1, rs_a1, ss_j, rs_j, ss_ja, rs_ja, ss_p, rs_p, ss_o, rs_o,
):
    y = lax.axis_index("grp")
    me = lax.axis_index("path")
    j = lax.div(me, 2)
    c = lax.rem(me, 2)
    x = lax.div(j, DEPTH)
    z = lax.rem(j, DEPTH)
    sib = 1 - c
    params = sens.shape[0]
    width = params // NB
    half = params // 2
    jrows = jac.shape[0]
    pad = xp.shape[2] // 2
    trades = cash.shape[1]

    def at_chip(xx, zz, cc):
        return {"grp": y, "path": (xx * DEPTH + zz) * 2 + cc}

    def rdma(src, dst, ss, rs, dev):
        return pltpu.make_async_remote_copy(
            src_ref=src, dst_ref=dst, send_sem=ss, recv_sem=rs, device_id=dev, device_id_type=MESH
        )

    sent = []

    def send(*args):
        d = rdma(*args)
        d.start()
        sent.append((None, d))

    def send_if(cond, *args):
        d = rdma(*args)

        @pl.when(cond)
        def _():
            d.start()

        sent.append((cond, d))

    sibling = at_chip(x, z, sib)

    def on_x(k):
        return at_chip(lax.rem(x + k, RING), z, c)

    def on_y(k):
        return {"grp": lax.rem(y + k, RING), "path": me}

    def on_z(k):
        return at_chip(x, lax.rem(z + k, DEPTH), c)

    lines = ((x, on_x), (y, on_y))

    barrier = pltpu.get_barrier_semaphore()
    partners = (
        [sibling]
        + [on_x(k) for k in range(1, RING)]
        + [on_y(k) for k in range(1, RING)]
        + [on_z(k) for k in range(1, DEPTH)]
    )
    for d in partners:
        pl.semaphore_signal(barrier, inc=1, device_id=d, device_id_type=MESH)

    fetched = [
        pltpu.make_async_copy(src, dst, ls.at[n])
        for n, (src, dst) in enumerate(
            (
                (disc, dv),
                (sens.at[pl.ds(pl.multiple_of(c * half, 16), half)], s_own),
                (cash, cv), (index, iv), (exer, ev), (steps, sv), (jac, jv),
            )
        )
    ]
    for f in fetched:
        f.start()

    first_cut = (half // 4 // 16 + 1) * 16
    cuts = (0, first_cut, half // 2, half // 2 + first_cut, half)

    def s_copy(q):
        n = cuts[q + 1] - cuts[q]
        return (
            sens.at[pl.ds(pl.multiple_of(sib * half + cuts[q], 16), n)],
            s_in.at[pl.ds(cuts[q], n)], ss_s.at[q], rs_s.at[q], sibling,
        )

    d_copy = (disc, d_in, ss_s.at[RING], rs_s.at[RING], sibling)

    pl.semaphore_wait(barrier, len(partners))
    send(*d_copy)
    for q in range(RING):
        send(*s_copy(q))

    xs[half : half + 8] = jnp.zeros((8, LANE), F32)
    for f in fetched[:2]:
        f.wait()
    for q in range(RING):
        xs[cuts[q] : cuts[q + 1]] = jnp.dot(
            s_own[cuts[q] : cuts[q + 1]], dv[...], preferred_element_type=F32
        )

    def part_rows(n, size):
        return pl.ds(pl.multiple_of(n * size, 8), size)

    class Scatter:
        def __init__(self, q):
            self.q = q
            self.i, self.on = lines[q % 2]
            self.nr, self.far, self.nl = (lax.rem(self.i + k, RING) for k in (1, 2, 3))
            self.right, self.left = self.on(1), self.on(3)

        def msg(self, n, h, k, dev):
            q = self.q
            return (
                xp.at[q, k, h * pad : (h + 1) * pad], r1.at[q, n],
                ss_1.at[q, n], rs_1.at[q, n], dev,
            )

        def first(self):
            send(*self.msg(0, 0, self.far, self.right))
            send(*self.msg(2, 1, self.far, self.left))
            send(*self.msg(3, 1, self.nr, self.right))
            send(*self.msg(1, 0, self.nl, self.left))

        def second(self):
            for h, n, k, dev in ((0, 0, self.nr, self.right), (1, 2, self.nl, self.left)):
                rdma(*self.msg(n, h, k, dev)).wait_recv()
                xp[self.q, k, h * pad : (h + 1) * pad] += r1[self.q, n]
                send(*self.msg(4 + h, h, k, dev))

        def result(self):
            for h, n in ((0, 1), (1, 3)):
                rdma(*self.msg(n, h, self.i, self.left)).wait_recv()
                rdma(*self.msg(4 + h, h, self.i, self.left)).wait_recv()
                rws = slice(h * pad, (h + 1) * pad)
                y2[self.q, rws] = xp[self.q, self.i, rws] + r1[self.q, n] + r1[self.q, 4 + h]

    one = [Scatter(q) for q in range(RING)]
    rdma(*d_copy).wait_recv()
    for q in range(RING):
        rdma(*s_copy(q)).wait_recv()
        xs[cuts[q] : cuts[q + 1]] += jnp.dot(
            s_in[cuts[q] : cuts[q + 1]], d_in[...], preferred_element_type=F32
        )
        for k in range(RING):
            for u in (0, 1):
                top = (8 * q + 2 * k + u) * jrows
                xp[q, k, u * pad : (u + 1) * pad] = xs[top : top + pad]
        one[q].first()

    tiles = jp.shape[0]
    tail = params - (tiles - 1) * LANE
    turn = lax.rem(z, RING) == y
    core = lax.div(x, 2)
    strip = jr.at[:, 2 * lax.rem(x, 2) + lax.div(z, RING), y, pl.ds(pl.multiple_of(c * pad, 16), pad)]
    j_sem = 4 * lax.rem(x, 2) + 2 * lax.div(z, RING) + c
    for f in fetched[2:]:
        f.wait()

    @pl.when(turn)
    def _():
        jp[...] = jnp.zeros(jp.shape, BF16)

        @pl.loop(0, tiles - 1)
        def _(t):
            jp[t, 0:jrows] = jv[:, pl.ds(pl.multiple_of(t * LANE, LANE), LANE)]

        jp[tiles - 1, 0:jrows, 0:tail] = jv[:, (tiles - 1) * LANE : params]

    def j_column(step):
        xx = lax.rem(x + step, RING)

        def one_tile(e, tile, zz):
            dst = (xx * DEPTH + zz) * 2 + core
            n = step * (DEPTH + EXTRA) + e * DEPTH + zz

            @pl.when(dst == me)
            def _():
                pltpu.make_async_copy(jp.at[tile], strip.at[e], rs_j.at[e, j_sem]).start()

            @pl.when(dst != me)
            def _():
                rdma(
                    jp.at[tile], strip.at[e], ss_j.at[n], rs_j.at[e, j_sem],
                    {"grp": y, "path": dst},
                ).start()

        @pl.when(turn)
        def _():
            @pl.loop(0, DEPTH)
            def _(k):
                zz = lax.rem(z + k, DEPTH)
                one_tile(0, xx * DEPTH + zz, zz)

                @pl.when(zz < EXTRA)
                def _():
                    one_tile(1, CHIPS + zz, zz)

    j_column(0)
    one[0].second()
    one[1].second()
    j_column(1)
    one[2].second()
    one[3].second()
    j_column(3)

    slots = cash.shape[0]
    forwards = lax.broadcasted_iota(jnp.int32, (LANE, trades), 0)
    late = forwards >= ev[...]
    weights = jnp.zeros((LANE, trades), F32)
    for s in range(slots):
        weights += jnp.where(late & (iv[s : s + 1] == forwards), cv[s : s + 1], 0.0)
    weights = weights * (1.0 / (disc.shape[0] * PATHS * RING))
    w_hi = weights.astype(BF16)
    w_lo = (weights - w_hi.astype(F32)).astype(BF16)
    wide = jnp.concatenate([w_hi, w_hi, w_lo], axis=0)

    part = y2.shape[1] // RING

    def two(q, k):
        i, on = lines[1 - q % 2]
        return (
            y2.at[q, part_rows(lax.rem(i + k, RING), part)], r2.at[q, i],
            ss_2.at[q, k], rs_2.at[q, i], on(k),
        )

    for g in (0, 1):
        for q in (2 * g, 2 * g + 1):
            one[q].result()
            for k in (2, 1, 3):
                send(*two(q, k))
    j_column(2)

    share = zr.shape[1]
    count = 2 * part // share
    spread = (4, 3, 5, 2, 6, 1, 7)

    def turn_of(g, d):
        return lax.rem(d + count * g, DEPTH)

    def z_piece(g, d):
        return part_rows(jnp.minimum(turn_of(g, d), count - 1), share)

    for g in (0, 1):
        for p in (0, 1):
            q = 2 * g + p
            i, on = lines[1 - p]
            total = y2[q, part_rows(i, part)]
            for k in (1, 3, 2):
                frm = lax.rem(i + k, RING)
                rdma(
                    y2.at[q, part_rows(i, part)], r2.at[q, frm], ss_2.at[q, k], rs_2.at[q, frm],
                    on(k),
                ).wait_recv()
                total += r2[q, frm]
            zb[g, p * part : (p + 1) * part] = total
        for k in spread:
            d = lax.rem(z + k, DEPTH)
            send_if(
                turn_of(g, d) < count,
                zb.at[g, z_piece(g, d)], rz.at[g, z], ss_z.at[g, k], rs_z.at[g, z], on_z(k),
            )

    has_extra = z < EXTRA
    jblocks = jr.shape[1] * 2

    def j_ring(e, half_, k, n, dev):
        ref = jr.at[e, pl.ds(2 * half_, 2), k]
        return ref, ref, ss_ja.at[e, n], rs_ja.at[e, n], dev

    yr, yl = on_y(1), on_y(3)
    ynr, yfar, ynl = (lax.rem(y + k, RING) for k in (1, 2, 3))

    def j_start(e):
        for n in range(jblocks):
            pltpu.make_async_copy(
                jp.at[0], jr.at[e, n // 2, 0, pl.ds(0, pad)], rs_j.at[e, n]
            ).wait()
        for n, (hh, d) in enumerate(((0, yr), (1, yl), (1, yr), (0, yl))):
            rdma(*j_ring(e, hh, y, n, d)).start()

    def j_forward(e):
        rdma(*j_ring(e, 0, ynl, 0, yr)).wait_recv()
        rdma(*j_ring(e, 0, ynl, 4, yr)).start()
        rdma(*j_ring(e, 1, ynr, 1, yl)).wait_recv()
        rdma(*j_ring(e, 1, ynr, 5, yl)).start()

    def j_finish(e):
        for hh, k, n, d in ((1, ynl, 2, yr), (0, ynr, 3, yl), (0, yfar, 4, yr), (1, yfar, 5, yl)):
            rdma(*j_ring(e, hh, k, n, d)).wait_recv()

        @pl.loop(0, jr.shape[1] * RING)
        def _(n):
            jt[e, n] = jr[e, lax.div(n, RING), lax.rem(n, RING)].T

    def both(f):
        f(0)

        @pl.when(has_extra)
        def _():
            f(1)

    for g in (0, 1):
        reducer = turn_of(g, z) < count

        @pl.when(reducer)
        def _():
            total = zb[g, z_piece(g, z)]
            for k in spread:
                d = lax.rem(z + k, DEPTH)
                rdma(zr.at[g], rz.at[g, d], ss_z.at[g, k], rs_z.at[g, d], on_z(k)).wait_recv()
                total += rz[g, d]
            zr[g] = total
            zf[g, z_piece(g, z)] = total

        for k in spread:
            send_if(
                reducer, zr.at[g], zf.at[g, z_piece(g, z)], ss_g.at[g, k], rs_g.at[g, z], on_z(k)
            )

    both(j_start)

    def home(q, i):
        return xf.at[q, lines[q % 2][0], part_rows(i, part)]

    for g in (0, 1):
        for k in spread:
            d = lax.rem(z + k, DEPTH)

            @pl.when(turn_of(g, d) < count)
            def _():
                rdma(
                    zr.at[g], zf.at[g, z_piece(g, d)], ss_g.at[g, k], rs_g.at[g, d], on_z(k)
                ).wait_recv()

        for p in (0, 1):
            q = 2 * g + p
            i, on = lines[1 - p]
            mine = zf.at[g, p * part : (p + 1) * part]
            for k in (2, 1, 3):
                send(mine, home(q, i), ss_a2.at[q, k], rs_a2.at[q, i], on(k))
            home(q, i)[...] = mine[...]

    both(j_forward)

    class Gather:
        def __init__(self, q):
            self.q = q
            self.i, self.on = lines[q % 2]
            self.nr, self.far, self.nl = (lax.rem(self.i + k, RING) for k in (1, 2, 3))
            self.right, self.left = self.on(1), self.on(3)

        def msg(self, n, h, k, dev):
            ref = xf.at[self.q, k, h * pad : (h + 1) * pad]
            return ref, ref, ss_a1.at[self.q, n], rs_a1.at[self.q, n], dev

        def start(self):
            q = self.q
            i, on = lines[1 - q % 2]
            for k in (1, 3, 2):
                frm = lax.rem(i + k, RING)
                rdma(
                    zf.at[0, 0:part], home(q, frm), ss_a2.at[q, k], rs_a2.at[q, frm], on(k)
                ).wait_recv()
            send(*self.msg(0, 0, self.i, self.right))
            send(*self.msg(1, 1, self.i, self.left))
            send(*self.msg(2, 1, self.i, self.right))
            send(*self.msg(3, 0, self.i, self.left))

        def forward(self):
            rdma(*self.msg(0, 0, self.nl, self.right)).wait_recv()
            send(*self.msg(4, 0, self.nl, self.right))
            rdma(*self.msg(1, 1, self.nr, self.left)).wait_recv()
            send(*self.msg(5, 1, self.nr, self.left))

        def near(self):
            rdma(*self.msg(2, 1, self.nl, self.right)).wait_recv()
            rdma(*self.msg(3, 0, self.nr, self.left)).wait_recv()

        def end(self):
            rdma(*self.msg(4, 0, self.far, self.right)).wait_recv()
            rdma(*self.msg(5, 1, self.far, self.left)).wait_recv()

    ring = [Gather(q) for q in range(RING)]
    for q in range(RING):
        ring[q].start()
    ring[0].forward()
    ring[1].forward()

    reach = sv[...] * width
    row = lax.broadcasted_iota(jnp.int32, (2 * pad, trades), 0)
    row = row - jnp.where(row >= pad, pad - jrows, 0) + c * half

    def block(q, k, fresh=False):
        values = xf[q, k]
        hi = values.astype(BF16)
        lo = (values - hi.astype(F32)).astype(BF16)
        vega = jnp.dot(jnp.concatenate([hi, lo, hi], axis=1), wide, preferred_element_type=F32)
        keep = row < reach - (8 * q + 2 * k) * jrows
        masked = jnp.where(keep, vega, 0.0).astype(BF16)
        mk[...] = masked
        n = RING * q + k
        prod = jnp.dot(jt[0, n], masked, preferred_element_type=F32)
        for s in (0, 1):
            span = slice(s * trades // 2, (s + 1) * trades // 2)
            if fresh:
                acc[s] = prod[:, span]
            else:
                acc[s] += prod[:, span]

        @pl.when(has_extra)
        def _():
            mine = mk[:, pl.ds(pl.multiple_of(x * LANE, LANE), LANE)]
            more = jnp.dot(jt[1, n], mine, preferred_element_type=F32)
            if fresh:
                acce[...] = more
            else:
                acce[...] += more

    both(j_finish)
    block(0, ring[0].i, True)
    block(1, ring[1].i)
    ring[2].forward()
    ring[3].forward()
    block(2, ring[2].i)
    block(3, ring[3].i)
    for q in range(RING):
        ring[q].near()

        @pl.loop(0, 2)
        def _(n):
            block(q, jnp.where(n == 0, ring[q].nl, ring[q].nr))

    for q in range(RING):
        ring[q].end()
        block(q, ring[q].far)

    swap = (acc.at[sib], pr, ss_p.at[0], rs_p.at[0], sibling)
    send(*swap)
    closer = lax.rem(z, 2)
    swap_extra = (acce, pre, ss_p.at[1], rs_p.at[1], sibling)
    send_if(has_extra & (c != closer), *swap_extra)

    strip_rows = out.shape[0]
    rdma(*swap).wait_recv()
    po[0] = (acc[c] + pr[...]).T.reshape(CHIPS, strip_rows, LANE)

    def deliver(e, n, tile, dst):
        @pl.when(dst != me)
        def _():
            rdma(
                po.at[e, n], ob.at[tile], ss_o.at[e, n], rs_o.at[tile], {"grp": y, "path": dst}
            ).start()

        @pl.when(dst == me)
        def _():
            ob[tile] = po[e, n]

    turned = 2 * z + (CHIPS // 2) * lax.rem(x, 2)

    @pl.loop(0, CHIPS)
    def _(k):
        n = lax.rem(turned + k, CHIPS)
        deliver(0, n, j, c * CHIPS + n)

    closing = has_extra & (c == closer)

    @pl.when(closing)
    def _():
        rdma(*swap_extra).wait_recv()
        po[1, 0 : CHIPS // 2] = (acce[...] + pre[...]).T.reshape(CHIPS // 2, strip_rows, LANE)

        @pl.loop(0, CHIPS // 2)
        def _(k):
            n = lax.rem(2 * z + k, CHIPS // 2)
            deliver(1, n, CHIPS + z, x * (CHIPS // 2) + n)

    for cond, d in sent:
        if cond is None:
            d.wait_send()
        else:
            pl.when(cond)(d.wait_send)

    def j_sent(e):
        for n, hh in enumerate((0, 1, 1, 0, 0, 1)):
            rdma(*j_ring(e, hh, y, n, yr)).wait_send()

    both(j_sent)

    @pl.when(turn)
    def _():
        for step in range(RING):
            xx = lax.rem(x + step, RING)

            @pl.loop(0, DEPTH + EXTRA)
            def _(n):
                zz = jnp.where(n < DEPTH, n, n - DEPTH)

                @pl.when((xx * DEPTH + zz) * 2 + core != me)
                def _():
                    rdma(
                        jp.at[0], strip.at[0], ss_j.at[step * (DEPTH + EXTRA) + n],
                        rs_j.at[0, 0], sibling,
                    ).wait_send()

    def arrived(tile, frm):
        @pl.when(frm != me)
        def _():
            rdma(po.at[0, 0], ob.at[tile], ss_o.at[0, 0], rs_o.at[tile], sibling).wait_recv()

    @pl.loop(0, CHIPS)
    def _(t):
        arrived(t, 2 * t + core)

    @pl.loop(0, EXTRA)
    def _(e):
        arrived(CHIPS + e, (x * DEPTH + e) * 2 + lax.rem(e, 2))

    for t in range(tiles - 1):
        out[:, t * LANE : (t + 1) * LANE] = ob[t]
    out[:, (tiles - 1) * LANE : params] = ob[tiles - 1, :, 0:tail]

    def po_sent(e, n, dst):
        @pl.when(dst != me)
        def _():
            rdma(po.at[0, 0], ob.at[0], ss_o.at[e, n], rs_o.at[0], sibling).wait_send()

    @pl.loop(0, CHIPS)
    def _(n):
        po_sent(0, n, c * CHIPS + n)

    @pl.when(closing)
    def _():
        @pl.loop(0, CHIPS // 2)
        def _(n):
            po_sent(1, n, x * (CHIPS // 2) + n)


def per_device(
    path_sens, discounts, cash_flows, flow_index, exercise_step, trade_steps, jacobian_inv
):
    paths_own, params = path_sens.shape
    trades = cash_flows.shape[0]
    jrows = jacobian_inv.shape[0]
    strip = trades // PATHS
    tiles = -(-params // LANE)
    pad = -(-jrows // 16) * 16
    half = params // 2
    slots = cash_flows.shape[1]
    part = pad // 2
    share = 16
    vm = pltpu.VMEM
    dma = pltpu.SemaphoreType.DMA
    scratch = [
        vm((paths_own, LANE), BF16),
        vm((slots, trades), F32),
        vm((slots, trades), jnp.int32),
        vm((1, trades), jnp.int32),
        vm((1, trades), jnp.int32),
        vm((half, paths_own), BF16),
        vm((half, paths_own), BF16),
        vm((paths_own, LANE), BF16),
        vm((half + 8, LANE), F32),
        vm((RING, RING, 2 * pad, LANE), F32),
        vm((RING, 6, pad, LANE), F32),
        vm((RING, 2 * pad, LANE), F32),
        vm((RING, RING, part, LANE), F32),
        vm((2, 2 * part, LANE), F32),
        vm((2, DEPTH, share, LANE), F32),
        vm((2, share, LANE), F32),
        vm((2, 2 * part, LANE), F32),
        vm((RING, RING, 2 * pad, LANE), F32),
        vm((jrows, params), BF16),
        vm((tiles, pad, LANE), BF16),
        vm((2, RING, RING, 2 * pad, LANE), BF16),
        vm((2, RING * RING, LANE, 2 * pad), BF16),
        vm((2 * pad, trades), BF16),
        vm((2, LANE, trades // 2), F32),
        vm((LANE, LANE), F32),
        vm((LANE, trades // 2), F32),
        vm((LANE, LANE), F32),
        vm((2, CHIPS, strip, LANE), F32),
        vm((tiles, strip, LANE), F32),
        dma((RING + 1,)), dma((RING + 1,)), dma((7,)),
        dma((RING, 6)), dma((RING, 6)),
        dma((RING, RING)), dma((RING, RING)),
        dma((2, DEPTH)), dma((2, DEPTH)),
        dma((2, DEPTH)), dma((2, DEPTH)),
        dma((RING, RING)), dma((RING, RING)),
        dma((RING, 6)), dma((RING, 6)),
        dma((RING * (DEPTH + EXTRA),)), dma((2, 8)),
        dma((2, 6)), dma((2, 6)),
        dma((2,)), dma((2,)),
        dma((2, CHIPS)), dma((tiles,)),
    ]
    vmem = pl.BlockSpec(memory_space=pltpu.VMEM)
    hbm = pl.BlockSpec(memory_space=pl.ANY)
    return pl.pallas_call(
        kernel,
        out_shape=jax.ShapeDtypeStruct((strip, params), F32),
        in_specs=[hbm] * 7,
        out_specs=vmem,
        scratch_shapes=scratch,
        compiler_params=pltpu.CompilerParams(
            collective_id=0, has_side_effects=True, vmem_limit_bytes=56 * 1024 * 1024
        ),
    )(
        discounts,
        path_sens.T,
        cash_flows.T,
        flow_index.T,
        exercise_step.reshape(1, trades),
        trade_steps.reshape(1, trades),
        jacobian_inv,
    )


def solution(mesh):
    placed = (
        P(("grp", "path"), None),
        P(("grp", "path"), None),
        P("grp", None),
        P("grp", None),
        P("grp"),
        P("grp"),
        P("path", None),
    )
    return jax.shard_map(
        per_device, mesh=mesh, in_specs=placed, out_specs=P(("grp", "path"), None), check_vma=False
    )
```

time: 74 us -> 74 us (level)
  no operation moved by 1% of the time
where the time goes in v4:
time: 74 us; the launch traced here: 73.3 us
  Pallas kernels  71.7 us (97%)
  local copies, waits for them, and re-layouts  1.59 us (2%)
    pallas_call x1, Pallas kernels, per_device(): pl.pallas_call(kernel, out_shape=jax.ShapeDtypeStruct((strip, params), F3...  71.7 us
    unnamed x1, local copies, waits for them, and re-layouts  1.59 us

profile of v4, /device:TPU:1, one launch (start us, length us, event | category | flops | bytes accessed | tf_op | source)
XLA Modules:
  0.0 73.3 jit_solution(8034323167031818306)
XLA Ops:
  0.0 71.7 %shard_map.73 = f32[8,4800]{1,0:T(8,128)} custom-call(bf16[256,128]{1,0:T(8,128)(2,1)} %disc.1, bf16[4800,256]{1,0:T(8,128)(2,1)} %bitcast.5, f32[8,512]{1,0:T(8,128)} %bitcast.6, s32[8,512]{1,0:T(8,128)} %bitcast.7, s32[1,512]{1,0:T(1,128)} %bitcast.8, s32[1,512]{1,0:T(1,128)} %bitcast.9, bf16[75,4800]{1,0:T(8,128)(2,1)} %jac.1), custom_call_target="tpu_custom_call" | custom-call | tf_op jit(solution)/shard_map/pallas_call | solution.py:622
  71.7 1.6 %copy.9 = f32[8,4800]{1,0:T(8,128)} copy(f32[8,4800]{1,0:T(8,128)} %shard_map.73) | data formatting | bytes 307200

commit v5 on v4

--- a/solution.py
+++ b/solution.py
@@ -20,9 +20,9 @@
 def kernel(
     disc, sens, cash, index, exer, steps, jac, out,
     dv, cv, iv, ev, sv, s_own, s_in, d_in, xs, xp, r1, y2, r2, zb, rz, zr, zf, xf,
-    jv, jp, jr, jt, mk, acc, acce, pr, pre, po, ob,
+    jv, jp, jz, jr, jt, mk, acc, acce, pr, pre, po, ob,
     ss_s, rs_s, ls, ss_1, rs_1, ss_2, rs_2, ss_z, rs_z, ss_g, rs_g,
-    ss_a2, rs_a2, ss_a1, rs_a1, ss_j, rs_j, ss_ja, rs_ja, ss_p, rs_p, ss_o, rs_o,
+    ss_a2, rs_a2, ss_a1, rs_a1, ss_j, ss_jx, rs_j, ss_ja, rs_ja, ss_p, rs_p, ss_o, rs_o, near_z,
 ):
     y = lax.axis_index("grp")
     me = lax.axis_index("path")
@@ -76,14 +76,19 @@
     lines = ((x, on_x), (y, on_y))
 
     barrier = pltpu.get_barrier_semaphore()
-    partners = (
-        [sibling]
-        + [on_x(k) for k in range(1, RING)]
-        + [on_y(k) for k in range(1, RING)]
-        + [on_z(k) for k in range(1, DEPTH)]
-    )
+    partners = [sibling] + [on(k) for on in (on_x, on_y) for k in (1, RING - 1)]
+    z_next = (on_z(1), on_z(DEPTH - 1))
+    partners += list(z_next)
     for d in partners:
         pl.semaphore_signal(barrier, inc=1, device_id=d, device_id_type=MESH)
+
+    def z_tell(n):
+        for k, d in enumerate(z_next):
+            pl.semaphore_signal(near_z.at[n, k], inc=1, device_id=d, device_id_type=MESH)
+
+    def z_hear(n):
+        for k in (0, 1):
+            pl.semaphore_wait(near_z.at[n, k], 1)
 
     fetched = [
         pltpu.make_async_copy(src, dst, ls.at[n])
@@ -110,18 +115,59 @@
 
     d_copy = (disc, d_in, ss_s.at[RING], rs_s.at[RING], sibling)
 
+    xs[half : half + 8] = jnp.zeros((8, LANE), F32)
+    for f in fetched[:2]:
+        f.wait()
+    third = half // 3
+
+    @pl.loop(0, 3)
+    def _(n):
+        rws = pl.ds(pl.multiple_of(n * third, 16), third)
+        xs[rws] = jnp.dot(s_own[rws], dv[...], preferred_element_type=F32)
+
     pl.semaphore_wait(barrier, len(partners))
     send(*d_copy)
     for q in range(RING):
         send(*s_copy(q))
-
-    xs[half : half + 8] = jnp.zeros((8, LANE), F32)
-    for f in fetched[:2]:
+    z_tell(0)
+
+    tiles = out.shape[1] // LANE + 1
+    tail = params - (tiles - 1) * LANE
+    turn = lax.rem(z, RING) == y
+    core = lax.div(x, 2)
+    high = lax.div(z, RING)
+    for f in fetched[2:]:
         f.wait()
-    for q in range(RING):
-        xs[cuts[q] : cuts[q + 1]] = jnp.dot(
-            s_own[cuts[q] : cuts[q + 1]], dv[...], preferred_element_type=F32
-        )
+
+    @pl.when(turn)
+    def _():
+        jp[...] = jnp.zeros(jp.shape, BF16)
+
+        @pl.loop(0, DEPTH)
+        def _(zz):
+            for t in range(RING):
+                col = pl.multiple_of((zz * RING + t) * LANE, LANE)
+                jp[zz, t, 0:jrows] = jv[:, pl.ds(col, LANE)]
+
+            @pl.when(zz < EXTRA - 1)
+            def _():
+                col = pl.multiple_of((CHIPS + zz) * LANE, LANE)
+                jp[zz, RING, 0:jrows] = jv[:, pl.ds(col, LANE)]
+
+        jp[EXTRA - 1, RING, 0:jrows, 0:tail] = jv[:, (tiles - 1) * LANE : params]
+        pltpu.make_async_copy(jp.at[z], jz.at[high], rs_j.at[2, high]).start()
+
+    def j_line(k):
+        zz = lax.rem(z + k, DEPTH)
+        return jp.at[zz], jz.at[high], ss_j.at[k], rs_j.at[2, high], on_z(k)
+
+    def j_depth(*steps_):
+        @pl.when(turn)
+        def _():
+            for k in steps_:
+                rdma(*j_line(k)).start()
+
+    j_depth(1, 7)
 
     def part_rows(n, size):
         return pl.ds(pl.multiple_of(n * size, 8), size)
@@ -172,61 +218,18 @@
                 xp[q, k, u * pad : (u + 1) * pad] = xs[top : top + pad]
         one[q].first()
 
-    tiles = jp.shape[0]
-    tail = params - (tiles - 1) * LANE
-    turn = lax.rem(z, RING) == y
-    core = lax.div(x, 2)
-    strip = jr.at[:, 2 * lax.rem(x, 2) + lax.div(z, RING), y, pl.ds(pl.multiple_of(c * pad, 16), pad)]
-    j_sem = 4 * lax.rem(x, 2) + 2 * lax.div(z, RING) + c
-    for f in fetched[2:]:
-        f.wait()
-
-    @pl.when(turn)
-    def _():
-        jp[...] = jnp.zeros(jp.shape, BF16)
-
-        @pl.loop(0, tiles - 1)
-        def _(t):
-            jp[t, 0:jrows] = jv[:, pl.ds(pl.multiple_of(t * LANE, LANE), LANE)]
-
-        jp[tiles - 1, 0:jrows, 0:tail] = jv[:, (tiles - 1) * LANE : params]
-
-    def j_column(step):
-        xx = lax.rem(x + step, RING)
-
-        def one_tile(e, tile, zz):
-            dst = (xx * DEPTH + zz) * 2 + core
-            n = step * (DEPTH + EXTRA) + e * DEPTH + zz
-
-            @pl.when(dst == me)
-            def _():
-                pltpu.make_async_copy(jp.at[tile], strip.at[e], rs_j.at[e, j_sem]).start()
-
-            @pl.when(dst != me)
-            def _():
-                rdma(
-                    jp.at[tile], strip.at[e], ss_j.at[n], rs_j.at[e, j_sem],
-                    {"grp": y, "path": dst},
-                ).start()
-
-        @pl.when(turn)
-        def _():
-            @pl.loop(0, DEPTH)
-            def _(k):
-                zz = lax.rem(z + k, DEPTH)
-                one_tile(0, xx * DEPTH + zz, zz)
-
-                @pl.when(zz < EXTRA)
-                def _():
-                    one_tile(1, CHIPS + zz, zz)
-
-    j_column(0)
+    z_hear(0)
+    z_tell(1)
+    j_depth(2, 6)
     one[0].second()
     one[1].second()
-    j_column(1)
+    z_hear(1)
+    z_tell(2)
+    j_depth(3, 5)
     one[2].second()
     one[3].second()
-    j_column(3)
+    z_hear(2)
+    j_depth(4)
 
     slots = cash.shape[0]
     forwards = lax.broadcasted_iota(jnp.int32, (LANE, trades), 0)
@@ -245,7 +248,7 @@
         i, on = lines[1 - q % 2]
         return (
             y2.at[q, part_rows(lax.rem(i + k, RING), part)], r2.at[q, i],
-            ss_2.at[q, k], rs_2.at[q, i], on(k),
+            ss_2.at[q, k], rs_2.at[q], on(k),
         )
 
     for g in (0, 1):
@@ -253,7 +256,40 @@
             one[q].result()
             for k in (2, 1, 3):
                 send(*two(q, k))
-    j_column(2)
+
+    has_extra = z < EXTRA
+
+    def j_cross(e, k):
+        xx = lax.rem(x + k, RING)
+        slot = xx if e == 0 else RING
+        dst = jr.at[
+            e, pl.ds(2 * lax.rem(x, 2), 2), y, pl.ds(pl.multiple_of(c * pad, 16), pad)
+        ]
+        return jz.at[:, slot], dst, ss_jx.at[e, k], rs_j.at[e, 0], at_chip(xx, z, core)
+
+    def both(f):
+        f(0)
+
+        @pl.when(has_extra)
+        def _():
+            f(1)
+
+    def j_send(e):
+        for k in (2, 1, 3):
+            rdma(*j_cross(e, k)).start()
+        src, dst, ss, rs, dev = j_cross(e, 0)
+
+        @pl.when(core == c)
+        def _():
+            pltpu.make_async_copy(src, dst, rs).start()
+
+        @pl.when(core != c)
+        def _():
+            rdma(src, dst, ss, rs, dev).start()
+
+    for n in (0, 1):
+        pltpu.make_async_copy(jp.at[0], jz.at[n], rs_j.at[2, n]).wait()
+    both(j_send)
 
     share = zr.shape[1]
     count = 2 * part // share
@@ -261,6 +297,9 @@
 
     def turn_of(g, d):
         return lax.rem(d + count * g, DEPTH)
+
+    def reduces(g):
+        return turn_of(g, z) < count
 
     def z_piece(g, d):
         return part_rows(jnp.minimum(turn_of(g, d), count - 1), share)
@@ -270,23 +309,18 @@
             q = 2 * g + p
             i, on = lines[1 - p]
             total = y2[q, part_rows(i, part)]
-            for k in (1, 3, 2):
-                frm = lax.rem(i + k, RING)
-                rdma(
-                    y2.at[q, part_rows(i, part)], r2.at[q, frm], ss_2.at[q, k], rs_2.at[q, frm],
-                    on(k),
-                ).wait_recv()
-                total += r2[q, frm]
+            three = r2.at[q, 0 : RING - 1]
+            rdma(three, three, ss_2.at[q, 0], rs_2.at[q], sibling).wait_recv()
+            for k in (1, 2, 3):
+                total += r2[q, lax.rem(i + k, RING)]
             zb[g, p * part : (p + 1) * part] = total
         for k in spread:
             d = lax.rem(z + k, DEPTH)
             send_if(
                 turn_of(g, d) < count,
-                zb.at[g, z_piece(g, d)], rz.at[g, z], ss_z.at[g, k], rs_z.at[g, z], on_z(k),
+                zb.at[g, z_piece(g, d)], rz.at[g, z], ss_z.at[g, k], rs_z.at[g], on_z(k),
             )
 
-    has_extra = z < EXTRA
-    jblocks = jr.shape[1] * 2
 
     def j_ring(e, half_, k, n, dev):
         ref = jr.at[e, pl.ds(2 * half_, 2), k]
@@ -296,10 +330,8 @@
     ynr, yfar, ynl = (lax.rem(y + k, RING) for k in (1, 2, 3))
 
     def j_start(e):
-        for n in range(jblocks):
-            pltpu.make_async_copy(
-                jp.at[0], jr.at[e, n // 2, 0, pl.ds(0, pad)], rs_j.at[e, n]
-            ).wait()
+        whole = jr.at[e, :, y]
+        pltpu.make_async_copy(whole, whole, rs_j.at[e, 0]).wait()
         for n, (hh, d) in enumerate(((0, yr), (1, yl), (1, yr), (0, yl))):
             rdma(*j_ring(e, hh, y, n, d)).start()
 
@@ -317,55 +349,45 @@
         def _(n):
             jt[e, n] = jr[e, lax.div(n, RING), lax.rem(n, RING)].T
 
-    def both(f):
-        f(0)
-
-        @pl.when(has_extra)
-        def _():
-            f(1)
+    both(j_start)
 
     for g in (0, 1):
-        reducer = turn_of(g, z) < count
+        reducer = reduces(g)
 
         @pl.when(reducer)
         def _():
             total = zb[g, z_piece(g, z)]
-            for k in spread:
-                d = lax.rem(z + k, DEPTH)
-                rdma(zr.at[g], rz.at[g, d], ss_z.at[g, k], rs_z.at[g, d], on_z(k)).wait_recv()
-                total += rz[g, d]
+            seven = rz.at[g, 0 : DEPTH - 1]
+            rdma(seven, seven, ss_z.at[g, 0], rs_z.at[g], sibling).wait_recv()
+            for k in range(1, DEPTH):
+                total += rz[g, lax.rem(z + k, DEPTH)]
             zr[g] = total
             zf[g, z_piece(g, z)] = total
 
         for k in spread:
             send_if(
-                reducer, zr.at[g], zf.at[g, z_piece(g, z)], ss_g.at[g, k], rs_g.at[g, z], on_z(k)
+                reducer, zr.at[g], zf.at[g, z_piece(g, z)], ss_g.at[g, k], rs_g.at[g], on_z(k)
             )
 
-    both(j_start)
+    both(j_forward)
 
     def home(q, i):
         return xf.at[q, lines[q % 2][0], part_rows(i, part)]
 
     for g in (0, 1):
-        for k in spread:
-            d = lax.rem(z + k, DEPTH)
-
-            @pl.when(turn_of(g, d) < count)
+        for some, ref in ((reduces(g), zf.at[g, 0 : (count - 1) * share]), (~reduces(g), zf.at[g])):
+
+            @pl.when(some)
             def _():
-                rdma(
-                    zr.at[g], zf.at[g, z_piece(g, d)], ss_g.at[g, k], rs_g.at[g, d], on_z(k)
-                ).wait_recv()
+                rdma(ref, ref, ss_g.at[g, 0], rs_g.at[g], sibling).wait_recv()
 
         for p in (0, 1):
             q = 2 * g + p
             i, on = lines[1 - p]
             mine = zf.at[g, p * part : (p + 1) * part]
             for k in (2, 1, 3):
-                send(mine, home(q, i), ss_a2.at[q, k], rs_a2.at[q, i], on(k))
+                send(mine, home(q, i), ss_a2.at[q, k], rs_a2.at[q], on(k))
             home(q, i)[...] = mine[...]
-
-    both(j_forward)
 
     class Gather:
         def __init__(self, q):
@@ -380,12 +402,8 @@
 
         def start(self):
             q = self.q
-            i, on = lines[1 - q % 2]
-            for k in (1, 3, 2):
-                frm = lax.rem(i + k, RING)
-                rdma(
-                    zf.at[0, 0:part], home(q, frm), ss_a2.at[q, k], rs_a2.at[q, frm], on(k)
-                ).wait_recv()
+            three = xf.at[q, 0, 0 : (RING - 1) * part]
+            rdma(three, three, ss_a2.at[q, 0], rs_a2.at[q], sibling).wait_recv()
             send(*self.msg(0, 0, self.i, self.right))
             send(*self.msg(1, 1, self.i, self.left))
             send(*self.msg(2, 1, self.i, self.right))
@@ -397,14 +415,6 @@
             rdma(*self.msg(1, 1, self.nr, self.left)).wait_recv()
             send(*self.msg(5, 1, self.nr, self.left))
 
-        def near(self):
-            rdma(*self.msg(2, 1, self.nl, self.right)).wait_recv()
-            rdma(*self.msg(3, 0, self.nr, self.left)).wait_recv()
-
-        def end(self):
-            rdma(*self.msg(4, 0, self.far, self.right)).wait_recv()
-            rdma(*self.msg(5, 1, self.far, self.left)).wait_recv()
-
     ring = [Gather(q) for q in range(RING)]
     for q in range(RING):
         ring[q].start()
@@ -415,7 +425,10 @@
     row = lax.broadcasted_iota(jnp.int32, (2 * pad, trades), 0)
     row = row - jnp.where(row >= pad, pad - jrows, 0) + c * half
 
-    def block(q, k, fresh=False):
+    acc[...] = jnp.zeros(acc.shape, F32)
+    acce[...] = jnp.zeros(acce.shape, F32)
+
+    def block(q, k):
         values = xf[q, k]
         hi = values.astype(BF16)
         lo = (values - hi.astype(F32)).astype(BF16)
@@ -426,38 +439,54 @@
         n = RING * q + k
         prod = jnp.dot(jt[0, n], masked, preferred_element_type=F32)
         for s in (0, 1):
-            span = slice(s * trades // 2, (s + 1) * trades // 2)
-            if fresh:
-                acc[s] = prod[:, span]
-            else:
-                acc[s] += prod[:, span]
+            acc[s] += prod[:, s * trades // 2 : (s + 1) * trades // 2]
 
         @pl.when(has_extra)
         def _():
             mine = mk[:, pl.ds(pl.multiple_of(x * LANE, LANE), LANE)]
-            more = jnp.dot(jt[1, n], mine, preferred_element_type=F32)
-            if fresh:
-                acce[...] = more
-            else:
-                acce[...] += more
+            acce[...] += jnp.dot(jt[1, n], mine, preferred_element_type=F32)
+
+    def landed(q, k, h, n):
+        ref = xf.at[q, k, h * pad : (h + 1) * pad]
+        rdma(ref, ref, ss_a1.at[q, n], rs_a1.at[q, n], sibling).wait_recv()
+
+    def ring_place(q, step):
+        return lax.rem(jnp.where(lax.rem(q, 2) == 0, x, y) + step, RING)
 
     both(j_finish)
-    block(0, ring[0].i, True)
-    block(1, ring[1].i)
+
+    @pl.loop(0, 2)
+    def _(q):
+        block(q, ring_place(q, 0))
+
     ring[2].forward()
     ring[3].forward()
-    block(2, ring[2].i)
-    block(3, ring[3].i)
-    for q in range(RING):
-        ring[q].near()
-
-        @pl.loop(0, 2)
-        def _(n):
-            block(q, jnp.where(n == 0, ring[q].nl, ring[q].nr))
-
-    for q in range(RING):
-        ring[q].end()
-        block(q, ring[q].far)
+
+    @pl.loop(2, RING)
+    def _(q):
+        block(q, ring_place(q, 0))
+
+    @pl.loop(0, 2 * RING)
+    def _(n):
+        q = lax.div(n, 2)
+        k = ring_place(q, 3 - 2 * lax.rem(n, 2))
+
+        @pl.when(lax.rem(n, 2) == 0)
+        def _():
+            landed(q, k, 1, 2)
+
+        @pl.when(lax.rem(n, 2) == 1)
+        def _():
+            landed(q, k, 0, 3)
+
+        block(q, k)
+
+    @pl.loop(0, RING)
+    def _(q):
+        k = ring_place(q, 2)
+        landed(q, k, 0, 4)
+        landed(q, k, 1, 5)
+        block(q, k)
 
     swap = (acc.at[sib], pr, ss_p.at[0], rs_p.at[0], sibling)
     send(*swap)
@@ -473,19 +502,19 @@
         @pl.when(dst != me)
         def _():
             rdma(
-                po.at[e, n], ob.at[tile], ss_o.at[e, n], rs_o.at[tile], {"grp": y, "path": dst}
+                po.at[e, n], ob.at[tile], ss_o.at[e], rs_o.at[0], {"grp": y, "path": dst}
             ).start()
 
         @pl.when(dst == me)
         def _():
-            ob[tile] = po[e, n]
-
-    turned = 2 * z + (CHIPS // 2) * lax.rem(x, 2)
-
-    @pl.loop(0, CHIPS)
-    def _(k):
-        n = lax.rem(turned + k, CHIPS)
-        deliver(0, n, j, c * CHIPS + n)
+            pltpu.make_async_copy(po.at[e, n], ob.at[tile], rs_o.at[0]).start()
+
+    for k in (4, 3, 5, 2, 6, 1, 7, 0):
+        zz = lax.rem(z + k, DEPTH)
+        for side in (0, 1):
+            for u in (0, 1):
+                n = side * 2 * DEPTH + 2 * zz + u
+                deliver(0, n, z * RING + x, c * CHIPS + n)
 
     closing = has_extra & (c == closer)
 
@@ -496,7 +525,7 @@
 
         @pl.loop(0, CHIPS // 2)
         def _(k):
-            n = lax.rem(2 * z + k, CHIPS // 2)
+            n = lax.rem(2 * z + DEPTH + k, CHIPS // 2)
             deliver(1, n, CHIPS + z, x * (CHIPS // 2) + n)
 
     for cond, d in sent:
@@ -511,53 +540,33 @@
 
     both(j_sent)
 
+    def j_crossed(e):
+        for k in (1, 2, 3):
+            rdma(*j_cross(e, k)).wait_send()
+
+        @pl.when(core != c)
+        def _():
+            rdma(*j_cross(e, 0)).wait_send()
+
+    both(j_crossed)
+
     @pl.when(turn)
     def _():
-        for step in range(RING):
-            xx = lax.rem(x + step, RING)
-
-            @pl.loop(0, DEPTH + EXTRA)
-            def _(n):
-                zz = jnp.where(n < DEPTH, n, n - DEPTH)
-
-                @pl.when((xx * DEPTH + zz) * 2 + core != me)
-                def _():
-                    rdma(
-                        jp.at[0], strip.at[0], ss_j.at[step * (DEPTH + EXTRA) + n],
-                        rs_j.at[0, 0], sibling,
-                    ).wait_send()
-
-    def arrived(tile, frm):
-        @pl.when(frm != me)
-        def _():
-            rdma(po.at[0, 0], ob.at[tile], ss_o.at[0, 0], rs_o.at[tile], sibling).wait_recv()
-
-    @pl.loop(0, CHIPS)
-    def _(t):
-        arrived(t, 2 * t + core)
-
-    @pl.loop(0, EXTRA)
-    def _(e):
-        arrived(CHIPS + e, (x * DEPTH + e) * 2 + lax.rem(e, 2))
+        for k in range(1, DEPTH):
+            rdma(*j_line(k)).wait_send()
+
+    pltpu.make_async_copy(ob, ob, rs_o.at[0]).wait()
 
     for t in range(tiles - 1):
         out[:, t * LANE : (t + 1) * LANE] = ob[t]
     out[:, (tiles - 1) * LANE : params] = ob[tiles - 1, :, 0:tail]
 
-    def po_sent(e, n, dst):
-        @pl.when(dst != me)
-        def _():
-            rdma(po.at[0, 0], ob.at[0], ss_o.at[e, n], rs_o.at[0], sibling).wait_send()
-
-    @pl.loop(0, CHIPS)
-    def _(n):
-        po_sent(0, n, c * CHIPS + n)
-
-    @pl.when(closing)
-    def _():
-        @pl.loop(0, CHIPS // 2)
-        def _(n):
-            po_sent(1, n, x * (CHIPS // 2) + n)
+    def po_sent(e, n):
+        rdma(po.at[e, 0:n], po.at[e, 0:n], ss_o.at[e], rs_o.at[0], sibling).wait_send()
+
+    pl.when(core == c)(lambda: po_sent(0, CHIPS - 1))
+    pl.when(core != c)(lambda: po_sent(0, CHIPS))
+    pl.when(closing)(lambda: po_sent(1, CHIPS // 2 - 1))
 
 
 def per_device(
@@ -595,7 +604,8 @@
         vm((2, 2 * part, LANE), F32),
         vm((RING, RING, 2 * pad, LANE), F32),
         vm((jrows, params), BF16),
-        vm((tiles, pad, LANE), BF16),
+        vm((DEPTH, RING + 1, pad, LANE), BF16),
+        vm((2, RING + 1, pad, LANE), BF16),
         vm((2, RING, RING, 2 * pad, LANE), BF16),
         vm((2, RING * RING, LANE, 2 * pad), BF16),
         vm((2 * pad, trades), BF16),
@@ -607,15 +617,16 @@
         vm((tiles, strip, LANE), F32),
         dma((RING + 1,)), dma((RING + 1,)), dma((7,)),
         dma((RING, 6)), dma((RING, 6)),
-        dma((RING, RING)), dma((RING, RING)),
-        dma((2, DEPTH)), dma((2, DEPTH)),
-        dma((2, DEPTH)), dma((2, DEPTH)),
-        dma((RING, RING)), dma((RING, RING)),
+        dma((RING, RING)), dma((RING,)),
+        dma((2, DEPTH)), dma((2,)),
+        dma((2, DEPTH)), dma((2,)),
+        dma((RING, RING)), dma((RING,)),
         dma((RING, 6)), dma((RING, 6)),
-        dma((RING * (DEPTH + EXTRA),)), dma((2, 8)),
+        dma((DEPTH,)), dma((2, RING)), dma((3, 2)),
         dma((2, 6)), dma((2, 6)),
         dma((2,)), dma((2,)),
-        dma((2, CHIPS)), dma((tiles,)),
+        dma((2,)), dma((1,)),
+        pltpu.SemaphoreType.REGULAR((3, 2)),
     ]
     vmem = pl.BlockSpec(memory_space=pltpu.VMEM)
     hbm = pl.BlockSpec(memory_space=pl.ANY)

time: 74 us -> 69.3 us (0.936)
  Pallas kernels: 71.7 us -> 67.6 us
    pallas_call x1, Pallas kernels: 71.7 us -> 67.6 us  [per_device(): pl.pallas_call(kernel, out_shape=jax.ShapeDtypeStruct((strip, params), F3...]
where the time goes in v5:
time: 69.3 us; the launch traced here: 69.2 us
  Pallas kernels  67.6 us (98%)
  local copies, waits for them, and re-layouts  1.59 us (2%)
    pallas_call x1, Pallas kernels, per_device(): pl.pallas_call(kernel, out_shape=jax.ShapeDtypeStruct((strip, params), F3...  67.6 us
    unnamed x1, local copies, waits for them, and re-layouts  1.59 us

profile of v5, /device:TPU:1, one launch (start us, length us, event | category | flops | bytes accessed | tf_op | source)
XLA Modules:
  0.0 69.2 jit_solution(13901334377069334693)
XLA Ops:
  0.0 67.6 %shard_map.73 = f32[8,4800]{1,0:T(8,128)} custom-call(bf16[256,128]{1,0:T(8,128)(2,1)} %disc.1, bf16[4800,256]{1,0:T(8,128)(2,1)} %bitcast.5, f32[8,512]{1,0:T(8,128)} %bitcast.6, s32[8,512]{1,0:T(8,128)} %bitcast.7, s32[1,512]{1,0:T(1,128)} %bitcast.8, s32[1,512]{1,0:T(1,128)} %bitcast.9, bf16[75,4800]{1,0:T(8,128)(2,1)} %jac.1), custom_call_target="tpu_custom_call" | custom-call | tf_op jit(solution)/shard_map/pallas_call | solution.py:633
  67.6 1.6 %copy.9 = f32[8,4800]{1,0:T(8,128)} copy(f32[8,4800]{1,0:T(8,128)} %shard_map.73) | data formatting | bytes 307200

commit v6 on v5

--- a/solution.py
+++ b/solution.py
@@ -20,7 +20,7 @@
 def kernel(
     disc, sens, cash, index, exer, steps, jac, out,
     dv, cv, iv, ev, sv, s_own, s_in, d_in, xs, xp, r1, y2, r2, zb, rz, zr, zf, xf,
-    jv, jp, jz, jr, jt, mk, acc, acce, pr, pre, po, ob,
+    jv, jp, jz, jr, wt, room, mk, acc, acce, pr, pre, po, ob,
     ss_s, rs_s, ls, ss_1, rs_1, ss_2, rs_2, ss_z, rs_z, ss_g, rs_g,
     ss_a2, rs_a2, ss_a1, rs_a1, ss_j, ss_jx, rs_j, ss_ja, rs_ja, ss_p, rs_p, ss_o, rs_o, near_z,
 ):
@@ -77,18 +77,9 @@
 
     barrier = pltpu.get_barrier_semaphore()
     partners = [sibling] + [on(k) for on in (on_x, on_y) for k in (1, RING - 1)]
-    z_next = (on_z(1), on_z(DEPTH - 1))
-    partners += list(z_next)
+    partners += [on_z(k) for k in (1, DEPTH - 1, 2, DEPTH - 2)]
     for d in partners:
         pl.semaphore_signal(barrier, inc=1, device_id=d, device_id_type=MESH)
-
-    def z_tell(n):
-        for k, d in enumerate(z_next):
-            pl.semaphore_signal(near_z.at[n, k], inc=1, device_id=d, device_id_type=MESH)
-
-    def z_hear(n):
-        for k in (0, 1):
-            pl.semaphore_wait(near_z.at[n, k], 1)
 
     fetched = [
         pltpu.make_async_copy(src, dst, ls.at[n])
@@ -129,7 +120,8 @@
     send(*d_copy)
     for q in range(RING):
         send(*s_copy(q))
-    z_tell(0)
+    for n, k in enumerate((2, DEPTH - 2)):
+        pl.semaphore_signal(near_z.at[n], inc=1, device_id=on_z(k), device_id_type=MESH)
 
     tiles = out.shape[1] // LANE + 1
     tail = params - (tiles - 1) * LANE
@@ -167,7 +159,7 @@
             for k in steps_:
                 rdma(*j_line(k)).start()
 
-    j_depth(1, 7)
+    j_depth(2, 6, 1, 7)
 
     def part_rows(n, size):
         return pl.ds(pl.multiple_of(n * size, 8), size)
@@ -218,18 +210,13 @@
                 xp[q, k, u * pad : (u + 1) * pad] = xs[top : top + pad]
         one[q].first()
 
-    z_hear(0)
-    z_tell(1)
-    j_depth(2, 6)
+    for n in (0, 1):
+        pl.semaphore_wait(near_z.at[n], 1)
+    j_depth(4, 3, 5)
     one[0].second()
     one[1].second()
-    z_hear(1)
-    z_tell(2)
-    j_depth(3, 5)
     one[2].second()
     one[3].second()
-    z_hear(2)
-    j_depth(4)
 
     slots = cash.shape[0]
     forwards = lax.broadcasted_iota(jnp.int32, (LANE, trades), 0)
@@ -238,9 +225,16 @@
     for s in range(slots):
         weights += jnp.where(late & (iv[s : s + 1] == forwards), cv[s : s + 1], 0.0)
     weights = weights * (1.0 / (disc.shape[0] * PATHS * RING))
+    weights = weights.T
     w_hi = weights.astype(BF16)
     w_lo = (weights - w_hi.astype(F32)).astype(BF16)
-    wide = jnp.concatenate([w_hi, w_hi, w_lo], axis=0)
+    wt[...] = jnp.concatenate([w_hi, w_hi, w_lo], axis=1)
+    reach = jnp.broadcast_to((sv[...] * width).astype(F32), (LANE, trades)).T.astype(jnp.int32)
+    lane = lax.broadcasted_iota(jnp.int32, (trades, 2 * pad), 1)
+    room[...] = (
+        jnp.concatenate([reach, reach[:, : 2 * pad - LANE]], axis=1)
+        - lane + jnp.where(lane >= pad, pad - jrows, 0) - c * half
+    )
 
     part = y2.shape[1] // RING
 
@@ -345,11 +339,7 @@
         for hh, k, n, d in ((1, ynl, 2, yr), (0, ynr, 3, yl), (0, yfar, 4, yr), (1, yfar, 5, yl)):
             rdma(*j_ring(e, hh, k, n, d)).wait_recv()
 
-        @pl.loop(0, jr.shape[1] * RING)
-        def _(n):
-            jt[e, n] = jr[e, lax.div(n, RING), lax.rem(n, RING)].T
-
-    both(j_start)
+    j_start(0)
 
     for g in (0, 1):
         reducer = reduces(g)
@@ -369,7 +359,8 @@
                 reducer, zr.at[g], zf.at[g, z_piece(g, z)], ss_g.at[g, k], rs_g.at[g], on_z(k)
             )
 
-    both(j_forward)
+    j_forward(0)
+    pl.when(has_extra)(lambda: j_start(1))
 
     def home(q, i):
         return xf.at[q, lines[q % 2][0], part_rows(i, part)]
@@ -388,6 +379,8 @@
             for k in (2, 1, 3):
                 send(mine, home(q, i), ss_a2.at[q, k], rs_a2.at[q], on(k))
             home(q, i)[...] = mine[...]
+
+    pl.when(has_extra)(lambda: j_forward(1))
 
     class Gather:
         def __init__(self, q):
@@ -421,30 +414,19 @@
     ring[0].forward()
     ring[1].forward()
 
-    reach = sv[...] * width
-    row = lax.broadcasted_iota(jnp.int32, (2 * pad, trades), 0)
-    row = row - jnp.where(row >= pad, pad - jrows, 0) + c * half
-
     acc[...] = jnp.zeros(acc.shape, F32)
-    acce[...] = jnp.zeros(acce.shape, F32)
 
     def block(q, k):
         values = xf[q, k]
         hi = values.astype(BF16)
         lo = (values - hi.astype(F32)).astype(BF16)
-        vega = jnp.dot(jnp.concatenate([hi, lo, hi], axis=1), wide, preferred_element_type=F32)
-        keep = row < reach - (8 * q + 2 * k) * jrows
-        masked = jnp.where(keep, vega, 0.0).astype(BF16)
-        mk[...] = masked
-        n = RING * q + k
-        prod = jnp.dot(jt[0, n], masked, preferred_element_type=F32)
-        for s in (0, 1):
-            acc[s] += prod[:, s * trades // 2 : (s + 1) * trades // 2]
-
-        @pl.when(has_extra)
-        def _():
-            mine = mk[:, pl.ds(pl.multiple_of(x * LANE, LANE), LANE)]
-            acce[...] += jnp.dot(jt[1, n], mine, preferred_element_type=F32)
+        vega = lax.dot_general(
+            wt[...], jnp.concatenate([hi, lo, hi], axis=1), (((1,), (1,)), ((), ())),
+            preferred_element_type=F32,
+        )
+        masked = jnp.where(room[...] > (8 * q + 2 * k) * jrows, vega, 0.0).astype(BF16)
+        mk[RING * q + k] = masked
+        acc[...] += jnp.dot(masked, jr[0, q, k], preferred_element_type=F32)
 
     def landed(q, k, h, n):
         ref = xf.at[q, k, h * pad : (h + 1) * pad]
@@ -453,7 +435,7 @@
     def ring_place(q, step):
         return lax.rem(jnp.where(lax.rem(q, 2) == 0, x, y) + step, RING)
 
-    both(j_finish)
+    j_finish(0)
 
     @pl.loop(0, 2)
     def _(q):
@@ -488,15 +470,25 @@
         landed(q, k, 1, 5)
         block(q, k)
 
-    swap = (acc.at[sib], pr, ss_p.at[0], rs_p.at[0], sibling)
+    rows_c = pl.ds(pl.multiple_of(c * (trades // 2), 8), trades // 2)
+    rows_sib = pl.ds(pl.multiple_of(sib * (trades // 2), 8), trades // 2)
+    swap = (acc.at[rows_sib], pr, ss_p.at[0], rs_p.at[0], sibling)
     send(*swap)
-    closer = lax.rem(z, 2)
-    swap_extra = (acce, pre, ss_p.at[1], rs_p.at[1], sibling)
-    send_if(has_extra & (c != closer), *swap_extra)
+    swap_extra = (acce.at[:, sib], pre, ss_p.at[1], rs_p.at[1], sibling)
+
+    @pl.when(has_extra)
+    def _():
+        j_finish(1)
+        mine = pl.ds(pl.multiple_of(x * LANE, LANE), LANE)
+        total = jnp.zeros((LANE, LANE), F32)
+        for n in range(RING * RING):
+            total += jnp.dot(mk[n, mine], jr[1, n // RING, n % RING], preferred_element_type=F32)
+        acce[...] = total.reshape(acce.shape)
+        rdma(*swap_extra).start()
 
     strip_rows = out.shape[0]
     rdma(*swap).wait_recv()
-    po[0] = (acc[c] + pr[...]).T.reshape(CHIPS, strip_rows, LANE)
+    po[0] = (acc[rows_c] + pr[...]).reshape(CHIPS, strip_rows, LANE)
 
     def deliver(e, n, tile, dst):
         @pl.when(dst != me)
@@ -516,17 +508,13 @@
                 n = side * 2 * DEPTH + 2 * zz + u
                 deliver(0, n, z * RING + x, c * CHIPS + n)
 
-    closing = has_extra & (c == closer)
-
-    @pl.when(closing)
+    @pl.when(has_extra)
     def _():
         rdma(*swap_extra).wait_recv()
-        po[1, 0 : CHIPS // 2] = (acce[...] + pre[...]).T.reshape(CHIPS // 2, strip_rows, LANE)
-
-        @pl.loop(0, CHIPS // 2)
-        def _(k):
-            n = lax.rem(2 * z + DEPTH + k, CHIPS // 2)
-            deliver(1, n, CHIPS + z, x * (CHIPS // 2) + n)
+        po[1, 0:DEPTH] = acce[:, c] + pre[...]
+        for k in (4, 3, 5, 2, 6, 1, 7, 0):
+            zz = lax.rem(z + k, DEPTH)
+            deliver(1, zz, CHIPS + z, (x * DEPTH + zz) * 2 + c)
 
     for cond, d in sent:
         if cond is None:
@@ -550,6 +538,10 @@
 
     both(j_crossed)
 
+    @pl.when(has_extra)
+    def _():
+        rdma(*swap_extra).wait_send()
+
     @pl.when(turn)
     def _():
         for k in range(1, DEPTH):
@@ -566,7 +558,7 @@
 
     pl.when(core == c)(lambda: po_sent(0, CHIPS - 1))
     pl.when(core != c)(lambda: po_sent(0, CHIPS))
-    pl.when(closing)(lambda: po_sent(1, CHIPS // 2 - 1))
+    pl.when(has_extra)(lambda: po_sent(1, DEPTH - 1))
 
 
 def per_device(
@@ -607,12 +599,13 @@
         vm((DEPTH, RING + 1, pad, LANE), BF16),
         vm((2, RING + 1, pad, LANE), BF16),
         vm((2, RING, RING, 2 * pad, LANE), BF16),
-        vm((2, RING * RING, LANE, 2 * pad), BF16),
-        vm((2 * pad, trades), BF16),
-        vm((2, LANE, trades // 2), F32),
-        vm((LANE, LANE), F32),
-        vm((LANE, trades // 2), F32),
-        vm((LANE, LANE), F32),
+        vm((trades, 3 * LANE), BF16),
+        vm((trades, 2 * pad), jnp.int32),
+        vm((RING * RING, trades, 2 * pad), BF16),
+        vm((trades, LANE), F32),
+        vm((DEPTH, 2, strip, LANE), F32),
+        vm((trades // 2, LANE), F32),
+        vm((DEPTH, strip, LANE), F32),
         vm((2, CHIPS, strip, LANE), F32),
         vm((tiles, strip, LANE), F32),
         dma((RING + 1,)), dma((RING + 1,)), dma((7,)),
@@ -626,7 +619,7 @@
         dma((2, 6)), dma((2, 6)),
         dma((2,)), dma((2,)),
         dma((2,)), dma((1,)),
-        pltpu.SemaphoreType.REGULAR((3, 2)),
+        pltpu.SemaphoreType.REGULAR((2,)),
     ]
     vmem = pl.BlockSpec(memory_space=pltpu.VMEM)
     hbm = pl.BlockSpec(memory_space=pl.ANY)

time: 69.3 us -> 65.3 us (0.942)
  Pallas kernels: 67.6 us -> 63.6 us
    pallas_call x1, Pallas kernels: 67.6 us -> 63.6 us  [per_device(): pl.pallas_call(kernel, out_shape=jax.ShapeDtypeStruct((strip, params), F3...]
where the time goes in v6:
time: 65.3 us; the launch traced here: 65.2 us
  Pallas kernels  63.6 us (97%)
  local copies, waits for them, and re-layouts  1.59 us (2%)
    pallas_call x1, Pallas kernels, per_device(): pl.pallas_call(kernel, out_shape=jax.ShapeDtypeStruct((strip, params), F3...  63.6 us
    unnamed x1, local copies, waits for them, and re-layouts  1.59 us

profile of v6, /device:TPU:1, one launch (start us, length us, event | category | flops | bytes accessed | tf_op | source)
XLA Modules:
  0.0 65.2 jit_solution(10881550680420646530)
XLA Ops:
  0.0 63.6 %shard_map.73 = f32[8,4800]{1,0:T(8,128)} custom-call(bf16[256,128]{1,0:T(8,128)(2,1)} %disc.1, bf16[4800,256]{1,0:T(8,128)(2,1)} %bitcast.5, f32[8,512]{1,0:T(8,128)} %bitcast.6, s32[8,512]{1,0:T(8,128)} %bitcast.7, s32[1,512]{1,0:T(1,128)} %bitcast.8, s32[1,512]{1,0:T(1,128)} %bitcast.9, bf16[75,4800]{1,0:T(8,128)(2,1)} %jac.1), custom_call_target="tpu_custom_call" | custom-call | tf_op jit(solution)/shard_map/pallas_call | solution.py:626
  63.6 1.6 %copy.9 = f32[8,4800]{1,0:T(8,128)} copy(f32[8,4800]{1,0:T(8,128)} %shard_map.73) | data formatting | bytes 307200

commit v7 on v6

--- a/solution.py
+++ b/solution.py
@@ -218,6 +218,40 @@
     one[2].second()
     one[3].second()
 
+    has_extra = z < EXTRA
+
+    def j_cross(e, k):
+        xx = lax.rem(x + k, RING)
+        slot = xx if e == 0 else RING
+        dst = jr.at[
+            e, pl.ds(2 * lax.rem(x, 2), 2), y, pl.ds(pl.multiple_of(c * pad, 16), pad)
+        ]
+        return jz.at[:, slot], dst, ss_jx.at[e, k], rs_j.at[e, 0], at_chip(xx, z, core)
+
+    def both(f):
+        f(0)
+
+        @pl.when(has_extra)
+        def _():
+            f(1)
+
+    def j_send(e):
+        for k in (1, 3):
+            rdma(*j_cross(e, k)).start()
+        src, dst, ss, rs, dev = j_cross(e, 0)
+
+        @pl.when(core == c)
+        def _():
+            pltpu.make_async_copy(src, dst, rs).start()
+
+        @pl.when(core != c)
+        def _():
+            rdma(src, dst, ss, rs, dev).start()
+
+    for n in (0, 1):
+        pltpu.make_async_copy(jp.at[0], jz.at[n], rs_j.at[2, n]).wait()
+    both(j_send)
+
     slots = cash.shape[0]
     forwards = lax.broadcasted_iota(jnp.int32, (LANE, trades), 0)
     late = forwards >= ev[...]
@@ -250,40 +284,7 @@
             one[q].result()
             for k in (2, 1, 3):
                 send(*two(q, k))
-
-    has_extra = z < EXTRA
-
-    def j_cross(e, k):
-        xx = lax.rem(x + k, RING)
-        slot = xx if e == 0 else RING
-        dst = jr.at[
-            e, pl.ds(2 * lax.rem(x, 2), 2), y, pl.ds(pl.multiple_of(c * pad, 16), pad)
-        ]
-        return jz.at[:, slot], dst, ss_jx.at[e, k], rs_j.at[e, 0], at_chip(xx, z, core)
-
-    def both(f):
-        f(0)
-
-        @pl.when(has_extra)
-        def _():
-            f(1)
-
-    def j_send(e):
-        for k in (2, 1, 3):
-            rdma(*j_cross(e, k)).start()
-        src, dst, ss, rs, dev = j_cross(e, 0)
-
-        @pl.when(core == c)
-        def _():
-            pltpu.make_async_copy(src, dst, rs).start()
-
-        @pl.when(core != c)
-        def _():
-            rdma(src, dst, ss, rs, dev).start()
-
-    for n in (0, 1):
-        pltpu.make_async_copy(jp.at[0], jz.at[n], rs_j.at[2, n]).wait()
-    both(j_send)
+    both(lambda e: rdma(*j_cross(e, 2)).start())
 
     share = zr.shape[1]
     count = 2 * part // share
@@ -359,8 +360,8 @@
                 reducer, zr.at[g], zf.at[g, z_piece(g, z)], ss_g.at[g, k], rs_g.at[g], on_z(k)
             )
 
+    pl.when(has_extra)(lambda: j_start(1))
     j_forward(0)
-    pl.when(has_extra)(lambda: j_start(1))
 
     def home(q, i):
         return xf.at[q, lines[q % 2][0], part_rows(i, part)]
@@ -379,8 +380,6 @@
             for k in (2, 1, 3):
                 send(mine, home(q, i), ss_a2.at[q, k], rs_a2.at[q], on(k))
             home(q, i)[...] = mine[...]
-
-    pl.when(has_extra)(lambda: j_forward(1))
 
     class Gather:
         def __init__(self, q):
@@ -411,10 +410,12 @@
     ring = [Gather(q) for q in range(RING)]
     for q in range(RING):
         ring[q].start()
+    pl.when(has_extra)(lambda: j_forward(1))
     ring[0].forward()
     ring[1].forward()
 
     acc[...] = jnp.zeros(acc.shape, F32)
+    acce[...] = jnp.zeros(acce.shape, F32)
 
     def block(q, k):
         values = xf[q, k]
@@ -463,6 +464,8 @@
 
         block(q, k)
 
+    pl.when(has_extra)(lambda: j_finish(1))
+
     @pl.loop(0, RING)
     def _(q):
         k = ring_place(q, 2)
@@ -470,6 +473,16 @@
         landed(q, k, 1, 5)
         block(q, k)
 
+        @pl.when(has_extra)
+        def _():
+            mine = pl.ds(pl.multiple_of(x * LANE, LANE), LANE)
+            more = jnp.zeros((LANE, LANE), F32)
+            for kk in range(RING):
+                more += jnp.dot(
+                    mk[RING * q + kk, mine], jr[1, q, kk], preferred_element_type=F32
+                )
+            acce[...] += more.reshape(acce.shape)
+
     rows_c = pl.ds(pl.multiple_of(c * (trades // 2), 8), trades // 2)
     rows_sib = pl.ds(pl.multiple_of(sib * (trades // 2), 8), trades // 2)
     swap = (acc.at[rows_sib], pr, ss_p.at[0], rs_p.at[0], sibling)
@@ -478,12 +491,6 @@
 
     @pl.when(has_extra)
     def _():
-        j_finish(1)
-        mine = pl.ds(pl.multiple_of(x * LANE, LANE), LANE)
-        total = jnp.zeros((LANE, LANE), F32)
-        for n in range(RING * RING):
-            total += jnp.dot(mk[n, mine], jr[1, n // RING, n % RING], preferred_element_type=F32)
-        acce[...] = total.reshape(acce.shape)
         rdma(*swap_extra).start()
 
     strip_rows = out.shape[0]

time: 65.3 us -> 66.2 us (1.014)
  Pallas kernels: 63.6 us -> 64.5 us
    pallas_call x1, Pallas kernels: 63.6 us -> 64.5 us  [per_device(): pl.pallas_call(kernel, out_shape=jax.ShapeDtypeStruct((strip, params), F3...]
where the time goes in v7:
time: 66.2 us; the launch traced here: 66.1 us
  Pallas kernels  64.5 us (97%)
  local copies, waits for them, and re-layouts  1.59 us (2%)
    pallas_call x1, Pallas kernels, per_device(): pl.pallas_call(kernel, out_shape=jax.ShapeDtypeStruct((strip, params), F3...  64.5 us
    unnamed x1, local copies, waits for them, and re-layouts  1.59 us

profile of v7, /device:TPU:1, one launch (start us, length us, event | category | flops | bytes accessed | tf_op | source)
XLA Modules:
  0.0 66.1 jit_solution(7950877521341429579)
XLA Ops:
  0.0 64.5 %shard_map.73 = f32[8,4800]{1,0:T(8,128)} custom-call(bf16[256,128]{1,0:T(8,128)(2,1)} %disc.1, bf16[4800,256]{1,0:T(8,128)(2,1)} %bitcast.5, f32[8,512]{1,0:T(8,128)} %bitcast.6, s32[8,512]{1,0:T(8,128)} %bitcast.7, s32[1,512]{1,0:T(1,128)} %bitcast.8, s32[1,512]{1,0:T(1,128)} %bitcast.9, bf16[75,4800]{1,0:T(8,128)(2,1)} %jac.1), custom_call_target="tpu_custom_call" | custom-call | tf_op jit(solution)/shard_map/pallas_call | solution.py:633
  64.5 1.6 %copy.9 = f32[8,4800]{1,0:T(8,128)} copy(f32[8,4800]{1,0:T(8,128)} %shard_map.73) | data formatting | bytes 307200

commit v8 on v7

--- a/solution.py
+++ b/solution.py
@@ -11,7 +11,7 @@
 DEPTH = 8
 CHIPS = RING * DEPTH
 PATHS = 2 * CHIPS
-EXTRA = 6
+GROUP = 16
 F32 = jnp.float32
 BF16 = jnp.bfloat16
 MESH = pl.DeviceIdType.MESH
@@ -20,7 +20,7 @@
 def kernel(
     disc, sens, cash, index, exer, steps, jac, out,
     dv, cv, iv, ev, sv, s_own, s_in, d_in, xs, xp, r1, y2, r2, zb, rz, zr, zf, xf,
-    jv, jp, jz, jr, wt, room, mk, acc, acce, pr, pre, po, ob,
+    jv, je, jp, jz, jr, jx, jb, wt, room, acc, pr, po, ob,
     ss_s, rs_s, ls, ss_1, rs_1, ss_2, rs_2, ss_z, rs_z, ss_g, rs_g,
     ss_a2, rs_a2, ss_a1, rs_a1, ss_j, ss_jx, rs_j, ss_ja, rs_ja, ss_p, rs_p, ss_o, rs_o, near_z,
 ):
@@ -123,8 +123,9 @@
     for n, k in enumerate((2, DEPTH - 2)):
         pl.semaphore_signal(near_z.at[n], inc=1, device_id=on_z(k), device_id_type=MESH)
 
-    tiles = out.shape[1] // LANE + 1
-    tail = params - (tiles - 1) * LANE
+    main = CHIPS * LANE
+    more = (params - main) // CHIPS
+    groups = pad // GROUP
     turn = lax.rem(z, RING) == y
     core = lax.div(x, 2)
     high = lax.div(z, RING)
@@ -141,12 +142,15 @@
                 col = pl.multiple_of((zz * RING + t) * LANE, LANE)
                 jp[zz, t, 0:jrows] = jv[:, pl.ds(col, LANE)]
 
-            @pl.when(zz < EXTRA - 1)
-            def _():
-                col = pl.multiple_of((CHIPS + zz) * LANE, LANE)
-                jp[zz, RING, 0:jrows] = jv[:, pl.ds(col, LANE)]
-
-        jp[EXTRA - 1, RING, 0:jrows, 0:tail] = jv[:, (tiles - 1) * LANE : params]
+        je[...] = jnp.zeros(je.shape, F32)
+        je[0:jrows, 0 : params - main] = jv[:, main:params].astype(F32)
+        for t in range(CHIPS):
+            packed = [
+                je[r * GROUP : (r + 1) * GROUP, t * more : (t + 1) * more] for r in range(groups)
+            ]
+            packed.append(jnp.zeros((GROUP, LANE - groups * more), F32))
+            jp[t // RING, t % RING, pad : pad + GROUP] = jnp.concatenate(packed, axis=1).astype(BF16)
+
         pltpu.make_async_copy(jp.at[z], jz.at[high], rs_j.at[2, high]).start()
 
     def j_line(k):
@@ -218,22 +222,20 @@
     one[2].second()
     one[3].second()
 
-    has_extra = z < EXTRA
-
     def j_cross(e, k):
         xx = lax.rem(x + k, RING)
-        slot = xx if e == 0 else RING
-        dst = jr.at[
-            e, pl.ds(2 * lax.rem(x, 2), 2), y, pl.ds(pl.multiple_of(c * pad, 16), pad)
-        ]
-        return jz.at[:, slot], dst, ss_jx.at[e, k], rs_j.at[e, 0], at_chip(xx, z, core)
+        two_ = pl.ds(2 * lax.rem(x, 2), 2)
+        if e == 0:
+            src = jz.at[:, xx, 0:pad]
+            dst = jr.at[two_, y, pl.ds(pl.multiple_of(c * pad, 16), pad)]
+        else:
+            src = jz.at[:, xx, pad : pad + GROUP]
+            dst = jx.at[two_, y, c]
+        return src, dst, ss_jx.at[e, k], rs_j.at[e, 0], at_chip(xx, z, core)
 
     def both(f):
         f(0)
-
-        @pl.when(has_extra)
-        def _():
-            f(1)
+        f(1)
 
     def j_send(e):
         for k in (1, 3):
@@ -317,30 +319,48 @@
             )
 
 
-    def j_ring(e, half_, k, n, dev):
-        ref = jr.at[e, pl.ds(2 * half_, 2), k]
-        return ref, ref, ss_ja.at[e, n], rs_ja.at[e, n], dev
+    def j_ring(half_, k, n, dev):
+        ref = jr.at[pl.ds(2 * half_, 2), k]
+        return ref, ref, ss_ja.at[0, n], rs_ja.at[0, n], dev
+
+    def j_fan(k):
+        ref = jx.at[:, y]
+        return ref, ref, ss_ja.at[1, k], rs_ja.at[1, 0], on_y(k)
 
     yr, yl = on_y(1), on_y(3)
     ynr, yfar, ynl = (lax.rem(y + k, RING) for k in (1, 2, 3))
 
-    def j_start(e):
-        whole = jr.at[e, :, y]
-        pltpu.make_async_copy(whole, whole, rs_j.at[e, 0]).wait()
+    def j_start():
+        for e, whole in ((0, jr.at[:, y]), (1, jx.at[:, y])):
+            pltpu.make_async_copy(whole, whole, rs_j.at[e, 0]).wait()
         for n, (hh, d) in enumerate(((0, yr), (1, yl), (1, yr), (0, yl))):
-            rdma(*j_ring(e, hh, y, n, d)).start()
-
-    def j_forward(e):
-        rdma(*j_ring(e, 0, ynl, 0, yr)).wait_recv()
-        rdma(*j_ring(e, 0, ynl, 4, yr)).start()
-        rdma(*j_ring(e, 1, ynr, 1, yl)).wait_recv()
-        rdma(*j_ring(e, 1, ynr, 5, yl)).start()
-
-    def j_finish(e):
+            send(*j_ring(hh, y, n, d))
+        for k in (2, 1, 3):
+            send(*j_fan(k))
+
+    def j_forward():
+        rdma(*j_ring(0, ynl, 0, yr)).wait_recv()
+        send(*j_ring(0, ynl, 4, yr))
+        rdma(*j_ring(1, ynr, 1, yl)).wait_recv()
+        send(*j_ring(1, ynr, 5, yl))
+
+    def j_finish():
         for hh, k, n, d in ((1, ynl, 2, yr), (0, ynr, 3, yl), (0, yfar, 4, yr), (1, yfar, 5, yl)):
-            rdma(*j_ring(e, hh, k, n, d)).wait_recv()
-
-    j_start(0)
+            rdma(*j_ring(hh, k, n, d)).wait_recv()
+        three = jx.at[0 : RING - 1]
+        rdma(three, three, ss_ja.at[1, 0], rs_ja.at[1, 0], sibling).wait_recv()
+
+        @pl.loop(0, RING * RING)
+        def _(n):
+            q, k = lax.div(n, RING), lax.rem(n, RING)
+            for u in (0, 1):
+                tile = jx[q, k, u].astype(F32)
+                for r in range(groups):
+                    at = u * pad + r * GROUP
+                    turned_ = tile if r == 0 else pltpu.roll(tile, LANE - r * more, 1)
+                    jb[n, at : at + GROUP] = turned_.astype(BF16)
+
+    j_start()
 
     for g in (0, 1):
         reducer = reduces(g)
@@ -360,8 +380,7 @@
                 reducer, zr.at[g], zf.at[g, z_piece(g, z)], ss_g.at[g, k], rs_g.at[g], on_z(k)
             )
 
-    pl.when(has_extra)(lambda: j_start(1))
-    j_forward(0)
+    j_forward()
 
     def home(q, i):
         return xf.at[q, lines[q % 2][0], part_rows(i, part)]
@@ -410,12 +429,10 @@
     ring = [Gather(q) for q in range(RING)]
     for q in range(RING):
         ring[q].start()
-    pl.when(has_extra)(lambda: j_forward(1))
     ring[0].forward()
     ring[1].forward()
 
     acc[...] = jnp.zeros(acc.shape, F32)
-    acce[...] = jnp.zeros(acce.shape, F32)
 
     def block(q, k):
         values = xf[q, k]
@@ -426,8 +443,8 @@
             preferred_element_type=F32,
         )
         masked = jnp.where(room[...] > (8 * q + 2 * k) * jrows, vega, 0.0).astype(BF16)
-        mk[RING * q + k] = masked
-        acc[...] += jnp.dot(masked, jr[0, q, k], preferred_element_type=F32)
+        both_ = jnp.concatenate([jr[q, k], jb[RING * q + k]], axis=1)
+        acc[...] += jnp.dot(masked, both_, preferred_element_type=F32)
 
     def landed(q, k, h, n):
         ref = xf.at[q, k, h * pad : (h + 1) * pad]
@@ -436,7 +453,7 @@
     def ring_place(q, step):
         return lax.rem(jnp.where(lax.rem(q, 2) == 0, x, y) + step, RING)
 
-    j_finish(0)
+    j_finish()
 
     @pl.loop(0, 2)
     def _(q):
@@ -463,8 +480,6 @@
             landed(q, k, 0, 3)
 
         block(q, k)
-
-    pl.when(has_extra)(lambda: j_finish(1))
 
     @pl.loop(0, RING)
     def _(q):
@@ -473,55 +488,34 @@
         landed(q, k, 1, 5)
         block(q, k)
 
-        @pl.when(has_extra)
-        def _():
-            mine = pl.ds(pl.multiple_of(x * LANE, LANE), LANE)
-            more = jnp.zeros((LANE, LANE), F32)
-            for kk in range(RING):
-                more += jnp.dot(
-                    mk[RING * q + kk, mine], jr[1, q, kk], preferred_element_type=F32
-                )
-            acce[...] += more.reshape(acce.shape)
-
     rows_c = pl.ds(pl.multiple_of(c * (trades // 2), 8), trades // 2)
     rows_sib = pl.ds(pl.multiple_of(sib * (trades // 2), 8), trades // 2)
     swap = (acc.at[rows_sib], pr, ss_p.at[0], rs_p.at[0], sibling)
     send(*swap)
-    swap_extra = (acce.at[:, sib], pre, ss_p.at[1], rs_p.at[1], sibling)
-
-    @pl.when(has_extra)
-    def _():
-        rdma(*swap_extra).start()
-
     strip_rows = out.shape[0]
     rdma(*swap).wait_recv()
-    po[0] = (acc[rows_c] + pr[...]).reshape(CHIPS, strip_rows, LANE)
-
-    def deliver(e, n, tile, dst):
+    total = acc[rows_c] + pr[...]
+    po[...] = jnp.concatenate(
+        [total[:, s * LANE : (s + 1) * LANE].reshape(CHIPS, strip_rows, LANE) for s in (0, 1)], axis=1
+    ).astype(BF16)
+
+    def deliver(n, dst):
+        tile = ob.at[z * RING + x]
+
         @pl.when(dst != me)
         def _():
-            rdma(
-                po.at[e, n], ob.at[tile], ss_o.at[e], rs_o.at[0], {"grp": y, "path": dst}
-            ).start()
+            rdma(po.at[n], tile, ss_o.at[0], rs_o.at[0], {"grp": y, "path": dst}).start()
 
         @pl.when(dst == me)
         def _():
-            pltpu.make_async_copy(po.at[e, n], ob.at[tile], rs_o.at[0]).start()
+            pltpu.make_async_copy(po.at[n], tile, rs_o.at[0]).start()
 
     for k in (4, 3, 5, 2, 6, 1, 7, 0):
         zz = lax.rem(z + k, DEPTH)
         for side in (0, 1):
             for u in (0, 1):
                 n = side * 2 * DEPTH + 2 * zz + u
-                deliver(0, n, z * RING + x, c * CHIPS + n)
-
-    @pl.when(has_extra)
-    def _():
-        rdma(*swap_extra).wait_recv()
-        po[1, 0:DEPTH] = acce[:, c] + pre[...]
-        for k in (4, 3, 5, 2, 6, 1, 7, 0):
-            zz = lax.rem(z + k, DEPTH)
-            deliver(1, zz, CHIPS + z, (x * DEPTH + zz) * 2 + c)
+                deliver(n, c * CHIPS + n)
 
     for cond, d in sent:
         if cond is None:
@@ -529,12 +523,6 @@
         else:
             pl.when(cond)(d.wait_send)
 
-    def j_sent(e):
-        for n, hh in enumerate((0, 1, 1, 0, 0, 1)):
-            rdma(*j_ring(e, hh, y, n, yr)).wait_send()
-
-    both(j_sent)
-
     def j_crossed(e):
         for k in (1, 2, 3):
             rdma(*j_cross(e, k)).wait_send()
@@ -544,10 +532,6 @@
             rdma(*j_cross(e, 0)).wait_send()
 
     both(j_crossed)
-
-    @pl.when(has_extra)
-    def _():
-        rdma(*swap_extra).wait_send()
 
     @pl.when(turn)
     def _():
@@ -556,16 +540,18 @@
 
     pltpu.make_async_copy(ob, ob, rs_o.at[0]).wait()
 
-    for t in range(tiles - 1):
-        out[:, t * LANE : (t + 1) * LANE] = ob[t]
-    out[:, (tiles - 1) * LANE : params] = ob[tiles - 1, :, 0:tail]
-
-    def po_sent(e, n):
-        rdma(po.at[e, 0:n], po.at[e, 0:n], ss_o.at[e], rs_o.at[0], sibling).wait_send()
-
-    pl.when(core == c)(lambda: po_sent(0, CHIPS - 1))
-    pl.when(core != c)(lambda: po_sent(0, CHIPS))
-    pl.when(has_extra)(lambda: po_sent(1, DEPTH - 1))
+    rest = []
+    for t in range(CHIPS):
+        tile = ob[t].astype(F32)
+        out[:, t * LANE : (t + 1) * LANE] = tile[0:strip_rows]
+        rest.append(tile[strip_rows : 2 * strip_rows, 0:more])
+    out[:, main:params] = jnp.concatenate(rest, axis=1)
+
+    def po_sent(n):
+        rdma(po.at[0:n], po.at[0:n], ss_o.at[0], rs_o.at[0], sibling).wait_send()
+
+    pl.when(core == c)(lambda: po_sent(CHIPS - 1))
+    pl.when(core != c)(lambda: po_sent(CHIPS))
 
 
 def per_device(
@@ -575,7 +561,7 @@
     trades = cash_flows.shape[0]
     jrows = jacobian_inv.shape[0]
     strip = trades // PATHS
-    tiles = -(-params // LANE)
+    rest = params - CHIPS * LANE
     pad = -(-jrows // 16) * 16
     half = params // 2
     slots = cash_flows.shape[1]
@@ -603,18 +589,18 @@
         vm((2, 2 * part, LANE), F32),
         vm((RING, RING, 2 * pad, LANE), F32),
         vm((jrows, params), BF16),
-        vm((DEPTH, RING + 1, pad, LANE), BF16),
-        vm((2, RING + 1, pad, LANE), BF16),
-        vm((2, RING, RING, 2 * pad, LANE), BF16),
+        vm((pad, -(-rest // LANE) * LANE), F32),
+        vm((DEPTH, RING, pad + GROUP, LANE), BF16),
+        vm((2, RING, pad + GROUP, LANE), BF16),
+        vm((RING, RING, 2 * pad, LANE), BF16),
+        vm((RING, RING, 2, GROUP, LANE), BF16),
+        vm((RING * RING, 2 * pad, LANE), BF16),
         vm((trades, 3 * LANE), BF16),
         vm((trades, 2 * pad), jnp.int32),
-        vm((RING * RING, trades, 2 * pad), BF16),
-        vm((trades, LANE), F32),
-        vm((DEPTH, 2, strip, LANE), F32),
-        vm((trades // 2, LANE), F32),
-        vm((DEPTH, strip, LANE), F32),
-        vm((2, CHIPS, strip, LANE), F32),
-        vm((tiles, strip, LANE), F32),
+        vm((trades, 2 * LANE), F32),
+        vm((trades // 2, 2 * LANE), F32),
+        vm((CHIPS, 2 * strip, LANE), BF16),
+        vm((CHIPS, 2 * strip, LANE), BF16),
         dma((RING + 1,)), dma((RING + 1,)), dma((7,)),
         dma((RING, 6)), dma((RING, 6)),
         dma((RING, RING)), dma((RING,)),
@@ -625,7 +611,7 @@
         dma((DEPTH,)), dma((2, RING)), dma((3, 2)),
         dma((2, 6)), dma((2, 6)),
         dma((2,)), dma((2,)),
-        dma((2,)), dma((1,)),
+        dma((1,)), dma((1,)),
         pltpu.SemaphoreType.REGULAR((2,)),
     ]
     vmem = pl.BlockSpec(memory_space=pltpu.VMEM)

time: 66.2 us -> 62.9 us (0.950)
  Pallas kernels: 64.5 us -> 61.2 us
    pallas_call x1, Pallas kernels: 64.5 us -> 61.2 us  [per_device(): pl.pallas_call(kernel, out_shape=jax.ShapeDtypeStruct((strip, params), F3...]
where the time goes in v8:
time: 62.9 us; the launch traced here: 62.8 us
  Pallas kernels  61.2 us (97%)
  local copies, waits for them, and re-layouts  1.59 us (3%)
    pallas_call x1, Pallas kernels, per_device(): pl.pallas_call(kernel, out_shape=jax.ShapeDtypeStruct((strip, params), F3...  61.2 us
    unnamed x1, local copies, waits for them, and re-layouts  1.59 us

profile of v8, /device:TPU:1, one launch (start us, length us, event | category | flops | bytes accessed | tf_op | source)
XLA Modules:
  0.0 62.8 jit_solution(9587818641854490577)
XLA Ops:
  0.0 61.2 %shard_map.73 = f32[8,4800]{1,0:T(8,128)} custom-call(bf16[256,128]{1,0:T(8,128)(2,1)} %disc.1, bf16[4800,256]{1,0:T(8,128)(2,1)} %bitcast.5, f32[8,512]{1,0:T(8,128)} %bitcast.6, s32[8,512]{1,0:T(8,128)} %bitcast.7, s32[1,512]{1,0:T(1,128)} %bitcast.8, s32[1,512]{1,0:T(1,128)} %bitcast.9, bf16[75,4800]{1,0:T(8,128)(2,1)} %jac.1), custom_call_target="tpu_custom_call" | custom-call | tf_op jit(solution)/shard_map/pallas_call | solution.py:619
  61.2 1.6 %copy.9 = f32[8,4800]{1,0:T(8,128)} copy(f32[8,4800]{1,0:T(8,128)} %shard_map.73) | data formatting | bytes 307200

commit v9 on v8

--- a/solution.py
+++ b/solution.py
@@ -266,9 +266,11 @@
     w_lo = (weights - w_hi.astype(F32)).astype(BF16)
     wt[...] = jnp.concatenate([w_hi, w_hi, w_lo], axis=1)
     reach = jnp.broadcast_to((sv[...] * width).astype(F32), (LANE, trades)).T.astype(jnp.int32)
-    lane = lax.broadcasted_iota(jnp.int32, (trades, 2 * pad), 1)
+    span = 4 * pad
+    lane = lax.broadcasted_iota(jnp.int32, (trades, span), 1)
+    lane = lane - jnp.where(lane >= 2 * pad, 2 * pad, 0)
     room[...] = (
-        jnp.concatenate([reach, reach[:, : 2 * pad - LANE]], axis=1)
+        jnp.concatenate([reach] * (span // LANE) + [reach[:, : span % LANE]], axis=1)
         - lane + jnp.where(lane >= pad, pad - jrows, 0) - c * half
     )
 
@@ -347,6 +349,8 @@
     def j_finish():
         for hh, k, n, d in ((1, ynl, 2, yr), (0, ynr, 3, yl), (0, yfar, 4, yr), (1, yfar, 5, yl)):
             rdma(*j_ring(hh, k, n, d)).wait_recv()
+
+    def j_unpack():
         three = jx.at[0 : RING - 1]
         rdma(three, three, ss_ja.at[1, 0], rs_ja.at[1, 0], sibling).wait_recv()
 
@@ -400,6 +404,8 @@
                 send(mine, home(q, i), ss_a2.at[q, k], rs_a2.at[q], on(k))
             home(q, i)[...] = mine[...]
 
+    j_unpack()
+
     class Gather:
         def __init__(self, q):
             self.q = q
@@ -434,17 +440,26 @@
 
     acc[...] = jnp.zeros(acc.shape, F32)
 
-    def block(q, k):
-        values = xf[q, k]
+    second_lane = lax.broadcasted_iota(jnp.int32, (1, span), 1) >= 2 * pad
+
+    def pair(*both_):
+        values = jnp.concatenate([xf[q, k] for q, k in both_], axis=0)
         hi = values.astype(BF16)
         lo = (values - hi.astype(F32)).astype(BF16)
         vega = lax.dot_general(
             wt[...], jnp.concatenate([hi, lo, hi], axis=1), (((1,), (1,)), ((), ())),
             preferred_element_type=F32,
         )
-        masked = jnp.where(room[...] > (8 * q + 2 * k) * jrows, vega, 0.0).astype(BF16)
-        both_ = jnp.concatenate([jr[q, k], jb[RING * q + k]], axis=1)
-        acc[...] += jnp.dot(masked, both_, preferred_element_type=F32)
+        start = [(8 * q + 2 * k) * jrows for q, k in both_]
+        masked = jnp.where(
+            room[...] > jnp.where(second_lane, start[1], start[0]), vega, 0.0
+        ).astype(BF16)
+        columns = [
+            jnp.concatenate([jr[q, k], jb[RING * q + k]], axis=1) for q, k in both_
+        ]
+        acc[...] += jnp.dot(
+            masked, jnp.concatenate(columns, axis=0), preferred_element_type=F32
+        )
 
     def landed(q, k, h, n):
         ref = xf.at[q, k, h * pad : (h + 1) * pad]
@@ -455,38 +470,26 @@
 
     j_finish()
 
-    @pl.loop(0, 2)
-    def _(q):
-        block(q, ring_place(q, 0))
-
+    pair((0, x), (1, y))
     ring[2].forward()
     ring[3].forward()
-
-    @pl.loop(2, RING)
-    def _(q):
-        block(q, ring_place(q, 0))
-
-    @pl.loop(0, 2 * RING)
-    def _(n):
-        q = lax.div(n, 2)
-        k = ring_place(q, 3 - 2 * lax.rem(n, 2))
-
-        @pl.when(lax.rem(n, 2) == 0)
-        def _():
-            landed(q, k, 1, 2)
-
-        @pl.when(lax.rem(n, 2) == 1)
-        def _():
-            landed(q, k, 0, 3)
-
-        block(q, k)
+    pair((2, x), (3, y))
 
     @pl.loop(0, RING)
     def _(q):
-        k = ring_place(q, 2)
-        landed(q, k, 0, 4)
-        landed(q, k, 1, 5)
-        block(q, k)
+        nl, nr = ring_place(q, 3), ring_place(q, 1)
+        landed(q, nl, 1, 2)
+        landed(q, nr, 0, 3)
+        pair((q, nl), (q, nr))
+
+    far_x, far_y = ring[0].far, ring[1].far
+
+    @pl.loop(0, 2)
+    def _(g):
+        for q, k in ((2 * g, far_x), (2 * g + 1, far_y)):
+            landed(q, k, 0, 4)
+            landed(q, k, 1, 5)
+        pair((2 * g, far_x), (2 * g + 1, far_y))
 
     rows_c = pl.ds(pl.multiple_of(c * (trades // 2), 8), trades // 2)
     rows_sib = pl.ds(pl.multiple_of(sib * (trades // 2), 8), trades // 2)
@@ -499,23 +502,25 @@
         [total[:, s * LANE : (s + 1) * LANE].reshape(CHIPS, strip_rows, LANE) for s in (0, 1)], axis=1
     ).astype(BF16)
 
+    tile = ob.at[z * RING + x]
+
     def deliver(n, dst):
-        tile = ob.at[z * RING + x]
-
-        @pl.when(dst != me)
-        def _():
-            rdma(po.at[n], tile, ss_o.at[0], rs_o.at[0], {"grp": y, "path": dst}).start()
-
-        @pl.when(dst == me)
-        def _():
-            pltpu.make_async_copy(po.at[n], tile, rs_o.at[0]).start()
+        rdma(po.at[n], tile, ss_o.at[0], rs_o.at[0], {"grp": y, "path": dst}).start()
 
     for k in (4, 3, 5, 2, 6, 1, 7, 0):
         zz = lax.rem(z + k, DEPTH)
         for side in (0, 1):
             for u in (0, 1):
                 n = side * 2 * DEPTH + 2 * zz + u
-                deliver(n, c * CHIPS + n)
+                dst = c * CHIPS + n
+                if k:
+                    deliver(n, dst)
+                else:
+                    pl.when(dst != me)(lambda n=n, dst=dst: deliver(n, dst))
+
+                    @pl.when(dst == me)
+                    def _():
+                        pltpu.make_async_copy(po.at[n], tile, rs_o.at[0]).start()
 
     for cond, d in sent:
         if cond is None:
@@ -596,7 +601,7 @@
         vm((RING, RING, 2, GROUP, LANE), BF16),
         vm((RING * RING, 2 * pad, LANE), BF16),
         vm((trades, 3 * LANE), BF16),
-        vm((trades, 2 * pad), jnp.int32),
+        vm((trades, 4 * pad), jnp.int32),
         vm((trades, 2 * LANE), F32),
         vm((trades // 2, 2 * LANE), F32),
         vm((CHIPS, 2 * strip, LANE), BF16),

time: 62.9 us -> 60.5 us (0.962)
  Pallas kernels: 61.2 us -> 58.8 us
    pallas_call x1, Pallas kernels: 61.2 us -> 58.8 us  [per_device(): pl.pallas_call(kernel, out_shape=jax.ShapeDtypeStruct((strip, params), F3...]
where the time goes in v9:
time: 60.5 us; the launch traced here: 60.4 us
  Pallas kernels  58.8 us (97%)
  local copies, waits for them, and re-layouts  1.59 us (3%)
    pallas_call x1, Pallas kernels, per_device(): pl.pallas_call(kernel, out_shape=jax.ShapeDtypeStruct((strip, params), F3...  58.8 us
    unnamed x1, local copies, waits for them, and re-layouts  1.59 us

profile of v9, /device:TPU:1, one launch (start us, length us, event | category | flops | bytes accessed | tf_op | source)
XLA Modules:
  0.0 60.4 jit_solution(5511884988522356249)
XLA Ops:
  0.0 58.8 %shard_map.73 = f32[8,4800]{1,0:T(8,128)} custom-call(bf16[256,128]{1,0:T(8,128)(2,1)} %disc.1, bf16[4800,256]{1,0:T(8,128)(2,1)} %bitcast.5, f32[8,512]{1,0:T(8,128)} %bitcast.6, s32[8,512]{1,0:T(8,128)} %bitcast.7, s32[1,512]{1,0:T(1,128)} %bitcast.8, s32[1,512]{1,0:T(1,128)} %bitcast.9, bf16[75,4800]{1,0:T(8,128)(2,1)} %jac.1), custom_call_target="tpu_custom_call" | custom-call | tf_op jit(solution)/shard_map/pallas_call | solution.py:624
  58.8 1.6 %copy.9 = f32[8,4800]{1,0:T(8,128)} copy(f32[8,4800]{1,0:T(8,128)} %shard_map.73) | data formatting | bytes 307200

commit v10 on v9

--- a/solution.py
+++ b/solution.py
@@ -20,7 +20,7 @@
 def kernel(
     disc, sens, cash, index, exer, steps, jac, out,
     dv, cv, iv, ev, sv, s_own, s_in, d_in, xs, xp, r1, y2, r2, zb, rz, zr, zf, xf,
-    jv, je, jp, jz, jr, jx, jb, wt, room, acc, pr, po, ob,
+    jv, je, jp, jz, jr, jx, jb, wt, room, mk, acc, pr, po, ob,
     ss_s, rs_s, ls, ss_1, rs_1, ss_2, rs_2, ss_z, rs_z, ss_g, rs_g,
     ss_a2, rs_a2, ss_a1, rs_a1, ss_j, ss_jx, rs_j, ss_ja, rs_ja, ss_p, rs_p, ss_o, rs_o, near_z,
 ):
@@ -291,11 +291,11 @@
     both(lambda e: rdma(*j_cross(e, 2)).start())
 
     share = zr.shape[1]
-    count = 2 * part // share
+    count = zb.shape[1] // share
     spread = (4, 3, 5, 2, 6, 1, 7)
 
     def turn_of(g, d):
-        return lax.rem(d + count * g, DEPTH)
+        return lax.rem(d + count, DEPTH)
 
     def reduces(g):
         return turn_of(g, z) < count
@@ -313,6 +313,7 @@
             for k in (1, 2, 3):
                 total += r2[q, lax.rem(i + k, RING)]
             zb[g, p * part : (p + 1) * part] = total
+        zb[g, 2 * part :] = jnp.zeros((zb.shape[1] - 2 * part, LANE), F32)
         for k in spread:
             d = lax.rem(z + k, DEPTH)
             send_if(
@@ -404,6 +405,18 @@
                 send(mine, home(q, i), ss_a2.at[q, k], rs_a2.at[q], on(k))
             home(q, i)[...] = mine[...]
 
+    def all_left():
+        while sent:
+            cond, d = sent.pop()
+            if cond is None:
+                d.wait_send()
+            else:
+                pl.when(cond)(d.wait_send)
+
+    later = sent[-4 * (RING - 1) - 2:]
+    del sent[-len(later) :]
+    all_left()
+    sent.extend(later)
     j_unpack()
 
     class Gather:
@@ -435,14 +448,12 @@
     ring = [Gather(q) for q in range(RING)]
     for q in range(RING):
         ring[q].start()
-    ring[0].forward()
-    ring[1].forward()
 
     acc[...] = jnp.zeros(acc.shape, F32)
 
     second_lane = lax.broadcasted_iota(jnp.int32, (1, span), 1) >= 2 * pad
 
-    def pair(*both_):
+    def mask(*both_):
         values = jnp.concatenate([xf[q, k] for q, k in both_], axis=0)
         hi = values.astype(BF16)
         lo = (values - hi.astype(F32)).astype(BF16)
@@ -451,9 +462,10 @@
             preferred_element_type=F32,
         )
         start = [(8 * q + 2 * k) * jrows for q, k in both_]
-        masked = jnp.where(
-            room[...] > jnp.where(second_lane, start[1], start[0]), vega, 0.0
-        ).astype(BF16)
+        keep = room[...] > jnp.where(second_lane, start[1], start[0])
+        return jnp.where(keep, vega, 0.0).astype(BF16)
+
+    def add(masked, *both_):
         columns = [
             jnp.concatenate([jr[q, k], jb[RING * q + k]], axis=1) for q, k in both_
         ]
@@ -461,6 +473,9 @@
             masked, jnp.concatenate(columns, axis=0), preferred_element_type=F32
         )
 
+    def pair(*both_):
+        add(mask(*both_), *both_)
+
     def landed(q, k, h, n):
         ref = xf.at[q, k, h * pad : (h + 1) * pad]
         rdma(ref, ref, ss_a1.at[q, n], rs_a1.at[q, n], sibling).wait_recv()
@@ -468,12 +483,19 @@
     def ring_place(q, step):
         return lax.rem(jnp.where(lax.rem(q, 2) == 0, x, y) + step, RING)
 
+    mine = lambda g: ((2 * g, x), (2 * g + 1, y))
+
+    @pl.loop(0, 2)
+    def _(g):
+        mk[g] = mask(*mine(g))
+
+    for r in ring:
+        r.forward()
     j_finish()
 
-    pair((0, x), (1, y))
-    ring[2].forward()
-    ring[3].forward()
-    pair((2, x), (3, y))
+    @pl.loop(0, 2)
+    def _(g):
+        add(mk[g], *mine(g))
 
     @pl.loop(0, RING)
     def _(q):
@@ -522,11 +544,7 @@
                     def _():
                         pltpu.make_async_copy(po.at[n], tile, rs_o.at[0]).start()
 
-    for cond, d in sent:
-        if cond is None:
-            d.wait_send()
-        else:
-            pl.when(cond)(d.wait_send)
+    all_left()
 
     def j_crossed(e):
         for k in (1, 2, 3):
@@ -571,7 +589,7 @@
     half = params // 2
     slots = cash_flows.shape[1]
     part = pad // 2
-    share = 16
+    share = 24
     vm = pltpu.VMEM
     dma = pltpu.SemaphoreType.DMA
     scratch = [
@@ -588,10 +606,10 @@
         vm((RING, 6, pad, LANE), F32),
         vm((RING, 2 * pad, LANE), F32),
         vm((RING, RING, part, LANE), F32),
-        vm((2, 2 * part, LANE), F32),
+        vm((2, RING * share, LANE), F32),
         vm((2, DEPTH, share, LANE), F32),
         vm((2, share, LANE), F32),
-        vm((2, 2 * part, LANE), F32),
+        vm((2, RING * share, LANE), F32),
         vm((RING, RING, 2 * pad, LANE), F32),
         vm((jrows, params), BF16),
         vm((pad, -(-rest // LANE) * LANE), F32),
@@ -602,6 +620,7 @@
         vm((RING * RING, 2 * pad, LANE), BF16),
         vm((trades, 3 * LANE), BF16),
         vm((trades, 4 * pad), jnp.int32),
+        vm((2, trades, 4 * pad), BF16),
         vm((trades, 2 * LANE), F32),
         vm((trades // 2, 2 * LANE), F32),
         vm((CHIPS, 2 * strip, LANE), BF16),

time: 60.5 us -> 60.1 us (level)
  no operation moved by 1% of the time
where the time goes in v10:
time: 60.1 us; the launch traced here: 60 us
  Pallas kernels  58.4 us (97%)
  local copies, waits for them, and re-layouts  1.59 us (3%)
    pallas_call x1, Pallas kernels, per_device(): pl.pallas_call(kernel, out_shape=jax.ShapeDtypeStruct((strip, params), F3...  58.4 us
    unnamed x1, local copies, waits for them, and re-layouts  1.59 us

profile of v10, /device:TPU:1, one launch (start us, length us, event | category | flops | bytes accessed | tf_op | source)
XLA Modules:
  0.0 60.0 jit_solution(13164891716660799662)
XLA Ops:
  0.0 58.4 %shard_map.73 = f32[8,4800]{1,0:T(8,128)} custom-call(bf16[256,128]{1,0:T(8,128)(2,1)} %disc.1, bf16[4800,256]{1,0:T(8,128)(2,1)} %bitcast.5, f32[8,512]{1,0:T(8,128)} %bitcast.6, s32[8,512]{1,0:T(8,128)} %bitcast.7, s32[1,512]{1,0:T(1,128)} %bitcast.8, s32[1,512]{1,0:T(1,128)} %bitcast.9, bf16[75,4800]{1,0:T(8,128)(2,1)} %jac.1), custom_call_target="tpu_custom_call" | custom-call | tf_op jit(solution)/shard_map/pallas_call | solution.py:643
  58.4 1.6 %copy.9 = f32[8,4800]{1,0:T(8,128)} copy(f32[8,4800]{1,0:T(8,128)} %shard_map.73) | data formatting | bytes 307200

commit v11 on v10

--- a/solution.py
+++ b/solution.py
@@ -118,7 +118,7 @@
 
     pl.semaphore_wait(barrier, len(partners))
     send(*d_copy)
-    for q in range(RING):
+    for q in (0, 1):
         send(*s_copy(q))
     for n, k in enumerate((2, DEPTH - 2)):
         pl.semaphore_signal(near_z.at[n], inc=1, device_id=on_z(k), device_id_type=MESH)
@@ -185,6 +185,8 @@
         def first(self):
             send(*self.msg(0, 0, self.far, self.right))
             send(*self.msg(2, 1, self.far, self.left))
+
+        def near(self):
             send(*self.msg(3, 1, self.nr, self.right))
             send(*self.msg(1, 0, self.nl, self.left))
 
@@ -205,6 +207,8 @@
     rdma(*d_copy).wait_recv()
     for q in range(RING):
         rdma(*s_copy(q)).wait_recv()
+        if q < 2:
+            send(*s_copy(q + 2))
         xs[cuts[q] : cuts[q + 1]] += jnp.dot(
             s_in[cuts[q] : cuts[q + 1]], d_in[...], preferred_element_type=F32
         )
@@ -213,6 +217,8 @@
                 top = (8 * q + 2 * k + u) * jrows
                 xp[q, k, u * pad : (u + 1) * pad] = xs[top : top + pad]
         one[q].first()
+    for r in one:
+        r.near()
 
     for n in (0, 1):
         pl.semaphore_wait(near_z.at[n], 1)
@@ -291,11 +297,11 @@
     both(lambda e: rdma(*j_cross(e, 2)).start())
 
     share = zr.shape[1]
-    count = zb.shape[1] // share
+    count = 2 * part // share
     spread = (4, 3, 5, 2, 6, 1, 7)
 
     def turn_of(g, d):
-        return lax.rem(d + count, DEPTH)
+        return lax.rem(d + count * g, DEPTH)
 
     def reduces(g):
         return turn_of(g, z) < count
@@ -313,7 +319,6 @@
             for k in (1, 2, 3):
                 total += r2[q, lax.rem(i + k, RING)]
             zb[g, p * part : (p + 1) * part] = total
-        zb[g, 2 * part :] = jnp.zeros((zb.shape[1] - 2 * part, LANE), F32)
         for k in spread:
             d = lax.rem(z + k, DEPTH)
             send_if(
@@ -436,6 +441,8 @@
             rdma(three, three, ss_a2.at[q, 0], rs_a2.at[q], sibling).wait_recv()
             send(*self.msg(0, 0, self.i, self.right))
             send(*self.msg(1, 1, self.i, self.left))
+
+        def rest(self):
             send(*self.msg(2, 1, self.i, self.right))
             send(*self.msg(3, 0, self.i, self.left))
 
@@ -489,6 +496,8 @@
     def _(g):
         mk[g] = mask(*mine(g))
 
+    for r in ring:
+        r.rest()
     for r in ring:
         r.forward()
     j_finish()
@@ -589,7 +598,7 @@
     half = params // 2
     slots = cash_flows.shape[1]
     part = pad // 2
-    share = 24
+    share = 16
     vm = pltpu.VMEM
     dma = pltpu.SemaphoreType.DMA
     scratch = [
@@ -606,10 +615,10 @@
         vm((RING, 6, pad, LANE), F32),
         vm((RING, 2 * pad, LANE), F32),
         vm((RING, RING, part, LANE), F32),
-        vm((2, RING * share, LANE), F32),
+        vm((2, 2 * part, LANE), F32),
         vm((2, DEPTH, share, LANE), F32),
         vm((2, share, LANE), F32),
-        vm((2, RING * share, LANE), F32),
+        vm((2, 2 * part, LANE), F32),
         vm((RING, RING, 2 * pad, LANE), F32),
         vm((jrows, params), BF16),
         vm((pad, -(-rest // LANE) * LANE), F32),

time: 60.1 us -> 59.9 us (level)
  no operation moved by 1% of the time
where the time goes in v11:
time: 59.9 us; the launch traced here: 59.8 us
  Pallas kernels  58.2 us (97%)
  local copies, waits for them, and re-layouts  1.59 us (3%)
    pallas_call x1, Pallas kernels, per_device(): pl.pallas_call(kernel, out_shape=jax.ShapeDtypeStruct((strip, params), F3...  58.2 us
    unnamed x1, local copies, waits for them, and re-layouts  1.59 us

profile of v11, /device:TPU:1, one launch (start us, length us, event | category | flops | bytes accessed | tf_op | source)
XLA Modules:
  0.0 59.8 jit_solution(16190985404384111650)
XLA Ops:
  0.0 58.2 %shard_map.73 = f32[8,4800]{1,0:T(8,128)} custom-call(bf16[256,128]{1,0:T(8,128)(2,1)} %disc.1, bf16[4800,256]{1,0:T(8,128)(2,1)} %bitcast.5, f32[8,512]{1,0:T(8,128)} %bitcast.6, s32[8,512]{1,0:T(8,128)} %bitcast.7, s32[1,512]{1,0:T(1,128)} %bitcast.8, s32[1,512]{1,0:T(1,128)} %bitcast.9, bf16[75,4800]{1,0:T(8,128)(2,1)} %jac.1), custom_call_target="tpu_custom_call" | custom-call | tf_op jit(solution)/shard_map/pallas_call | solution.py:652
  58.2 1.6 %copy.9 = f32[8,4800]{1,0:T(8,128)} copy(f32[8,4800]{1,0:T(8,128)} %shard_map.73) | data formatting | bytes 307200

commit v12 on v11

--- a/solution.py
+++ b/solution.py
@@ -244,7 +244,7 @@
         f(1)
 
     def j_send(e):
-        for k in (1, 3):
+        for k in (2, 1, 3):
             rdma(*j_cross(e, k)).start()
         src, dst, ss, rs, dev = j_cross(e, 0)
 
@@ -256,9 +256,6 @@
         def _():
             rdma(src, dst, ss, rs, dev).start()
 
-    for n in (0, 1):
-        pltpu.make_async_copy(jp.at[0], jz.at[n], rs_j.at[2, n]).wait()
-    both(j_send)
 
     slots = cash.shape[0]
     forwards = lax.broadcasted_iota(jnp.int32, (LANE, trades), 0)
@@ -294,7 +291,9 @@
             one[q].result()
             for k in (2, 1, 3):
                 send(*two(q, k))
-    both(lambda e: rdma(*j_cross(e, 2)).start())
+    for n in (0, 1):
+        pltpu.make_async_copy(jp.at[0], jz.at[n], rs_j.at[2, n]).wait()
+    both(j_send)
 
     share = zr.shape[1]
     count = 2 * part // share
@@ -390,7 +389,6 @@
                 reducer, zr.at[g], zf.at[g, z_piece(g, z)], ss_g.at[g, k], rs_g.at[g], on_z(k)
             )
 
-    j_forward()
 
     def home(q, i):
         return xf.at[q, lines[q % 2][0], part_rows(i, part)]
@@ -418,10 +416,11 @@
             else:
                 pl.when(cond)(d.wait_send)
 
-    later = sent[-4 * (RING - 1) - 2:]
+    later = sent[-4 * (RING - 1):]
     del sent[-len(later) :]
     all_left()
     sent.extend(later)
+    j_forward()
     j_unpack()
 
     class Gather:

time: 59.9 us -> 58.1 us (0.970)
  Pallas kernels: 58.2 us -> 56.4 us
    pallas_call x1, Pallas kernels: 58.2 us -> 56.4 us  [per_device(): pl.pallas_call(kernel, out_shape=jax.ShapeDtypeStruct((strip, params), F3...]
where the time goes in v12:
time: 58.1 us; the launch traced here: 58 us
  Pallas kernels  56.4 us (97%)
  local copies, waits for them, and re-layouts  1.59 us (3%)
    pallas_call x1, Pallas kernels, per_device(): pl.pallas_call(kernel, out_shape=jax.ShapeDtypeStruct((strip, params), F3...  56.4 us
    unnamed x1, local copies, waits for them, and re-layouts  1.59 us

profile of v12, /device:TPU:1, one launch (start us, length us, event | category | flops | bytes accessed | tf_op | source)
XLA Modules:
  0.0 58.0 jit_solution(3149572291252612121)
XLA Ops:
  0.0 56.4 %shard_map.73 = f32[8,4800]{1,0:T(8,128)} custom-call(bf16[256,128]{1,0:T(8,128)(2,1)} %disc.1, bf16[4800,256]{1,0:T(8,128)(2,1)} %bitcast.5, f32[8,512]{1,0:T(8,128)} %bitcast.6, s32[8,512]{1,0:T(8,128)} %bitcast.7, s32[1,512]{1,0:T(1,128)} %bitcast.8, s32[1,512]{1,0:T(1,128)} %bitcast.9, bf16[75,4800]{1,0:T(8,128)(2,1)} %jac.1), custom_call_target="tpu_custom_call" | custom-call | tf_op jit(solution)/shard_map/pallas_call | solution.py:651
  56.4 1.6 %copy.9 = f32[8,4800]{1,0:T(8,128)} copy(f32[8,4800]{1,0:T(8,128)} %shard_map.73) | data formatting | bytes 307200

commit v13 on v12

--- a/solution.py
+++ b/solution.py
@@ -118,8 +118,9 @@
 
     pl.semaphore_wait(barrier, len(partners))
     send(*d_copy)
-    for q in (0, 1):
-        send(*s_copy(q))
+    leading = [rdma(*s_copy(q)) for q in (0, 1)]
+    for d in leading:
+        d.start()
     for n, k in enumerate((2, DEPTH - 2)):
         pl.semaphore_signal(near_z.at[n], inc=1, device_id=on_z(k), device_id_type=MESH)
 
@@ -204,11 +205,12 @@
                 y2[self.q, rws] = xp[self.q, self.i, rws] + r1[self.q, n] + r1[self.q, 4 + h]
 
     one = [Scatter(q) for q in range(RING)]
+    for q, d in enumerate(leading):
+        d.wait_send()
+        send(*s_copy(q + 2))
     rdma(*d_copy).wait_recv()
     for q in range(RING):
         rdma(*s_copy(q)).wait_recv()
-        if q < 2:
-            send(*s_copy(q + 2))
         xs[cuts[q] : cuts[q + 1]] += jnp.dot(
             s_in[cuts[q] : cuts[q + 1]], d_in[...], preferred_element_type=F32
         )
@@ -255,6 +257,119 @@
         @pl.when(core != c)
         def _():
             rdma(src, dst, ss, rs, dev).start()
+
+
+    part = y2.shape[1] // RING
+
+    def two(q, k):
+        i, on = lines[1 - q % 2]
+        return (
+            y2.at[q, part_rows(lax.rem(i + k, RING), part)], r2.at[q, i],
+            ss_2.at[q, k], rs_2.at[q], on(k),
+        )
+
+    for g in (0, 1):
+        for q in (2 * g, 2 * g + 1):
+            one[q].result()
+            for k in (2, 1, 3):
+                send(*two(q, k))
+    for n in (0, 1):
+        pltpu.make_async_copy(jp.at[0], jz.at[n], rs_j.at[2, n]).wait()
+    both(j_send)
+
+    share = zr.shape[1]
+    count = 2 * part // share
+    spread = (4, 3, 5, 2, 6, 1, 7)
+
+    def turn_of(g, d):
+        return lax.rem(d + count * g, DEPTH)
+
+    def reduces(g):
+        return turn_of(g, z) < count
+
+    def z_piece(g, d):
+        return part_rows(jnp.minimum(turn_of(g, d), count - 1), share)
+
+    for g in (0, 1):
+        for p in (0, 1):
+            q = 2 * g + p
+            i, on = lines[1 - p]
+            total = y2[q, part_rows(i, part)]
+            three = r2.at[q, 0 : RING - 1]
+            rdma(three, three, ss_2.at[q, 0], rs_2.at[q], sibling).wait_recv()
+            for k in (1, 2, 3):
+                total += r2[q, lax.rem(i + k, RING)]
+            zb[g, p * part : (p + 1) * part] = total
+        for k in spread:
+            d = lax.rem(z + k, DEPTH)
+            send_if(
+                turn_of(g, d) < count,
+                zb.at[g, z_piece(g, d)], rz.at[g, z], ss_z.at[g, k], rs_z.at[g], on_z(k),
+            )
+
+
+    def j_ring(half_, k, n, dev):
+        ref = jr.at[pl.ds(2 * half_, 2), k]
+        return ref, ref, ss_ja.at[0, n], rs_ja.at[0, n], dev
+
+    def j_fan(k):
+        ref = jx.at[:, y]
+        return ref, ref, ss_ja.at[1, k], rs_ja.at[1, 0], on_y(k)
+
+    yr, yl = on_y(1), on_y(3)
+    ynr, yfar, ynl = (lax.rem(y + k, RING) for k in (1, 2, 3))
+
+    def j_start():
+        for e, whole in ((0, jr.at[:, y]), (1, jx.at[:, y])):
+            pltpu.make_async_copy(whole, whole, rs_j.at[e, 0]).wait()
+        for n, (hh, d) in enumerate(((0, yr), (1, yl), (1, yr), (0, yl))):
+            send(*j_ring(hh, y, n, d))
+        for k in (2, 1, 3):
+            send(*j_fan(k))
+
+    def j_forward():
+        rdma(*j_ring(0, ynl, 0, yr)).wait_recv()
+        send(*j_ring(0, ynl, 4, yr))
+        rdma(*j_ring(1, ynr, 1, yl)).wait_recv()
+        send(*j_ring(1, ynr, 5, yl))
+
+    def j_finish():
+        for hh, k, n, d in ((1, ynl, 2, yr), (0, ynr, 3, yl), (0, yfar, 4, yr), (1, yfar, 5, yl)):
+            rdma(*j_ring(hh, k, n, d)).wait_recv()
+
+    def j_unpack():
+        three = jx.at[0 : RING - 1]
+        rdma(three, three, ss_ja.at[1, 0], rs_ja.at[1, 0], sibling).wait_recv()
+
+        @pl.loop(0, RING * RING)
+        def _(n):
+            q, k = lax.div(n, RING), lax.rem(n, RING)
+            for u in (0, 1):
+                tile = jx[q, k, u].astype(F32)
+                for r in range(groups):
+                    at = u * pad + r * GROUP
+                    turned_ = tile if r == 0 else pltpu.roll(tile, LANE - r * more, 1)
+                    jb[n, at : at + GROUP] = turned_.astype(BF16)
+
+    j_start()
+
+    for g in (0, 1):
+        reducer = reduces(g)
+
+        @pl.when(reducer)
+        def _():
+            total = zb[g, z_piece(g, z)]
+            seven = rz.at[g, 0 : DEPTH - 1]
+            rdma(seven, seven, ss_z.at[g, 0], rs_z.at[g], sibling).wait_recv()
+            for k in range(1, DEPTH):
+                total += rz[g, lax.rem(z + k, DEPTH)]
+            zr[g] = total
+            zf[g, z_piece(g, z)] = total
+
+        for k in spread:
+            send_if(
+                reducer, zr.at[g], zf.at[g, z_piece(g, z)], ss_g.at[g, k], rs_g.at[g], on_z(k)
+            )
 
 
     slots = cash.shape[0]
@@ -277,119 +392,6 @@
         - lane + jnp.where(lane >= pad, pad - jrows, 0) - c * half
     )
 
-    part = y2.shape[1] // RING
-
-    def two(q, k):
-        i, on = lines[1 - q % 2]
-        return (
-            y2.at[q, part_rows(lax.rem(i + k, RING), part)], r2.at[q, i],
-            ss_2.at[q, k], rs_2.at[q], on(k),
-        )
-
-    for g in (0, 1):
-        for q in (2 * g, 2 * g + 1):
-            one[q].result()
-            for k in (2, 1, 3):
-                send(*two(q, k))
-    for n in (0, 1):
-        pltpu.make_async_copy(jp.at[0], jz.at[n], rs_j.at[2, n]).wait()
-    both(j_send)
-
-    share = zr.shape[1]
-    count = 2 * part // share
-    spread = (4, 3, 5, 2, 6, 1, 7)
-
-    def turn_of(g, d):
-        return lax.rem(d + count * g, DEPTH)
-
-    def reduces(g):
-        return turn_of(g, z) < count
-
-    def z_piece(g, d):
-        return part_rows(jnp.minimum(turn_of(g, d), count - 1), share)
-
-    for g in (0, 1):
-        for p in (0, 1):
-            q = 2 * g + p
-            i, on = lines[1 - p]
-            total = y2[q, part_rows(i, part)]
-            three = r2.at[q, 0 : RING - 1]
-            rdma(three, three, ss_2.at[q, 0], rs_2.at[q], sibling).wait_recv()
-            for k in (1, 2, 3):
-                total += r2[q, lax.rem(i + k, RING)]
-            zb[g, p * part : (p + 1) * part] = total
-        for k in spread:
-            d = lax.rem(z + k, DEPTH)
-            send_if(
-                turn_of(g, d) < count,
-                zb.at[g, z_piece(g, d)], rz.at[g, z], ss_z.at[g, k], rs_z.at[g], on_z(k),
-            )
-
-
-    def j_ring(half_, k, n, dev):
-        ref = jr.at[pl.ds(2 * half_, 2), k]
-        return ref, ref, ss_ja.at[0, n], rs_ja.at[0, n], dev
-
-    def j_fan(k):
-        ref = jx.at[:, y]
-        return ref, ref, ss_ja.at[1, k], rs_ja.at[1, 0], on_y(k)
-
-    yr, yl = on_y(1), on_y(3)
-    ynr, yfar, ynl = (lax.rem(y + k, RING) for k in (1, 2, 3))
-
-    def j_start():
-        for e, whole in ((0, jr.at[:, y]), (1, jx.at[:, y])):
-            pltpu.make_async_copy(whole, whole, rs_j.at[e, 0]).wait()
-        for n, (hh, d) in enumerate(((0, yr), (1, yl), (1, yr), (0, yl))):
-            send(*j_ring(hh, y, n, d))
-        for k in (2, 1, 3):
-            send(*j_fan(k))
-
-    def j_forward():
-        rdma(*j_ring(0, ynl, 0, yr)).wait_recv()
-        send(*j_ring(0, ynl, 4, yr))
-        rdma(*j_ring(1, ynr, 1, yl)).wait_recv()
-        send(*j_ring(1, ynr, 5, yl))
-
-    def j_finish():
-        for hh, k, n, d in ((1, ynl, 2, yr), (0, ynr, 3, yl), (0, yfar, 4, yr), (1, yfar, 5, yl)):
-            rdma(*j_ring(hh, k, n, d)).wait_recv()
-
-    def j_unpack():
-        three = jx.at[0 : RING - 1]
-        rdma(three, three, ss_ja.at[1, 0], rs_ja.at[1, 0], sibling).wait_recv()
-
-        @pl.loop(0, RING * RING)
-        def _(n):
-            q, k = lax.div(n, RING), lax.rem(n, RING)
-            for u in (0, 1):
-                tile = jx[q, k, u].astype(F32)
-                for r in range(groups):
-                    at = u * pad + r * GROUP
-                    turned_ = tile if r == 0 else pltpu.roll(tile, LANE - r * more, 1)
-                    jb[n, at : at + GROUP] = turned_.astype(BF16)
-
-    j_start()
-
-    for g in (0, 1):
-        reducer = reduces(g)
-
-        @pl.when(reducer)
-        def _():
-            total = zb[g, z_piece(g, z)]
-            seven = rz.at[g, 0 : DEPTH - 1]
-            rdma(seven, seven, ss_z.at[g, 0], rs_z.at[g], sibling).wait_recv()
-            for k in range(1, DEPTH):
-                total += rz[g, lax.rem(z + k, DEPTH)]
-            zr[g] = total
-            zf[g, z_piece(g, z)] = total
-
-        for k in spread:
-            send_if(
-                reducer, zr.at[g], zf.at[g, z_piece(g, z)], ss_g.at[g, k], rs_g.at[g], on_z(k)
-            )
-
-
     def home(q, i):
         return xf.at[q, lines[q % 2][0], part_rows(i, part)]
 
@@ -440,8 +442,6 @@
             rdma(three, three, ss_a2.at[q, 0], rs_a2.at[q], sibling).wait_recv()
             send(*self.msg(0, 0, self.i, self.right))
             send(*self.msg(1, 1, self.i, self.left))
-
-        def rest(self):
             send(*self.msg(2, 1, self.i, self.right))
             send(*self.msg(3, 0, self.i, self.left))
 
@@ -495,8 +495,6 @@
     def _(g):
         mk[g] = mask(*mine(g))
 
-    for r in ring:
-        r.rest()
     for r in ring:
         r.forward()
     j_finish()

time: 58.1 us -> 57.6 us (level)
  no operation moved by 1% of the time
where the time goes in v13:
time: 57.6 us; the launch traced here: 57.5 us
  Pallas kernels  55.9 us (97%)
  local copies, waits for them, and re-layouts  1.59 us (3%)
    pallas_call x1, Pallas kernels, per_device(): pl.pallas_call(kernel, out_shape=jax.ShapeDtypeStruct((strip, params), F3...  55.9 us
    unnamed x1, local copies, waits for them, and re-layouts  1.59 us

profile of v13, /device:TPU:1, one launch (start us, length us, event | category | flops | bytes accessed | tf_op | source)
XLA Modules:
  0.0 57.5 jit_solution(17831800265185748754)
XLA Ops:
  0.0 55.9 %shard_map.73 = f32[8,4800]{1,0:T(8,128)} custom-call(bf16[256,128]{1,0:T(8,128)(2,1)} %disc.1, bf16[4800,256]{1,0:T(8,128)(2,1)} %bitcast.5, f32[8,512]{1,0:T(8,128)} %bitcast.6, s32[8,512]{1,0:T(8,128)} %bitcast.7, s32[1,512]{1,0:T(1,128)} %bitcast.8, s32[1,512]{1,0:T(1,128)} %bitcast.9, bf16[75,4800]{1,0:T(8,128)(2,1)} %jac.1), custom_call_target="tpu_custom_call" | custom-call | tf_op jit(solution)/shard_map/pallas_call | solution.py:649
  55.9 1.6 %copy.9 = f32[8,4800]{1,0:T(8,128)} copy(f32[8,4800]{1,0:T(8,128)} %shard_map.73) | data formatting | bytes 307200

commit v14 on v13

--- a/solution.py
+++ b/solution.py
@@ -219,8 +219,9 @@
                 top = (8 * q + 2 * k + u) * jrows
                 xp[q, k, u * pad : (u + 1) * pad] = xs[top : top + pad]
         one[q].first()
-    for r in one:
-        r.near()
+        if q % 2:
+            one[q - 1].near()
+            one[q].near()
 
     for n in (0, 1):
         pl.semaphore_wait(near_z.at[n], 1)
@@ -519,25 +520,35 @@
             landed(q, k, 1, 5)
         pair((2 * g, far_x), (2 * g + 1, far_y))
 
-    rows_c = pl.ds(pl.multiple_of(c * (trades // 2), 8), trades // 2)
-    rows_sib = pl.ds(pl.multiple_of(sib * (trades // 2), 8), trades // 2)
-    swap = (acc.at[rows_sib], pr, ss_p.at[0], rs_p.at[0], sibling)
-    send(*swap)
     strip_rows = out.shape[0]
-    rdma(*swap).wait_recv()
-    total = acc[rows_c] + pr[...]
-    po[...] = jnp.concatenate(
-        [total[:, s * LANE : (s + 1) * LANE].reshape(CHIPS, strip_rows, LANE) for s in (0, 1)], axis=1
-    ).astype(BF16)
+    side_rows = trades // 4
+
+    def side_of(half_, side):
+        return pl.ds(pl.multiple_of((2 * half_ + side) * side_rows, 8), side_rows)
+
+    swaps = [
+        (acc.at[side_of(sib, n)], pr.at[n], ss_p.at[n], rs_p.at[n], sibling) for n in (0, 1)
+    ]
+    for swap in swaps:
+        send(*swap)
 
     tile = ob.at[z * RING + x]
 
     def deliver(n, dst):
         rdma(po.at[n], tile, ss_o.at[0], rs_o.at[0], {"grp": y, "path": dst}).start()
 
-    for k in (4, 3, 5, 2, 6, 1, 7, 0):
-        zz = lax.rem(z + k, DEPTH)
-        for side in (0, 1):
+    for side in (0, 1):
+        rdma(*swaps[side]).wait_recv()
+        total = acc[side_of(c, side)] + pr[side]
+        po[side * 2 * DEPTH : (side + 1) * 2 * DEPTH] = jnp.concatenate(
+            [
+                total[:, h * LANE : (h + 1) * LANE].reshape(2 * DEPTH, strip_rows, LANE)
+                for h in (0, 1)
+            ],
+            axis=1,
+        ).astype(BF16)
+        for k in (4, 3, 5, 2, 6, 1, 7, 0):
+            zz = lax.rem(z + k, DEPTH)
             for u in (0, 1):
                 n = side * 2 * DEPTH + 2 * zz + u
                 dst = c * CHIPS + n
@@ -628,7 +639,7 @@
         vm((trades, 4 * pad), jnp.int32),
         vm((2, trades, 4 * pad), BF16),
         vm((trades, 2 * LANE), F32),
-        vm((trades // 2, 2 * LANE), F32),
+        vm((2, trades // 4, 2 * LANE), F32),
         vm((CHIPS, 2 * strip, LANE), BF16),
         vm((CHIPS, 2 * strip, LANE), BF16),
         dma((RING + 1,)), dma((RING + 1,)), dma((7,)),

time: 57.6 us -> 57.7 us (level)
  no operation moved by 1% of the time
where the time goes in v14:
time: 57.7 us; the launch traced here: 57.6 us
  Pallas kernels  56 us (97%)
  local copies, waits for them, and re-layouts  1.59 us (3%)
    pallas_call x1, Pallas kernels, per_device(): pl.pallas_call(kernel, out_shape=jax.ShapeDtypeStruct((strip, params), F3...  56 us
    unnamed x1, local copies, waits for them, and re-layouts  1.59 us

profile of v14, /device:TPU:1, one launch (start us, length us, event | category | flops | bytes accessed | tf_op | source)
XLA Modules:
  0.0 57.6 jit_solution(10097240905058575881)
XLA Ops:
  0.0 56.0 %shard_map.73 = f32[8,4800]{1,0:T(8,128)} custom-call(bf16[256,128]{1,0:T(8,128)(2,1)} %disc.1, bf16[4800,256]{1,0:T(8,128)(2,1)} %bitcast.5, f32[8,512]{1,0:T(8,128)} %bitcast.6, s32[8,512]{1,0:T(8,128)} %bitcast.7, s32[1,512]{1,0:T(1,128)} %bitcast.8, s32[1,512]{1,0:T(1,128)} %bitcast.9, bf16[75,4800]{1,0:T(8,128)(2,1)} %jac.1), custom_call_target="tpu_custom_call" | custom-call | tf_op jit(solution)/shard_map/pallas_call | solution.py:660
  56.0 1.6 %copy.9 = f32[8,4800]{1,0:T(8,128)} copy(f32[8,4800]{1,0:T(8,128)} %shard_map.73) | data formatting | bytes 307200

commit v15 on v13

--- a/solution.py
+++ b/solution.py
@@ -384,11 +384,11 @@
     w_lo = (weights - w_hi.astype(F32)).astype(BF16)
     wt[...] = jnp.concatenate([w_hi, w_hi, w_lo], axis=1)
     reach = jnp.broadcast_to((sv[...] * width).astype(F32), (LANE, trades)).T.astype(jnp.int32)
-    span = 4 * pad
+    span = room.shape[1]
     lane = lax.broadcasted_iota(jnp.int32, (trades, span), 1)
-    lane = lane - jnp.where(lane >= 2 * pad, 2 * pad, 0)
+    lane = lax.rem(lane, 2 * pad)
     room[...] = (
-        jnp.concatenate([reach] * (span // LANE) + [reach[:, : span % LANE]], axis=1)
+        jnp.concatenate([reach] * (span // LANE), axis=1)
         - lane + jnp.where(lane >= pad, pad - jrows, 0) - c * half
     )
 
@@ -457,7 +457,6 @@
 
     acc[...] = jnp.zeros(acc.shape, F32)
 
-    second_lane = lax.broadcasted_iota(jnp.int32, (1, span), 1) >= 2 * pad
 
     def mask(*both_):
         values = jnp.concatenate([xf[q, k] for q, k in both_], axis=0)
@@ -467,8 +466,12 @@
             wt[...], jnp.concatenate([hi, lo, hi], axis=1), (((1,), (1,)), ((), ())),
             preferred_element_type=F32,
         )
-        start = [(8 * q + 2 * k) * jrows for q, k in both_]
-        keep = room[...] > jnp.where(second_lane, start[1], start[0])
+        wide_ = len(both_) * 2 * pad
+        lanes = lax.broadcasted_iota(jnp.int32, (1, wide_), 1)
+        start = jnp.zeros((1, wide_), jnp.int32)
+        for n, (q, k) in enumerate(both_):
+            start = jnp.where(lanes >= n * 2 * pad, (8 * q + 2 * k) * jrows, start)
+        keep = room[:, 0:wide_] > start
         return jnp.where(keep, vega, 0.0).astype(BF16)
 
     def add(masked, *both_):
@@ -486,9 +489,6 @@
         ref = xf.at[q, k, h * pad : (h + 1) * pad]
         rdma(ref, ref, ss_a1.at[q, n], rs_a1.at[q, n], sibling).wait_recv()
 
-    def ring_place(q, step):
-        return lax.rem(jnp.where(lax.rem(q, 2) == 0, x, y) + step, RING)
-
     mine = lambda g: ((2 * g, x), (2 * g + 1, y))
 
     @pl.loop(0, 2)
@@ -503,12 +503,15 @@
     def _(g):
         add(mk[g], *mine(g))
 
-    @pl.loop(0, RING)
-    def _(q):
-        nl, nr = ring_place(q, 3), ring_place(q, 1)
-        landed(q, nl, 1, 2)
-        landed(q, nr, 0, 3)
-        pair((q, nl), (q, nr))
+    @pl.loop(0, 2)
+    def _(g):
+        blocks = []
+        for p in (0, 1):
+            q = 2 * g + p
+            landed(q, ring[p].nl, 1, 2)
+            landed(q, ring[p].nr, 0, 3)
+            blocks += [(q, ring[p].nl), (q, ring[p].nr)]
+        pair(*blocks)
 
     far_x, far_y = ring[0].far, ring[1].far
 
@@ -625,7 +628,7 @@
         vm((RING, RING, 2, GROUP, LANE), BF16),
         vm((RING * RING, 2 * pad, LANE), BF16),
         vm((trades, 3 * LANE), BF16),
-        vm((trades, 4 * pad), jnp.int32),
+        vm((trades, 8 * pad), jnp.int32),
         vm((2, trades, 4 * pad), BF16),
         vm((trades, 2 * LANE), F32),
         vm((trades // 2, 2 * LANE), F32),

time: 57.6 us -> 56.7 us (0.984)
  Pallas kernels: 55.9 us -> 55 us
    pallas_call x1, Pallas kernels: 55.9 us -> 55 us  [per_device(): pl.pallas_call(kernel, out_shape=jax.ShapeDtypeStruct((strip, params), F3...]
where the time goes in v15:
time: 56.7 us; the launch traced here: 56.6 us
  Pallas kernels  55 us (97%)
  local copies, waits for them, and re-layouts  1.59 us (3%)
    pallas_call x1, Pallas kernels, per_device(): pl.pallas_call(kernel, out_shape=jax.ShapeDtypeStruct((strip, params), F3...  55 us
    unnamed x1, local copies, waits for them, and re-layouts  1.59 us

profile of v15, /device:TPU:1, one launch (start us, length us, event | category | flops | bytes accessed | tf_op | source)
XLA Modules:
  0.0 56.6 jit_solution(15255919582798436559)
XLA Ops:
  0.0 55.0 %shard_map.73 = f32[8,4800]{1,0:T(8,128)} custom-call(bf16[256,128]{1,0:T(8,128)(2,1)} %disc.1, bf16[4800,256]{1,0:T(8,128)(2,1)} %bitcast.5, f32[8,512]{1,0:T(8,128)} %bitcast.6, s32[8,512]{1,0:T(8,128)} %bitcast.7, s32[1,512]{1,0:T(1,128)} %bitcast.8, s32[1,512]{1,0:T(1,128)} %bitcast.9, bf16[75,4800]{1,0:T(8,128)(2,1)} %jac.1), custom_call_target="tpu_custom_call" | custom-call | tf_op jit(solution)/shard_map/pallas_call | solution.py:652
  55.0 1.6 %copy.9 = f32[8,4800]{1,0:T(8,128)} copy(f32[8,4800]{1,0:T(8,128)} %shard_map.73) | data formatting | bytes 307200

commit v16 on v15

--- a/solution.py
+++ b/solution.py
@@ -352,6 +352,7 @@
                     jb[n, at : at + GROUP] = turned_.astype(BF16)
 
     j_start()
+    early = len(sent)
 
     for g in (0, 1):
         reducer = reduces(g)
@@ -392,6 +393,16 @@
         - lane + jnp.where(lane >= pad, pad - jrows, 0) - c * half
     )
 
+    def all_left(n):
+        for cond, d in sent[:n]:
+            if cond is None:
+                d.wait_send()
+            else:
+                pl.when(cond)(d.wait_send)
+        del sent[:n]
+
+    all_left(early)
+
     def home(q, i):
         return xf.at[q, lines[q % 2][0], part_rows(i, part)]
 
@@ -410,20 +421,7 @@
                 send(mine, home(q, i), ss_a2.at[q, k], rs_a2.at[q], on(k))
             home(q, i)[...] = mine[...]
 
-    def all_left():
-        while sent:
-            cond, d = sent.pop()
-            if cond is None:
-                d.wait_send()
-            else:
-                pl.when(cond)(d.wait_send)
-
-    later = sent[-4 * (RING - 1):]
-    del sent[-len(later) :]
-    all_left()
-    sent.extend(later)
     j_forward()
-    j_unpack()
 
     class Gather:
         def __init__(self, q):
@@ -495,6 +493,8 @@
     def _(g):
         mk[g] = mask(*mine(g))
 
+    j_unpack()
+
     for r in ring:
         r.forward()
     j_finish()
@@ -553,7 +553,7 @@
                     def _():
                         pltpu.make_async_copy(po.at[n], tile, rs_o.at[0]).start()
 
-    all_left()
+    all_left(len(sent))
 
     def j_crossed(e):
         for k in (1, 2, 3):

time: 56.7 us -> 56.5 us (level)
  no operation moved by 1% of the time
where the time goes in v16:
time: 56.5 us; the launch traced here: 56.4 us
  Pallas kernels  54.8 us (97%)
  local copies, waits for them, and re-layouts  1.59 us (3%)
    pallas_call x1, Pallas kernels, per_device(): pl.pallas_call(kernel, out_shape=jax.ShapeDtypeStruct((strip, params), F3...  54.8 us
    unnamed x1, local copies, waits for them, and re-layouts  1.59 us

profile of v16, /device:TPU:1, one launch (start us, length us, event | category | flops | bytes accessed | tf_op | source)
XLA Modules:
  0.0 56.4 jit_solution(12369861270400441812)
XLA Ops:
  0.0 54.8 %shard_map.73 = f32[8,4800]{1,0:T(8,128)} custom-call(bf16[256,128]{1,0:T(8,128)(2,1)} %disc.1, bf16[4800,256]{1,0:T(8,128)(2,1)} %bitcast.5, f32[8,512]{1,0:T(8,128)} %bitcast.6, s32[8,512]{1,0:T(8,128)} %bitcast.7, s32[1,512]{1,0:T(1,128)} %bitcast.8, s32[1,512]{1,0:T(1,128)} %bitcast.9, bf16[75,4800]{1,0:T(8,128)(2,1)} %jac.1), custom_call_target="tpu_custom_call" | custom-call | tf_op jit(solution)/shard_map/pallas_call | solution.py:652
  54.8 1.6 %copy.9 = f32[8,4800]{1,0:T(8,128)} copy(f32[8,4800]{1,0:T(8,128)} %shard_map.73) | data formatting | bytes 307200

commit v17 on v16

--- a/solution.py
+++ b/solution.py
@@ -487,11 +487,9 @@
         ref = xf.at[q, k, h * pad : (h + 1) * pad]
         rdma(ref, ref, ss_a1.at[q, n], rs_a1.at[q, n], sibling).wait_recv()
 
-    mine = lambda g: ((2 * g, x), (2 * g + 1, y))
-
-    @pl.loop(0, 2)
-    def _(g):
-        mk[g] = mask(*mine(g))
+    mine = ((0, x), (1, y), (2, x), (3, y))
+
+    mk[...] = mask(*mine)
 
     j_unpack()
 
@@ -499,9 +497,7 @@
         r.forward()
     j_finish()
 
-    @pl.loop(0, 2)
-    def _(g):
-        add(mk[g], *mine(g))
+    add(mk[...], *mine)
 
     @pl.loop(0, 2)
     def _(g):
@@ -629,7 +625,7 @@
         vm((RING * RING, 2 * pad, LANE), BF16),
         vm((trades, 3 * LANE), BF16),
         vm((trades, 8 * pad), jnp.int32),
-        vm((2, trades, 4 * pad), BF16),
+        vm((trades, 8 * pad), BF16),
         vm((trades, 2 * LANE), F32),
         vm((trades // 2, 2 * LANE), F32),
         vm((CHIPS, 2 * strip, LANE), BF16),

time: 56.5 us -> 56.5 us (level)
  no operation moved by 1% of the time
where the time goes in v17:
time: 56.5 us; the launch traced here: 56.4 us
  Pallas kernels  54.8 us (97%)
  local copies, waits for them, and re-layouts  1.59 us (3%)
    pallas_call x1, Pallas kernels, per_device(): pl.pallas_call(kernel, out_shape=jax.ShapeDtypeStruct((strip, params), F3...  54.8 us
    unnamed x1, local copies, waits for them, and re-layouts  1.59 us

profile of v17, /device:TPU:1, one launch (start us, length us, event | category | flops | bytes accessed | tf_op | source)
XLA Modules:
  0.0 56.4 jit_solution(7226074687151666030)
XLA Ops:
  0.0 54.8 %shard_map.73 = f32[8,4800]{1,0:T(8,128)} custom-call(bf16[256,128]{1,0:T(8,128)(2,1)} %disc.1, bf16[4800,256]{1,0:T(8,128)(2,1)} %bitcast.5, f32[8,512]{1,0:T(8,128)} %bitcast.6, s32[8,512]{1,0:T(8,128)} %bitcast.7, s32[1,512]{1,0:T(1,128)} %bitcast.8, s32[1,512]{1,0:T(1,128)} %bitcast.9, bf16[75,4800]{1,0:T(8,128)(2,1)} %jac.1), custom_call_target="tpu_custom_call" | custom-call | tf_op jit(solution)/shard_map/pallas_call | solution.py:648
  54.8 1.6 %copy.9 = f32[8,4800]{1,0:T(8,128)} copy(f32[8,4800]{1,0:T(8,128)} %shard_map.73) | data formatting | bytes 307200
